TPU v7x, 256 devices: a whole 4x4x8 slice. The times are simulated.
256 devices in a mesh: seq: 32 (over z_hi, y, core), res: 8 (over x, z_lo).
Axes of the slice: x: 4, y: 4, z: 8 (z_hi: 4, z_lo: 2; z = z_hi * 2 + z_lo), core: 2. Of those that a mesh axis runs over, the one named last changes fastest.
Arguments:
- alignment_embeddings: bfloat16 [128, 1024, 768], P('seq', 'res'), may hold values from -10 to 10
- query_matrix: bfloat16 [768, 768], replicated, may hold values from -0.21875 to 0.21875
- key_matrix: bfloat16 [768, 768], replicated, may hold values from -0.21875 to 0.21875
- value_matrix: bfloat16 [768, 768], replicated, may hold values from -0.21875 to 0.21875
- output_matrix: bfloat16 [768, 768], replicated, may hold values from -0.21875 to 0.21875
Outputs:
- updated: bfloat16 [128, 1024, 768], P('seq', 'res')
All inputs are finite; a program needn't handle non-finite values.
Results may differ from a plain program's by a relative error of at most 0.0076.
Values may be sent and summed in bfloat16 or wider, within the bound.
No kernel may reach another device: no remote copies, remote signals or barrier semaphores. Data moves between devices by JAX's collectives and lax.ppermute only.
A program may use at most 64 MiB of HBM per device.

v0:
```python
import jax
import jax.numpy as jnp
from jax import lax
from jax.sharding import PartitionSpec as P

HEADS = 12
HEAD = 64


def apply_projection(data, weight):
    flattened_rows = data.reshape(-1, data.shape[-1])
    return (
        jnp.dot(flattened_rows, weight, preferred_element_type=jnp.float32)
        .astype(jnp.bfloat16)
        .reshape(data.shape)
    )


def separate_heads(arr):
    return arr.reshape(arr.shape[0], arr.shape[1], HEADS, -1)


def normalize(logits, scale):
    scaled = logits * scale
    shifted = scaled - jnp.max(scaled, axis=-1, keepdims=True)
    expo = jnp.exp(shifted)
    return (expo / jnp.sum(expo, axis=-1, keepdims=True)).astype(jnp.bfloat16)


def per_device(alignment_embeddings, query_matrix, key_matrix, value_matrix, output_matrix):
    row_total = alignment_embeddings.shape[0]
    column_total = alignment_embeddings.shape[1]
    query_rows = separate_heads(apply_projection(alignment_embeddings, query_matrix))
    local_key_rows = apply_projection(alignment_embeddings, key_matrix)
    local_value_rows = apply_projection(alignment_embeddings, value_matrix)
    total_rows = row_total * lax.axis_size("seq")
    scale = HEAD ** (-0.5) / jnp.sqrt(jnp.float32(total_rows))
    partial_logits = jnp.einsum(
        "rihd,rjhd->hij",
        query_rows,
        separate_heads(lax.all_gather(local_key_rows, "res", axis=1, tiled=True)),
        preferred_element_type=jnp.float32,
    )
    logits = lax.psum(partial_logits, "seq")
    probs = normalize(logits, scale)
    mixed = jnp.einsum(
        "hij,rjhd->rihd",
        probs,
        separate_heads(lax.all_gather(local_value_rows, "res", axis=1, tiled=True)),
        preferred_element_type=jnp.float32,
    )
    attended = mixed.astype(jnp.bfloat16).reshape(row_total, column_total, -1)
    return apply_projection(attended, output_matrix)


def solution(mesh):
    return jax.shard_map(
        per_device,
        mesh=mesh,
        in_specs=(P("seq", "res", None), P(), P(), P(), P()),
        out_specs=P("seq", "res", None),
        check_vma=False,
    )
```

profile of v0, /device:TPU:1, one launch (start us, length us, event | category | flops | bytes accessed | tf_op | source)
XLA Modules:
  0.0 616.7 jit_solution(11597637677404840972)
XLA Ops:
  6.5 0.0 copy-start
  6.5 0.0 all-gather.5.cloned.1.call-start
  6.5 1.3 copy-done
  7.8 1.9 convolution_convert_fusion.1
  9.7 1.2 copy.9
  10.9 0.0 all-gather.5.cloned.1.call-update
  10.9 0.0 all-reduce.2.cloned.1.call-start
  11.0 2.3 convolution_convert_fusion.2
  13.2 0.3 copy.8
  13.5 0.2 reshape_reshape.6
  13.7 132.5 %all-gather.5.cloned.1.call-done = bf16[4,1024,768]{1,2,0:T(8,128)(2,1)} async-done(((bf16[4,128,768]{1,2,0:T(8,128)(2,1)}), bf16[4,1024,768]{1,2,0:T(8,128)(2,1)}) %all-gather.5.cloned.1.call-update) | async-done | bytes 6291472 | tf_op jit(solution)/shard_map/all_gather | solution.py:41
  146.2 6.5 %fusion.10 = f32[12,128,1024]{2,1,0:T(8,128)} fusion(bf16[4,1024,12,64]{1,3,2,0:T(8,128)(2,1)} %bitcast.36, bf16[4,128,12,64]{1,0,3,2:T(4,128)(2,1)S(1)} %reshape_reshape.6), kind=kOutput, calls=%fused_computation.11 | convolution fusion | flops 805306368 | bytes 13369344 | tf_op jit(solution)/shard_map/rihd,rjhd->hij/dot_general | solution.py:38
  152.7 0.0 copy-start.1
  152.7 0.0 all-reduce.2.cloned.1.call-update
  152.8 0.0 all-gather.3.cloned.1.call-start
  152.8 1.2 copy-done.1
  154.0 1.9 convolution_convert_fusion.3
  155.9 1.2 copy.7
  157.1 0.0 all-gather.3.cloned.1.call-update
  157.1 307.8 %all-reduce.2.cloned.1.call-done = f32[12,128,1024]{2,1,0:T(8,128)} async-done(((f32[12,128,1024]{2,1,0:T(8,128)}), f32[12,128,1024]{2,1,0:T(8,128)}) %all-reduce.2.cloned.1.call-update) | async-done | bytes 6291472 | tf_op jit(solution)/shard_map/psum | solution.py:44
  464.9 6.4 %fusion.34 = f32[12,128]{1,0:T(8,128)S(1)} fusion(f32[12,128,1024]{2,1,0:T(8,128)} %all-reduce.2.cloned.1.call-done), kind=kOutput, calls=%fused_computation.24 | output fusion | flops 6292479 | bytes 6297600 | tf_op jit(solution)/shard_map/sub | solution.py:25
  471.4 126.9 %all-gather.3.cloned.1.call-done = bf16[4,1024,768]{1,2,0:T(8,128)(2,1)} async-done(((bf16[4,128,768]{1,2,0:T(8,128)(2,1)}), bf16[4,1024,768]{1,2,0:T(8,128)(2,1)}) %all-gather.3.cloned.1.call-update) | async-done | bytes 6291472 | tf_op jit(solution)/shard_map/all_gather | solution.py:49
  598.3 0.0 copy-start.2
  598.3 9.5 %fusion.18 = bf16[4,128,12,64]{1,3,0,2:T(8,128)(2,1)S(1)} fusion(f32[12,128]{1,0:T(8,128)S(1)} %fusion.34, bf16[4,1024,12,64]{1,3,2,0:T(8,128)(2,1)} %bitcast.40, f32[12,128,1024]{2,1,0:T(8,128)} %all-reduce.2.cloned.1.call-done), kind=kOutput, calls=%fused_computation.17 | convolution fusion | flops 813566464 | bytes 13375488 | tf_op jit(solution)/shard_map/hij,rjhd->rihd/dot_general | solution.py:46
  607.8 0.6 copy.13
  608.5 0.0 copy-done.2
  608.5 1.7 convolution_convert_fusion
Async XLA Ops:
  6.5 1.3 copy-start
  6.5 139.7 %all-gather.5.cloned.1.call-start = ((), (), s32[]{:S(2)}) async-start(), calls=%async_computation.1 | async-start | bytes 7077888 | tf_op jit(solution)/shard_map/all_gather | solution.py:41
  10.9 454.0 %all-reduce.2.cloned.1.call-start = ((), (), s32[]{:S(2)}) async-start(), calls=%async_computation.2 | async-start | bytes 12582912 | tf_op jit(solution)/shard_map/psum | solution.py:44
  152.7 1.3 copy-start.1
  152.8 445.5 %all-gather.3.cloned.1.call-start = ((), (), s32[]{:S(2)}) async-start(), calls=%async_computation | async-start | bytes 7077888 | tf_op jit(solution)/shard_map/all_gather | solution.py:49
  598.3 10.2 %copy-start.2 = (bf16[768,768]{1,0:T(8,128)(2,1)S(1)}, bf16[768,768]{1,0:T(8,128)(2,1)}, u32[]{:S(2)}) copy-start(bf16[768,768]{1,0:T(8,128)(2,1)} %param.9) | copy-start | bytes 3538948
Sparse Core Ops, SparseCore 0:
  11.0 135.1 all-gather.4
  152.9 312.0 all-reduce.1
  466.7 131.5 all-gather.2
where the time goes:
time: 617 us
  waiting for transfers between devices  567 us (92%)
  matrix products  23.8 us (4%)
  between operations  13.2 us (2%)
  other arithmetic  6.41 us (1%)
    psum x1, waiting for transfers between devices, per_device(): logits = lax.psum(partial_logits, 'seq')  308 us
    all_gather x1, waiting for transfers between devices, per_device(): lax.all_gather(local_key_rows, 'res', axis=1, tiled=True)  133 us
    all_gather x1, waiting for transfers between devices, per_device(): lax.all_gather(local_value_rows, 'res', axis=1, tiled=True)  127 us
  transfers between devices with their start and end apart: 3, of which 3 were waited for; matrix products, arithmetic and copies ran while one was open for 2% of the time, Pallas kernels for 0%

commit v1 on v0

v1 whole, which is shorter than its diff:
```python
import functools

import jax
import jax.numpy as jnp
from jax import lax
from jax.experimental import pallas as pl
from jax.experimental.pallas import tpu as pltpu
from jax.sharding import Mesh, PartitionSpec as P

HEADS = 12
HEAD = 64
AXES = ("z_hi", "y", "core", "x", "z_lo")
SIZES = (4, 4, 2, 4, 2)
SIZE = dict(zip(AXES, SIZES))
BF16 = jnp.bfloat16
F32 = jnp.float32
PARTS = 4
VMEM = 24 << 20


def shift(arr, axis, step):
    n = SIZE[axis]
    return lax.ppermute(arr, axis, [(i, (i + step) % n) for i in range(n)])


def whole(shape):
    return pl.BlockSpec(shape, lambda *_: (0,) * len(shape))


def call(body, place, ins, in_specs, outs, out_specs, grid, flops, name, late=()):
    moved = sum(a.size * a.dtype.itemsize for a in ins)
    moved += sum(o.size * o.dtype.itemsize for o in outs)
    n = 1 + len(ins)

    def run(*refs):
        body(*refs[:n], *refs[n + len(late) :])

    in_specs = [*in_specs] + [pl.BlockSpec(memory_space=pl.ANY)] * len(late)
    return pl.pallas_call(
        run,
        out_shape=outs,
        grid_spec=pltpu.PrefetchScalarGridSpec(
            num_scalar_prefetch=1, grid=grid, in_specs=in_specs, out_specs=out_specs
        ),
        compiler_params=pltpu.CompilerParams(vmem_limit_bytes=VMEM),
        cost_estimate=pl.CostEstimate(flops=flops, bytes_accessed=moved, transcendentals=0),
        name=name,
    )(place, *ins, *late)


def tie(arrays, late):
    n = len(arrays)
    free = pl.BlockSpec(memory_space=pl.ANY)
    return pl.pallas_call(
        lambda *refs: None,
        out_shape=[jax.ShapeDtypeStruct(a.shape, a.dtype) for a in arrays],
        in_specs=[free] * (n + 1),
        out_specs=[free] * n,
        input_output_aliases={i: i for i in range(n)},
        name="tie",
    )(*arrays, late)


def rel(index):
    return lax.rem(index + PARTS, PARTS)


def project_body(kinds, blocks, place, *refs):
    xs = refs[: 2 * blocks]
    weights = refs[2 * blocks : 2 * blocks + len(kinds)]
    outs = refs[2 * blocks + len(kinds) :]
    y = place[1]
    seqs, rows, width = xs[0].shape
    lanes = 2 * HEAD
    pairs = weights[0].shape[1] // lanes
    group = rows // PARTS
    for b in range(blocks):
        for half in range(2):
            x = xs[2 * b + half][...].reshape(seqs * rows, width)
            for kind, weight, out in zip(kinds, weights, outs):
                got = jnp.dot(x, weight[...], preferred_element_type=F32).astype(BF16)
                for s in range(seqs):
                    at = (half * seqs + s) * lanes
                    for p in range(pairs):
                        part = got[s * rows : (s + 1) * rows, p * lanes : (p + 1) * lanes]
                        if kind != "q":
                            out[p, b * rows : (b + 1) * rows, at : at + lanes] = part
                            continue
                        first = lax.broadcasted_iota(jnp.int32, part.shape, 1) < HEAD
                        for h in range(2):
                            kept = jnp.where(first == (h == 0), part, jnp.zeros_like(part))
                            for a in range(PARTS):
                                out[p, rel(a - y), h, :, at : at + lanes] = kept[
                                    a * group : (a + 1) * group
                                ]


def project(place, blocks, weights, kinds, name, late=()):
    seqs, rows, width = blocks[0][0].shape
    own = width // 2
    pairs, span = HEADS // 4, 2 * seqs * 2 * HEAD
    ins = [a for block in blocks for a in block] + list(weights)
    in_specs = [whole((seqs, rows, width))] * (2 * len(blocks))
    in_specs += [pl.BlockSpec((width, own), lambda i, s: (0, s[0]))] * len(weights)
    shapes = [
        (pairs, PARTS, 2, rows // PARTS, span)
        if k == "q"
        else (pairs, rows * len(blocks), span)
        for k in kinds
    ]
    flops = 2 * len(blocks) * 2 * seqs * rows * width * own * len(kinds)
    return call(
        functools.partial(project_body, kinds, len(blocks)),
        place,
        ins,
        in_specs,
        [jax.ShapeDtypeStruct(s, BF16) for s in shapes],
        [whole(s) for s in shapes],
        (1,),
        flops,
        name,
        late,
    )


def logits_body(blocks, place, *refs):
    queries, keys, outs = refs[:2], refs[2 : 2 + blocks], refs[2 + blocks :]
    half = outs[0].shape[2]
    k = jnp.concatenate([ref[0] for ref in keys], axis=0)
    for i, ref in enumerate(queries):
        q = ref[0].reshape(PARTS * half, -1)
        got = lax.dot_general(q, k, (((1,), (1,)), ((), ())), preferred_element_type=F32)
        for d, out in enumerate(outs):
            out[i, 0] = got[d * half : (d + 1) * half].astype(BF16)


def make_logits(place, queries, keys, name):
    pairs, _, _, group, span = queries[0].shape
    rows = sum(k.shape[1] for k in keys)
    half = 2 * group
    shape = jax.ShapeDtypeStruct((2, pairs, half, rows), BF16)
    return call(
        functools.partial(logits_body, len(keys)),
        place,
        [*queries, *keys],
        [pl.BlockSpec((1, PARTS, 2, group, span), lambda p, s: (p, 0, 0, 0, 0))] * 2
        + [pl.BlockSpec((1, k.shape[1], span), lambda p, s: (p, 0, 0)) for k in keys],
        [shape] * PARTS,
        [pl.BlockSpec((2, 1, half, rows), lambda p, s: (0, p, 0, 0))] * PARTS,
        (pairs,),
        2 * pairs * 2 * PARTS * half * span * rows,
        name,
    )


def add_body(count, place, *refs):
    out, parts = refs[-1], refs[:-1]
    z_lo = place[3]
    sums = []
    for n in range(0, len(parts), count):
        total = parts[n][...].astype(F32)
        for ref in parts[n + 1 : n + count]:
            total += ref[...].astype(F32)
        sums.append(total)
    total = jnp.concatenate(sums, axis=-1).astype(BF16)
    share = out.shape[2]
    for i in range(2):
        for z in range(PARTS):
            out[z, i ^ z_lo] = total[i, z * share : (z + 1) * share]


def add_parts(place, groups):
    parts = [a for g in groups for a in g]
    rows = parts[0].shape[1]
    cols = sum(g[0].shape[2] for g in groups)
    shape = (PARTS, 2, rows // PARTS, cols)
    return call(
        functools.partial(add_body, PARTS),
        place,
        parts,
        [whole(a.shape) for a in parts],
        [jax.ShapeDtypeStruct(shape, BF16)],
        [whole(shape)],
        (1,),
        sum(a.size for a in parts),
        "add_over_y",
    )[0]


def softmax_body(scale, place, parts, out):
    z_lo = place[3]
    sides = []
    for side in (z_lo, 1 - z_lo):
        total = parts[0, side].astype(F32)
        for z in range(1, PARTS):
            total += parts[z, side].astype(F32)
        sides.append(total)
    scaled = jnp.concatenate(sides, axis=-1) * scale
    expo = jnp.exp(scaled - jnp.max(scaled, axis=-1, keepdims=True))
    out[...] = (expo / jnp.sum(expo, axis=-1, keepdims=True)).astype(BF16)


def softmax(place, parts, scale):
    shape = (parts.shape[2], 2 * parts.shape[3])
    return call(
        functools.partial(softmax_body, scale),
        place,
        [parts],
        [whole(parts.shape)],
        [jax.ShapeDtypeStruct(shape, BF16)],
        [whole(shape)],
        (1,),
        parts.size * 8,
        "softmax",
    )[0]


def order_body(place, *refs):
    out, parts = refs[-1], refs[:-1]
    for d, ref in enumerate(parts):
        out[rel(place[2] - d)] = ref[...]


def order(place, parts):
    shape = (PARTS, *parts[0].shape)
    return call(
        order_body,
        place,
        parts,
        [whole(a.shape) for a in parts],
        [jax.ShapeDtypeStruct(shape, BF16)],
        [whole(shape)],
        (1,),
        0,
        "order",
    )[0]


def mix_body(place, *refs):
    probs, values, outs = refs[:PARTS], refs[PARTS:-2], refs[-2:]
    y = place[1]
    group = probs[0].shape[1] // 2
    lanes = 2 * HEAD
    seqs = outs[0].shape[0]
    p = jnp.concatenate([ref[0] for ref in probs], axis=0)
    v = jnp.concatenate([ref[0] for ref in values], axis=0)
    got = jnp.dot(p, v, preferred_element_type=F32)
    first = lax.broadcasted_iota(jnp.int32, (group, lanes), 1) < HEAD
    for d in range(PARTS):
        at = pl.multiple_of(rel(y - d) * group, group)
        for s in range(2 * seqs):
            one, two = (
                got[(2 * d + h) * group : (2 * d + h + 1) * group, s * lanes : (s + 1) * lanes]
                for h in range(2)
            )
            outs[s // seqs][s % seqs, pl.ds(at, group), :] = jnp.where(first, one, two).astype(BF16)


def mix(place, probs, values, seqs):
    pairs, half, cols = probs[0].shape
    span = values[0].shape[2]
    rows = PARTS * half // 2
    lanes = 2 * HEAD
    shape = jax.ShapeDtypeStruct((seqs, rows, pairs * lanes), BF16)
    return call(
        mix_body,
        place,
        [*probs, *values],
        [pl.BlockSpec((1, half, cols), lambda p, s: (p, 0, 0))] * PARTS
        + [pl.BlockSpec((1, v.shape[1], span), lambda p, s: (p, 0, 0)) for v in values],
        [shape] * 2,
        [pl.BlockSpec((seqs, rows, lanes), lambda p, s: (0, 0, p))] * 2,
        (pairs,),
        2 * pairs * PARTS * half * cols * span,
        "mix",
    )


def finish_body(place, mine, theirs, weight_mine, weight_theirs, out):
    seqs, rows, own = mine.shape
    got = jnp.dot(mine[...].reshape(seqs * rows, own), weight_mine[...], preferred_element_type=F32)
    got += jnp.dot(
        theirs[...].reshape(seqs * rows, own), weight_theirs[...], preferred_element_type=F32
    )
    out[...] = got.astype(BF16).reshape(out.shape)


def finish(place, mine, theirs, weight):
    seqs, rows, own = mine.shape
    width = weight.shape[1]
    return call(
        finish_body,
        place,
        [mine, theirs, weight, weight],
        [pl.BlockSpec((1, rows, own), lambda r, s: (r, 0, 0))] * 2
        + [
            pl.BlockSpec((own, width), lambda r, s: (s[0], 0)),
            pl.BlockSpec((own, width), lambda r, s: (1 - s[0], 0)),
        ],
        [jax.ShapeDtypeStruct((seqs, rows, width), BF16)],
        [pl.BlockSpec((1, rows, width), lambda r, s: (r, 0, 0))],
        (seqs,),
        2 * seqs * rows * width * width,
        "finish",
    )[0]


def ring_table(axis_of):
    return [
        (c * SIZE["x"] + i, c * SIZE["x"] + (i + (1 if c == axis_of else -1)) % SIZE["x"])
        for c in range(2)
        for i in range(SIZE["x"])
    ]


def send_x(arr, way):
    return lax.ppermute(arr, ("core", "x"), ring_table(way))


def per_device(data, query_matrix, key_matrix, value_matrix, output_matrix):
    seqs, rows, width = data.shape
    place = jnp.stack([lax.axis_index(a) for a in ("core", "y", "z_hi", "z_lo")])
    place = place.astype(jnp.int32)

    def swap(arr):
        return shift(arr, "core", 1)

    first, second = send_x(data, 0), send_x(data, 1)
    partner = shift(data, "z_lo", 1)
    own = (data, swap(data))
    queries, keys, values = project(
        place, [own], [query_matrix, key_matrix, value_matrix], "qkv", "project_own"
    )
    first, second, partner = tie([first, second, partner], queries)
    far = send_x(first, 0)
    near = [(first, swap(second)), (second, swap(first))]
    partner2 = (partner, swap(partner))
    (partner_queries,) = project(place, [partner2], [query_matrix], "q", "project_partner")
    (near_keys,) = project(place, near, [key_matrix], "k", "project_near")
    both = [queries, partner_queries]
    near_logits = make_logits(place, both, [keys, near_keys], "logits_near")
    (far,) = tie([far], near_logits[0])
    far2 = (far, swap(far))
    (far_keys,) = project(place, [far2], [key_matrix], "k", "project_far")
    far_logits = make_logits(place, both, [far_keys], "logits_far")

    def over_y(parts):
        parts = [a.reshape(2, -1, a.shape[-1]) for a in parts]
        return [parts[0]] + [shift(parts[d], "y", d) for d in range(1, PARTS)]

    groups = [over_y(near_logits), over_y(far_logits)]
    (z_own,) = project(place, [partner2], [value_matrix], "v", "values_partner", far_logits[:1])
    sent = add_parts(place, groups)
    (near_values,) = project(place, [*near, far2], [value_matrix], "v", "values_near", [sent])
    (z_sent,) = tie([z_own], sent)
    z_first, z_second = send_x(z_sent, 0), send_x(z_sent, 1)

    sent = sent.reshape(2 * PARTS, *sent.shape[2:])
    got = lax.all_to_all(sent, ("z_hi", "z_lo"), 0, 0, tiled=True)
    got = got.reshape(PARTS, 2, *got.shape[1:])
    all_rows = seqs * lax.axis_size(("z_hi", "y", "core"))
    probs = softmax(place, got, HEAD ** (-0.5) * all_rows ** (-0.5))
    (z_first,) = tie([z_first], probs)
    z_far = send_x(z_first, 0)
    z_values = [z_sent, z_first, z_second, z_far]
    probs = order(place, [probs] + [shift(probs, "z_hi", d) for d in range(1, PARTS)])
    probs = probs.reshape(HEADS // 4, 2 * rows // PARTS, probs.shape[-1])
    probs = [probs] + [shift(probs, "y", d) for d in range(1, PARTS)]
    mine, theirs = mix(place, probs, [values, near_values, *z_values], seqs)
    return finish(place, mine, swap(theirs), output_matrix)


def solution(mesh):
    fine = Mesh(mesh.devices.reshape(SIZES), AXES)
    spec = P(("z_hi", "y", "core"), ("x", "z_lo"), None)
    return jax.shard_map(
        per_device,
        mesh=fine,
        in_specs=(spec, P(), P(), P(), P()),
        out_specs=spec,
        check_vma=False,
    )
```

time: 617 us -> 136 us (0.22)
  waiting for transfers between devices: 567 us -> 47.7 us
  starting transfers between devices: 0.09 us -> 36.1 us
  Pallas kernels: 0 us -> 30.1 us
  matrix products: 23.8 us -> 0 us
  local copies, waits for them, and re-layouts: 5.85 us -> 21.4 us
  between operations: 13.2 us -> 0.41 us
  other arithmetic: 6.41 us -> 0.08 us
    psum x1 -> x0, waiting for transfers between devices: 308 us -> none  [per_device(): logits = lax.psum(partial_logits, 'seq')]
    all_gather x2 -> x0, waiting for transfers between devices: 259 us -> none  [the longest x1 133 us: per_device(): lax.all_gather(local_key_rows, 'res', axis=1, tiled=True)]
    ppermute x0 -> x25, waiting for transfers between devices: none -> 33.5 us  [the longest x19 26.2 us: shift(): return lax.ppermute(arr, axis, [(i, (i + step) % n) for i in range(n)])]
    pallas_call x0 -> x17, Pallas kernels: none -> 30.1 us  [the longest x13 30.1 us: call(): pl.pallas_call(run, out_shape=outs, grid_spec=pltpu.PrefetchScalarGridSpe...]
    ppermute x0 -> x25, starting transfers between devices: none -> 27.7 us  [the longest x19 23.7 us: shift(): return lax.ppermute(arr, axis, [(i, (i + step) % n) for i in range(n)])]
    dot_general x6 -> x0, matrix products: 23.8 us -> none  [the longest x1 9.51 us: per_device(): jnp.einsum('hij,rjhd->rihd', probs, separate_heads(lax.all_gather(local_v...]
    unnamed x6 -> x86, local copies, waits for them, and re-layouts: 2.47 us -> 21.4 us
    all_to_all x0 -> x1, waiting for transfers between devices: none -> 14.2 us  [per_device(): got = lax.all_to_all(sent, ('z_hi', 'z_lo'), 0, 0, tiled=True)]
  transfers between devices with their start and end apart: 3 -> 26, of which waited for: 3 -> 13; matrix products, arithmetic and copies ran while one was open for 2% -> 0% of each run, Pallas kernels for 0% -> 16%
where the time goes in v1:
time: 136 us
  waiting for transfers between devices  47.7 us (35%)
  starting transfers between devices  36.1 us (27%)
  Pallas kernels  30.1 us (22%)
  local copies, waits for them, and re-layouts  21.4 us (16%)
    pallas_call x13, Pallas kernels, call(): pl.pallas_call(run, out_shape=outs, grid_spec=pltpu.PrefetchScalarGridSpe...  30.1 us
    ppermute x19, waiting for transfers between devices, shift(): return lax.ppermute(arr, axis, [(i, (i + step) % n) for i in range(n)])  26.2 us
    ppermute x19, starting transfers between devices, shift(): return lax.ppermute(arr, axis, [(i, (i + step) % n) for i in range(n)])  23.7 us
    unnamed x86, local copies, waits for them, and re-layouts  21.4 us
    all_to_all x1, waiting for transfers between devices, per_device(): got = lax.all_to_all(sent, ('z_hi', 'z_lo'), 0, 0, tiled=True)  14.2 us
    all_to_all x1, starting transfers between devices, per_device(): got = lax.all_to_all(sent, ('z_hi', 'z_lo'), 0, 0, tiled=True)  8.41 us
    ppermute x6, waiting for transfers between devices, send_x(): return lax.ppermute(arr, ('core', 'x'), ring_table(way))  7.29 us
    ppermute x6, starting transfers between devices, send_x(): return lax.ppermute(arr, ('core', 'x'), ring_table(way))  3.99 us
  transfers between devices with their start and end apart: 26, of which 13 were waited for; matrix products, arithmetic and copies ran while one was open for 0% of the time, Pallas kernels for 16%

profile of v1, /device:TPU:1, one launch (start us, length us, event | category | flops | bytes accessed | tf_op | source)
XLA Modules:
  0.0 135.8 jit_solution(3745968698731314172)
XLA Ops:
  0.0 3.2 %collective-permute-start = (bf16[4,128,768]{2,1,0:T(8,128)(2,1)}, bf16[4,128,768]{2,1,0:T(8,128)(2,1)S(1)}, u32[]{:S(2)}, u32[]{:S(2)}) collective-permute-start(bf16[4,128,768]{2,1,0:T(8,128)(2,1)} %refs_1_.1), channel_id=1, source_target_pairs={{0,8},{8,0},{1,9},{9,1},{2,10},{10,2},{3,11},{11,3},{4,12},{12,4},... | collective-permute-start | bytes 2359304 | tf_op jit(solution)/shard_map/ppermute | solution.py:23
  5.7 1.3 copy-done.15
  10.7 3.4 %project_own.1 = (bf16[3,4,2,32,1024]{4,3,2,1,0:T(8,128)(2,1)S(1)}, bf16[3,128,1024]{2,1,0:T(8,128)(2,1)S(1)}, bf16[3,128,1024]{2,1,0:T(8,128)(2,1)S(1)}) custom-call(s32[4]{0:T(128)S(1)} %pad_add_fusion.refs_0_, bf16[4,128,768]{2,1,0:T(8,128)(2,1)S(1)} %copy-done.40, bf16[4,128,768]{2,1,0:T(8,128)(2,1)S(1)} %collective-permute-done.refs_2_, ...), custom_call_target="tpu_custom_call" | custom-call | flops 1811939328 | bytes 8257536 | tf_op jit(solution)/shard_map/project_own/pallas_call | solution.py:39
  17.1 5.5 %collective-permute-done.1.refs_0_ = bf16[4,128,768]{2,1,0:T(8,128)(2,1)S(1)} collective-permute-done((bf16[4,128,768]{2,1,0:T(8,128)(2,1)}, bf16[4,128,768]{2,1,0:T(8,128)(2,1)S(1)}, u32[]{:S(2)}, u32[]{:S(2)}) %collective-permute-start.1) | collective-permute-done | bytes 786464 | tf_op jit(solution)/shard_map/ppermute | solution.py:317
  22.6 1.8 %collective-permute-done.2.refs_1_ = bf16[4,128,768]{2,1,0:T(8,128)(2,1)S(1)} collective-permute-done((bf16[4,128,768]{2,1,0:T(8,128)(2,1)}, bf16[4,128,768]{2,1,0:T(8,128)(2,1)S(1)}, u32[]{:S(2)}, u32[]{:S(2)}) %collective-permute-start.2) | collective-permute-done | bytes 786464 | tf_op jit(solution)/shard_map/ppermute | solution.py:317
  26.8 1.3 collective-permute-start.10
  29.5 1.7 %project_partner.1.refs_2_ = bf16[3,4,2,32,1024]{4,3,2,1,0:T(8,128)(2,1)S(1)} custom-call(s32[4]{0:T(128)S(1)} %pad_add_fusion.refs_0_, bf16[4,128,768]{2,1,0:T(8,128)(2,1)S(1)} %copy-done.9, bf16[4,128,768]{2,1,0:T(8,128)(2,1)S(1)} %collective-permute-done.4.refs_2_, bf16[768,768]{1,0:T(8,128)(2,1)S(1)} %copy-done.31), custom_call_target="tpu_custom_call" | custom-call | flops 603979776 | bytes 4325376 | tf_op jit(solution)/shard_map/project_partner/pallas_call | solution.py:39
  31.4 2.4 %project_near.1.refs_4_ = bf16[3,256,1024]{2,1,0:T(8,128)(2,1)S(1)} custom-call(s32[4]{0:T(128)S(1)} %pad_add_fusion.refs_0_, bf16[4,128,768]{2,1,0:T(8,128)(2,1)S(1)} %copy-done.3, bf16[4,128,768]{2,1,0:T(8,128)(2,1)S(1)} %collective-permute-done.5.refs_2_, bf16[4,128,768]{2,1,0:T(8,128)(2,1)S(1)} %copy-done.6, ...), custom_call_target="tpu_custom_call" | custom-call | flops 1207959552 | bytes 5898240 | tf_op jit(solution)/shard_map/project_near/pallas_call | solution.py:39
  33.8 2.9 %logits_near.1 = (bf16[2,3,64,384]{3,2,1,0:T(8,128)(2,1)S(1)}, bf16[2,3,64,384]{3,2,1,0:T(8,128)(2,1)S(1)}, bf16[2,3,64,384]{3,2,1,0:T(8,128)(2,1)S(1)}, bf16[2,3,64,384]{3,2,1,0:T(8,128)(2,1)S(1)}) custom-call(s32[4]{0:T(128)S(1)} %pad_add_fusion.refs_0_, bf16[3,4,2,32,1024]{4,3,2,1,0:T(8,128)(2,1)S(1)} %copy-done.1, ...), custom_call_target="tpu_custom_call" | custom-call | flops 1207959552 | bytes 6684672 | tf_op jit(solution)/shard_map/logits_near/pallas_call | solution.py:39
  38.8 1.5 %collective-permute-start.11 = (bf16[4,128,768]{2,1,0:T(8,128)(2,1)}, bf16[4,128,768]{2,1,0:T(8,128)(2,1)S(1)}, u32[]{:S(2)}, u32[]{:S(2)}) collective-permute-start(bf16[4,128,768]{2,1,0:T(8,128)(2,1)} %tie.5.refs_1_.refs_5_), channel_id=1, source_target_pairs={{0,8},{8,0},{1,9},{9,1},{2,10},{10,2},{3,11},{11,3},{4,12},{12,4},... | collective-permute-start | bytes 2359304 | tf_op jit(solution)/shard_map/ppermute | solution.py:23
  40.7 2.6 %collective-permute-start.8 = (bf16[2,192,384]{2,1,0:T(8,128)(2,1)}, bf16[2,192,384]{2,1,0:T(8,128)(2,1)S(1)}, u32[]{:S(2)}, u32[]{:S(2)}) collective-permute-start(bf16[2,192,384]{2,1,0:T(8,128)(2,1)} %bitcast.24), channel_id=1, source_target_pairs={{0,32},{16,48},{32,0},{48,16},{1,33},{17,49},{33,1},{49,17},{2,34}... | collective-permute-start | bytes 884744 | tf_op jit(solution)/shard_map/ppermute | solution.py:23
  44.4 1.3 copy-done.20
  45.7 2.7 %project_far.1.refs_3_ = bf16[3,128,1024]{2,1,0:T(8,128)(2,1)S(1)} custom-call(s32[4]{0:T(128)S(1)} %pad_add_fusion.refs_0_, bf16[4,128,768]{2,1,0:T(8,128)(2,1)} %tie.5.refs_1_.refs_5_, bf16[4,128,768]{2,1,0:T(8,128)(2,1)S(1)} %collective-permute-done.11.refs_2_.refs_6_, bf16[768,768]{1,0:T(8,128)(2,1)S(1)} %copy-done.20), custom_call_target="tpu_custom_call" | custom-call | flops 603979776 | bytes 3538944 | tf_op jit(solution)/shard_map/project_far/pallas_call | solution.py:39
  49.3 1.9 %logits_far.1 = (bf16[2,3,64,128]{3,2,1,0:T(8,128)(2,1)S(1)}, bf16[2,3,64,128]{3,2,1,0:T(8,128)(2,1)S(1)}, bf16[2,3,64,128]{3,2,1,0:T(8,128)(2,1)S(1)}, bf16[2,3,64,128]{3,2,1,0:T(8,128)(2,1)S(1)}) custom-call(s32[4]{0:T(128)S(1)} %pad_add_fusion.refs_0_, bf16[3,4,2,32,1024]{4,3,2,1,0:T(8,128)(2,1)S(1)} %copy-done.1, ...), custom_call_target="tpu_custom_call" | custom-call | flops 402653184 | bytes 4325376 | tf_op jit(solution)/shard_map/logits_far/pallas_call | solution.py:39
  52.5 1.9 %collective-permute-start.14 = (bf16[2,192,128]{2,1,0:T(8,128)(2,1)S(1)}, bf16[2,192,128]{2,1,0:T(8,128)(2,1)S(1)}, u32[]{:S(2)}, u32[]{:S(2)}) collective-permute-start(bf16[2,192,128]{2,1,0:T(8,128)(2,1)S(1)} %bitcast.26), channel_id=1, source_target_pairs={{0,48},{16,0},{32,16},{48,32},{1,49},{17,1},{33,17},{49,33},{2,50}... | collective-permute-start | bytes 294920 | tf_op jit(solution)/shard_map/ppermute | solution.py:23
  54.4 1.6 %values_partner.1.refs_0_ = bf16[3,128,1024]{2,1,0:T(8,128)(2,1)S(1)} custom-call(s32[4]{0:T(128)S(1)} %pad_add_fusion.refs_0_, bf16[4,128,768]{2,1,0:T(8,128)(2,1)S(1)} %copy-done.10, bf16[4,128,768]{2,1,0:T(8,128)(2,1)S(1)} %copy-done.29, bf16[768,768]{1,0:T(8,128)(2,1)S(1)} %copy-done.16, bf16[2,3,64,128]{3,2,1,0:T(8,128)(2,1)S(1)} %get-tuple-element.30.refs_4_), custom_call_target="tpu_custom_call" | custom-call | flops 603979776 | bytes 3538944 | tf_op jit(solution)/shard_map/values_partner/pallas_call | solution.py:39
  57.1 2.6 %collective-permute-done.12.refs_6_ = bf16[2,192,128]{2,1,0:T(8,128)(2,1)S(1)} collective-permute-done((bf16[2,192,128]{2,1,0:T(8,128)(2,1)S(1)}, bf16[2,192,128]{2,1,0:T(8,128)(2,1)S(1)}, u32[]{:S(2)}, u32[]{:S(2)}) %collective-permute-start.12) | collective-permute-done | bytes 98336 | tf_op jit(solution)/shard_map/ppermute | solution.py:23
  59.7 1.6 %collective-permute-done.13.refs_7_ = bf16[2,192,128]{2,1,0:T(8,128)(2,1)S(1)} collective-permute-done((bf16[2,192,128]{2,1,0:T(8,128)(2,1)S(1)}, bf16[2,192,128]{2,1,0:T(8,128)(2,1)S(1)}, u32[]{:S(2)}, u32[]{:S(2)}) %collective-permute-start.13) | collective-permute-done | bytes 98336 | tf_op jit(solution)/shard_map/ppermute | solution.py:23
  63.1 8.4 %all-to-all-start = ((bf16[8,48,512]{2,1,0:T(8,128)(2,1)}), bf16[8,48,512]{2,1,0:T(8,128)(2,1)S(1)}, u32[]{:S(2)}, u32[]{:S(2)}) async-start(bf16[8,48,512]{2,1,0:T(8,128)(2,1)} %bitcast.15), calls=%async_computation | async-start | bytes 786432 | tf_op jit(solution)/shard_map/all_to_all | solution.py:359
  72.4 14.2 %all-to-all-done = bf16[8,48,512]{2,1,0:T(8,128)(2,1)S(1)} async-done(((bf16[8,48,512]{2,1,0:T(8,128)(2,1)}), bf16[8,48,512]{2,1,0:T(8,128)(2,1)S(1)}, u32[]{:S(2)}, u32[]{:S(2)}) %all-to-all-start) | async-done | bytes 393248 | tf_op jit(solution)/shard_map/all_to_all | solution.py:359
  88.1 1.9 %collective-permute-start.16 = (bf16[48,1024]{1,0:T(8,128)(2,1)}, bf16[48,1024]{1,0:T(8,128)(2,1)S(1)}, u32[]{:S(2)}, u32[]{:S(2)}) collective-permute-start(bf16[48,1024]{1,0:T(8,128)(2,1)} %copy-done.34), channel_id=1, source_target_pairs={{0,128},{64,192},{128,0},{192,64},{1,129},{65,193},{129,1},{193,65... | collective-permute-start | bytes 294920 | tf_op jit(solution)/shard_map/ppermute | solution.py:23
  90.0 1.7 %collective-permute-start.17 = (bf16[48,1024]{1,0:T(8,128)(2,1)}, bf16[48,1024]{1,0:T(8,128)(2,1)S(1)}, u32[]{:S(2)}, u32[]{:S(2)}) collective-permute-start(bf16[48,1024]{1,0:T(8,128)(2,1)} %copy-done.34), channel_id=1, source_target_pairs={{0,192},{64,0},{128,64},{192,128},{1,193},{65,1},{129,65},{193,129... | collective-permute-start | bytes 294920 | tf_op jit(solution)/shard_map/ppermute | solution.py:23
  91.7 2.6 %collective-permute-done.15.refs_2_ = bf16[48,1024]{1,0:T(8,128)(2,1)S(1)} collective-permute-done((bf16[48,1024]{1,0:T(8,128)(2,1)}, bf16[48,1024]{1,0:T(8,128)(2,1)S(1)}, u32[]{:S(2)}, u32[]{:S(2)}) %collective-permute-start.15) | collective-permute-done | bytes 98336 | tf_op jit(solution)/shard_map/ppermute | solution.py:23
  94.3 2.9 %collective-permute-done.16.refs_3_ = bf16[48,1024]{1,0:T(8,128)(2,1)S(1)} collective-permute-done((bf16[48,1024]{1,0:T(8,128)(2,1)}, bf16[48,1024]{1,0:T(8,128)(2,1)S(1)}, u32[]{:S(2)}, u32[]{:S(2)}) %collective-permute-start.16) | collective-permute-done | bytes 98336 | tf_op jit(solution)/shard_map/ppermute | solution.py:23
  97.2 5.2 %collective-permute-done.17.refs_4_ = bf16[48,1024]{1,0:T(8,128)(2,1)S(1)} collective-permute-done((bf16[48,1024]{1,0:T(8,128)(2,1)}, bf16[48,1024]{1,0:T(8,128)(2,1)S(1)}, u32[]{:S(2)}, u32[]{:S(2)}) %collective-permute-start.17) | collective-permute-done | bytes 98336 | tf_op jit(solution)/shard_map/ppermute | solution.py:23
  103.9 4.7 %collective-permute-start.19 = (bf16[3,64,1024]{2,1,0:T(8,128)(2,1)S(1)}, bf16[3,64,1024]{2,1,0:T(8,128)(2,1)S(1)}, u32[]{:S(2)}, u32[]{:S(2)}) collective-permute-start(bf16[3,64,1024]{2,1,0:T(8,128)(2,1)S(1)} %bitcast.17), channel_id=1, source_target_pairs={{0,32},{16,48},{32,0},{48,16},{1,33},{17,49},{33,1},{49,17},{2,34}... | collective-permute-start | bytes 1179656 | tf_op jit(solution)/shard_map/ppermute | solution.py:23
  112.1 4.3 %values_near.1.refs_6_ = bf16[3,384,1024]{2,1,0:T(8,128)(2,1)S(1)} custom-call(s32[4]{0:T(128)S(1)} %pad_add_fusion.refs_0_, bf16[4,128,768]{2,1,0:T(8,128)(2,1)S(1)} %copy-done.4, bf16[4,128,768]{2,1,0:T(8,128)(2,1)S(1)} %copy-done.23, bf16[4,128,768]{2,1,0:T(8,128)(2,1)S(1)} %copy-done.7, bf16[4,128,768]{2,1,0:T(8,128)(2,1)S(1)} %copy-done.25, ...), custom_call_target="tpu_custom_call" | custom-call | flops 1811939328 | bytes 8257536 | tf_op jit(solution)/shard_map/values_near/pallas_call | solution.py:39
  116.5 9.3 %collective-permute-done.19.refs_3_ = bf16[3,64,1024]{2,1,0:T(8,128)(2,1)S(1)} collective-permute-done((bf16[3,64,1024]{2,1,0:T(8,128)(2,1)S(1)}, bf16[3,64,1024]{2,1,0:T(8,128)(2,1)S(1)}, u32[]{:S(2)}, u32[]{:S(2)}) %collective-permute-start.19) | collective-permute-done | bytes 393248 | tf_op jit(solution)/shard_map/ppermute | solution.py:23
  125.8 4.2 %mix.1 = (bf16[4,128,384]{2,1,0:T(8,128)(2,1)S(1)}, bf16[4,128,384]{2,1,0:T(8,128)(2,1)S(1)}) custom-call(s32[4]{0:T(128)S(1)} %pad_add_fusion.refs_0_, bf16[3,64,1024]{2,1,0:T(8,128)(2,1)S(1)} %bitcast.19, bf16[3,64,1024]{2,1,0:T(8,128)(2,1)S(1)} %collective-permute-done.18.refs_2_, bf16[3,64,1024]{2,1,0:T(8,128)(2,1)S(1)} %collective-permute-done.19.refs_3_, ...), custom_call_target="tpu_custom_call" | custom-call | flops 1610612736 | bytes 8650752 | tf_op jit(solution)/shard_map/mix/pallas_call | solution.py:39
  130.0 1.4 %collective-permute-start.24 = (bf16[4,128,384]{2,1,0:T(8,128)(2,1)S(1)}, bf16[4,128,384]{2,1,0:T(8,128)(2,1)S(1)}, u32[]{:S(2)}, u32[]{:S(2)}) collective-permute-start(bf16[4,128,384]{2,1,0:T(8,128)(2,1)S(1)} %get-tuple-element.36), channel_id=1, source_target_pairs={{0,8},{8,0},{1,9},{9,1},{2,10},{10,2},{3,11},{11,3},{4,12},{12,4},... | collective-permute-start | bytes 1179656 | tf_op jit(solution)/shard_map/ppermute | solution.py:23
  131.4 1.3 collective-permute-done.24.refs_2_
  132.8 3.0 %finish.1 = bf16[4,128,768]{2,1,0:T(8,128)(2,1)} custom-call(s32[4]{0:T(128)S(1)} %pad_add_fusion.refs_0_, bf16[4,128,384]{2,1,0:T(8,128)(2,1)S(1)} %get-tuple-element.35.refs_1_, bf16[4,128,384]{2,1,0:T(8,128)(2,1)S(1)} %collective-permute-done.24.refs_2_, bf16[768,768]{1,0:T(8,128)(2,1)S(1)} %copy-done.21, bf16[768,768]{1,0:T(8,128)(2,1)S(1)} %copy-done.21), custom_call_target="tpu_custom_call" | custom-call | flops 603979776 | bytes 3932160 | tf_op jit(solution)/shard_map/finish/pallas_call | solution.py:39
  (124 shorter events, 29.1 us)
Async XLA Ops:
  0.0 5.7 %collective-permute-start = (bf16[4,128,768]{2,1,0:T(8,128)(2,1)}, bf16[4,128,768]{2,1,0:T(8,128)(2,1)S(1)}, u32[]{:S(2)}, u32[]{:S(2)}) collective-permute-start(bf16[4,128,768]{2,1,0:T(8,128)(2,1)} %refs_1_.1), channel_id=1, source_target_pairs={{0,8},{8,0},{1,9},{9,1},{2,10},{10,2},{3,11},{11,3},{4,12},{12,4},... | collective-permute-start | bytes 2359304 | tf_op jit(solution)/shard_map/ppermute | solution.py:23
  3.2 19.4 %collective-permute-start.1 = (bf16[4,128,768]{2,1,0:T(8,128)(2,1)}, bf16[4,128,768]{2,1,0:T(8,128)(2,1)S(1)}, u32[]{:S(2)}, u32[]{:S(2)}) collective-permute-start(bf16[4,128,768]{2,1,0:T(8,128)(2,1)} %refs_1_.1), channel_id=1, source_target_pairs={{0,2},{2,4},{4,6},{6,0},{8,14},{10,8},{12,10},{14,12},{1,3},{3,5},... | collective-permute-start | bytes 2359304 | tf_op jit(solution)/shard_map/ppermute | solution.py:317
  4.0 20.4 %collective-permute-start.2 = (bf16[4,128,768]{2,1,0:T(8,128)(2,1)}, bf16[4,128,768]{2,1,0:T(8,128)(2,1)S(1)}, u32[]{:S(2)}, u32[]{:S(2)}) collective-permute-start(bf16[4,128,768]{2,1,0:T(8,128)(2,1)} %refs_1_.1), channel_id=1, source_target_pairs={{0,6},{2,0},{4,2},{6,4},{8,10},{10,12},{12,14},{14,8},{1,7},{3,1},... | collective-permute-start | bytes 2359304 | tf_op jit(solution)/shard_map/ppermute | solution.py:317
  4.7 19.7 %collective-permute-start.3 = (bf16[4,128,768]{2,1,0:T(8,128)(2,1)}, bf16[4,128,768]{2,1,0:T(8,128)(2,1)S(1)}, u32[]{:S(2)}, u32[]{:S(2)}) collective-permute-start(bf16[4,128,768]{2,1,0:T(8,128)(2,1)} %refs_1_.1), channel_id=1, source_target_pairs={{0,1},{1,0},{2,3},{3,2},{4,5},{5,4},{6,7},{7,6},{8,9},{9,8},{10,11... | collective-permute-start | bytes 2359304 | tf_op jit(solution)/shard_map/ppermute | solution.py:23
  25.7 2.7 %collective-permute-start.4 = (bf16[4,128,768]{2,1,0:T(8,128)(2,1)}, bf16[4,128,768]{2,1,0:T(8,128)(2,1)S(1)}, u32[]{:S(2)}, u32[]{:S(2)}) collective-permute-start(bf16[4,128,768]{2,1,0:T(8,128)(2,1)} %get-tuple-element.22.refs_1_), channel_id=1, source_target_pairs={{0,8},{8,0},{1,9},{9,1},{2,10},{10,2},{3,11},{11,3},{4,12},{12,4},... | collective-permute-start | bytes 2359304 | tf_op jit(solution)/shard_map/ppermute | solution.py:23
  26.3 5.0 %collective-permute-start.5 = (bf16[4,128,768]{2,1,0:T(8,128)(2,1)}, bf16[4,128,768]{2,1,0:T(8,128)(2,1)S(1)}, u32[]{:S(2)}, u32[]{:S(2)}) collective-permute-start(bf16[4,128,768]{2,1,0:T(8,128)(2,1)} %get-tuple-element.25.refs_3_), channel_id=1, source_target_pairs={{0,8},{8,0},{1,9},{9,1},{2,10},{10,2},{3,11},{11,3},{4,12},{12,4},... | collective-permute-start | bytes 2359304 | tf_op jit(solution)/shard_map/ppermute | solution.py:23
  26.3 5.0 %collective-permute-start.6 = (bf16[4,128,768]{2,1,0:T(8,128)(2,1)}, bf16[4,128,768]{2,1,0:T(8,128)(2,1)S(1)}, u32[]{:S(2)}, u32[]{:S(2)}) collective-permute-start(bf16[4,128,768]{2,1,0:T(8,128)(2,1)} %get-tuple-element.24.refs_1_), channel_id=1, source_target_pairs={{0,8},{8,0},{1,9},{9,1},{2,10},{10,2},{3,11},{11,3},{4,12},{12,4},... | collective-permute-start | bytes 2359304 | tf_op jit(solution)/shard_map/ppermute | solution.py:23
  26.8 12.0 %collective-permute-start.10 = (bf16[4,128,768]{2,1,0:T(8,128)(2,1)}, bf16[4,128,768]{2,1,0:T(8,128)(2,1)}, u32[]{:S(2)}, u32[]{:S(2)}) collective-permute-start(bf16[4,128,768]{2,1,0:T(8,128)(2,1)} %get-tuple-element.24.refs_1_), channel_id=1, source_target_pairs={{0,2},{2,4},{4,6},{6,0},{8,14},{10,8},{12,10},{14,12},{1,3},{3,5},... | collective-permute-start | bytes 2359304 | tf_op jit(solution)/shard_map/ppermute | solution.py:317
  38.8 5.5 %collective-permute-start.11 = (bf16[4,128,768]{2,1,0:T(8,128)(2,1)}, bf16[4,128,768]{2,1,0:T(8,128)(2,1)S(1)}, u32[]{:S(2)}, u32[]{:S(2)}) collective-permute-start(bf16[4,128,768]{2,1,0:T(8,128)(2,1)} %tie.5.refs_1_.refs_5_), channel_id=1, source_target_pairs={{0,8},{8,0},{1,9},{9,1},{2,10},{10,2},{3,11},{11,3},{4,12},{12,4},... | collective-permute-start | bytes 2359304 | tf_op jit(solution)/shard_map/ppermute | solution.py:23
  40.3 12.2 %collective-permute-start.7 = (bf16[2,192,384]{2,1,0:T(8,128)(2,1)}, bf16[2,192,384]{2,1,0:T(8,128)(2,1)S(1)}, u32[]{:S(2)}, u32[]{:S(2)}) collective-permute-start(bf16[2,192,384]{2,1,0:T(8,128)(2,1)} %bitcast.25), channel_id=1, source_target_pairs={{0,16},{16,32},{32,48},{48,0},{1,17},{17,33},{33,49},{49,1},{2,18}... | collective-permute-start | bytes 884744 | tf_op jit(solution)/shard_map/ppermute | solution.py:23
  40.7 16.4 %collective-permute-start.8 = (bf16[2,192,384]{2,1,0:T(8,128)(2,1)}, bf16[2,192,384]{2,1,0:T(8,128)(2,1)S(1)}, u32[]{:S(2)}, u32[]{:S(2)}) collective-permute-start(bf16[2,192,384]{2,1,0:T(8,128)(2,1)} %bitcast.24), channel_id=1, source_target_pairs={{0,32},{16,48},{32,0},{48,16},{1,33},{17,49},{33,1},{49,17},{2,34}... | collective-permute-start | bytes 884744 | tf_op jit(solution)/shard_map/ppermute | solution.py:23
  43.3 13.7 %collective-permute-start.9 = (bf16[2,192,384]{2,1,0:T(8,128)(2,1)S(1)}, bf16[2,192,384]{2,1,0:T(8,128)(2,1)S(1)}, u32[]{:S(2)}, u32[]{:S(2)}) collective-permute-start(bf16[2,192,384]{2,1,0:T(8,128)(2,1)S(1)} %bitcast.23), channel_id=1, source_target_pairs={{0,48},{16,0},{32,16},{48,32},{1,49},{17,1},{33,17},{49,33},{2,50}... | collective-permute-start | bytes 884744 | tf_op jit(solution)/shard_map/ppermute | solution.py:23
  51.2 8.4 %collective-permute-start.12 = (bf16[2,192,128]{2,1,0:T(8,128)(2,1)S(1)}, bf16[2,192,128]{2,1,0:T(8,128)(2,1)S(1)}, u32[]{:S(2)}, u32[]{:S(2)}) collective-permute-start(bf16[2,192,128]{2,1,0:T(8,128)(2,1)S(1)} %bitcast.28), channel_id=1, source_target_pairs={{0,16},{16,32},{32,48},{48,0},{1,17},{17,33},{33,49},{49,1},{2,18}... | collective-permute-start | bytes 294920 | tf_op jit(solution)/shard_map/ppermute | solution.py:23
  51.7 9.6 %collective-permute-start.13 = (bf16[2,192,128]{2,1,0:T(8,128)(2,1)S(1)}, bf16[2,192,128]{2,1,0:T(8,128)(2,1)S(1)}, u32[]{:S(2)}, u32[]{:S(2)}) collective-permute-start(bf16[2,192,128]{2,1,0:T(8,128)(2,1)S(1)} %bitcast.27), channel_id=1, source_target_pairs={{0,32},{16,48},{32,0},{48,16},{1,33},{17,49},{33,1},{49,17},{2,34}... | collective-permute-start | bytes 294920 | tf_op jit(solution)/shard_map/ppermute | solution.py:23
  52.5 8.8 %collective-permute-start.14 = (bf16[2,192,128]{2,1,0:T(8,128)(2,1)S(1)}, bf16[2,192,128]{2,1,0:T(8,128)(2,1)S(1)}, u32[]{:S(2)}, u32[]{:S(2)}) collective-permute-start(bf16[2,192,128]{2,1,0:T(8,128)(2,1)S(1)} %bitcast.26), channel_id=1, source_target_pairs={{0,48},{16,0},{32,16},{48,32},{1,49},{17,1},{33,17},{49,33},{2,50}... | collective-permute-start | bytes 294920 | tf_op jit(solution)/shard_map/ppermute | solution.py:23
  62.8 25.3 %collective-permute-start.21 = (bf16[3,128,1024]{2,1,0:T(8,128)(2,1)}, bf16[3,128,1024]{2,1,0:T(8,128)(2,1)}, u32[]{:S(2)}, u32[]{:S(2)}) collective-permute-start(bf16[3,128,1024]{2,1,0:T(8,128)(2,1)} %tie.6.refs_7_), channel_id=1, source_target_pairs={{0,2},{2,4},{4,6},{6,0},{8,14},{10,8},{12,10},{14,12},{1,3},{3,5},... | collective-permute-start | bytes 2359304 | tf_op jit(solution)/shard_map/ppermute | solution.py:317
  63.1 45.5 %copy-start.17 = (bf16[768,768]{1,0:T(8,128)(2,1)S(1)}, bf16[768,768]{1,0:T(8,128)(2,1)}, u32[]{:S(2)}) copy-start(bf16[768,768]{1,0:T(8,128)(2,1)} %refs_3_.8) | copy-start | bytes 3538948
  63.1 23.6 %all-to-all-start = ((bf16[8,48,512]{2,1,0:T(8,128)(2,1)}), bf16[8,48,512]{2,1,0:T(8,128)(2,1)S(1)}, u32[]{:S(2)}, u32[]{:S(2)}) async-start(bf16[8,48,512]{2,1,0:T(8,128)(2,1)} %bitcast.15), calls=%async_computation | async-start | bytes 786432 | tf_op jit(solution)/shard_map/all_to_all | solution.py:359
  71.5 37.1 %copy-start.4 = (bf16[4,128,768]{2,1,0:T(8,128)(2,1)S(1)}, bf16[4,128,768]{2,1,0:T(8,128)(2,1)}, u32[]{:S(2)}) copy-start(bf16[4,128,768]{2,1,0:T(8,128)(2,1)} %get-tuple-element.24.refs_1_) | copy-start | bytes 2359300
  71.5 37.1 %copy-start.7 = (bf16[4,128,768]{2,1,0:T(8,128)(2,1)S(1)}, bf16[4,128,768]{2,1,0:T(8,128)(2,1)}, u32[]{:S(2)}) copy-start(bf16[4,128,768]{2,1,0:T(8,128)(2,1)} %get-tuple-element.25.refs_3_) | copy-start | bytes 2359300
  71.5 37.1 %copy-start.14 = (bf16[4,2,48,512]{3,2,1,0:T(8,128)(2,1)S(1)}, bf16[4,2,48,512]{3,2,1,0:T(8,128)(2,1)}, u32[]{:S(2)}) copy-start(bf16[4,2,48,512]{3,2,1,0:T(8,128)(2,1)} %copy-done.13) | copy-start | bytes 1179652
  71.5 44.9 %collective-permute-start.22 = (bf16[3,128,1024]{2,1,0:T(8,128)(2,1)}, bf16[3,128,1024]{2,1,0:T(8,128)(2,1)}, u32[]{:S(2)}, u32[]{:S(2)}) collective-permute-start(bf16[3,128,1024]{2,1,0:T(8,128)(2,1)} %tie.6.refs_7_), channel_id=1, source_target_pairs={{0,6},{2,0},{4,2},{6,4},{8,10},{10,12},{12,14},{14,8},{1,7},{3,1},... | collective-permute-start | bytes 2359304 | tf_op jit(solution)/shard_map/ppermute | solution.py:317
  88.1 37.7 %collective-permute-start.23 = (bf16[3,128,1024]{2,1,0:T(8,128)(2,1)}, bf16[3,128,1024]{2,1,0:T(8,128)(2,1)S(1)}, u32[]{:S(2)}, u32[]{:S(2)}) collective-permute-start(bf16[3,128,1024]{2,1,0:T(8,128)(2,1)} %tie.7.refs_8_), channel_id=1, source_target_pairs={{0,2},{2,4},{4,6},{6,0},{8,14},{10,8},{12,10},{14,12},{1,3},{3,5},... | collective-permute-start | bytes 2359304 | tf_op jit(solution)/shard_map/ppermute | solution.py:317
  88.1 6.2 %collective-permute-start.15 = (bf16[48,1024]{1,0:T(8,128)(2,1)}, bf16[48,1024]{1,0:T(8,128)(2,1)S(1)}, u32[]{:S(2)}, u32[]{:S(2)}) collective-permute-start(bf16[48,1024]{1,0:T(8,128)(2,1)} %copy-done.34), channel_id=1, source_target_pairs={{0,64},{64,128},{128,192},{192,0},{1,65},{65,129},{129,193},{193,1... | collective-permute-start | bytes 294920 | tf_op jit(solution)/shard_map/ppermute | solution.py:23
  88.1 9.1 %collective-permute-start.16 = (bf16[48,1024]{1,0:T(8,128)(2,1)}, bf16[48,1024]{1,0:T(8,128)(2,1)S(1)}, u32[]{:S(2)}, u32[]{:S(2)}) collective-permute-start(bf16[48,1024]{1,0:T(8,128)(2,1)} %copy-done.34), channel_id=1, source_target_pairs={{0,128},{64,192},{128,0},{192,64},{1,129},{65,193},{129,1},{193,65... | collective-permute-start | bytes 294920 | tf_op jit(solution)/shard_map/ppermute | solution.py:23
  90.0 12.4 %collective-permute-start.17 = (bf16[48,1024]{1,0:T(8,128)(2,1)}, bf16[48,1024]{1,0:T(8,128)(2,1)S(1)}, u32[]{:S(2)}, u32[]{:S(2)}) collective-permute-start(bf16[48,1024]{1,0:T(8,128)(2,1)} %copy-done.34), channel_id=1, source_target_pairs={{0,192},{64,0},{128,64},{192,128},{1,193},{65,1},{129,65},{193,129... | collective-permute-start | bytes 294920 | tf_op jit(solution)/shard_map/ppermute | solution.py:23
  103.8 22.0 %copy-start.12 = (bf16[3,128,1024]{2,1,0:T(8,128)(2,1)S(1)}, bf16[3,128,1024]{2,1,0:T(8,128)(2,1)}, u32[]{:S(2)}) copy-start(bf16[3,128,1024]{2,1,0:T(8,128)(2,1)} %tie.6.refs_7_) | copy-start | bytes 2359300
  103.9 12.7 %collective-permute-start.18 = (bf16[3,64,1024]{2,1,0:T(8,128)(2,1)S(1)}, bf16[3,64,1024]{2,1,0:T(8,128)(2,1)S(1)}, u32[]{:S(2)}, u32[]{:S(2)}) collective-permute-start(bf16[3,64,1024]{2,1,0:T(8,128)(2,1)S(1)} %bitcast.16), channel_id=1, source_target_pairs={{0,16},{16,32},{32,48},{48,0},{1,17},{17,33},{33,49},{49,1},{2,18}... | collective-permute-start | bytes 1179656 | tf_op jit(solution)/shard_map/ppermute | solution.py:23
  103.9 21.9 %collective-permute-start.19 = (bf16[3,64,1024]{2,1,0:T(8,128)(2,1)S(1)}, bf16[3,64,1024]{2,1,0:T(8,128)(2,1)S(1)}, u32[]{:S(2)}, u32[]{:S(2)}) collective-permute-start(bf16[3,64,1024]{2,1,0:T(8,128)(2,1)S(1)} %bitcast.17), channel_id=1, source_target_pairs={{0,32},{16,48},{32,0},{48,16},{1,33},{17,49},{33,1},{49,17},{2,34}... | collective-permute-start | bytes 1179656 | tf_op jit(solution)/shard_map/ppermute | solution.py:23
  108.6 17.2 %collective-permute-start.20 = (bf16[3,64,1024]{2,1,0:T(8,128)(2,1)S(1)}, bf16[3,64,1024]{2,1,0:T(8,128)(2,1)S(1)}, u32[]{:S(2)}, u32[]{:S(2)}) collective-permute-start(bf16[3,64,1024]{2,1,0:T(8,128)(2,1)S(1)} %bitcast.18), channel_id=1, source_target_pairs={{0,48},{16,0},{32,16},{48,32},{1,49},{17,1},{33,17},{49,33},{2,50}... | collective-permute-start | bytes 1179656 | tf_op jit(solution)/shard_map/ppermute | solution.py:23
  112.1 13.7 %copy-start.39 = (bf16[3,128,1024]{2,1,0:T(8,128)(2,1)S(1)}, bf16[3,128,1024]{2,1,0:T(8,128)(2,1)}, u32[]{:S(2)}) copy-start(bf16[3,128,1024]{2,1,0:T(8,128)(2,1)} %copy-done.38) | copy-start | bytes 2359300
  130.0 2.8 %collective-permute-start.24 = (bf16[4,128,384]{2,1,0:T(8,128)(2,1)S(1)}, bf16[4,128,384]{2,1,0:T(8,128)(2,1)S(1)}, u32[]{:S(2)}, u32[]{:S(2)}) collective-permute-start(bf16[4,128,384]{2,1,0:T(8,128)(2,1)S(1)} %get-tuple-element.36), channel_id=1, source_target_pairs={{0,8},{8,0},{1,9},{9,1},{2,10},{10,2},{3,11},{11,3},{4,12},{12,4},... | collective-permute-start | bytes 1179656 | tf_op jit(solution)/shard_map/ppermute | solution.py:23
  (37 other events, 79.4 us)

commit v2 on v1

v2 whole, which is shorter than its diff:
```python
import functools

import jax
import jax.numpy as jnp
from jax import lax
from jax.experimental import pallas as pl
from jax.experimental.pallas import tpu as pltpu
from jax.sharding import Mesh, PartitionSpec as P

HEADS = 12
HEAD = 64
AXES = ("z_hi", "y", "core", "x", "z_lo")
SIZES = (4, 4, 2, 4, 2)
SIZE = dict(zip(AXES, SIZES))
BF16 = jnp.bfloat16
F32 = jnp.float32
PARTS = 4
VMEM = 16 << 20


def shift(arr, axis, step):
    n = SIZE[axis]
    return lax.ppermute(arr, axis, [(i, (i + step) % n) for i in range(n)])


def whole(shape):
    return pl.BlockSpec(shape, lambda *_: (0,) * len(shape), pipeline_mode=pl.Buffered(1))


def call(body, place, ins, in_specs, outs, out_specs, grid, flops, name, late=()):
    moved = sum(a.size * a.dtype.itemsize for a in ins)
    moved += sum(o.size * o.dtype.itemsize for o in outs)
    n = 1 + len(ins)

    def run(*refs):
        body(*refs[:n], *refs[n + len(late) :])

    in_specs = [*in_specs] + [pl.BlockSpec(memory_space=pl.ANY)] * len(late)
    return pl.pallas_call(
        run,
        out_shape=outs,
        grid_spec=pltpu.PrefetchScalarGridSpec(
            num_scalar_prefetch=1, grid=grid, in_specs=in_specs, out_specs=out_specs
        ),
        compiler_params=pltpu.CompilerParams(vmem_limit_bytes=VMEM),
        cost_estimate=pl.CostEstimate(flops=flops, bytes_accessed=moved, transcendentals=0),
        name=name,
    )(place, *ins, *late)


def tie(arrays, late):
    n = len(arrays)
    free = pl.BlockSpec(memory_space=pl.ANY)
    return pl.pallas_call(
        lambda *refs: None,
        out_shape=[jax.ShapeDtypeStruct(a.shape, a.dtype) for a in arrays],
        in_specs=[free] * (n + 1),
        out_specs=[free] * n,
        input_output_aliases={i: i for i in range(n)},
        compiler_params=pltpu.CompilerParams(vmem_limit_bytes=1 << 20),
        name="tie",
    )(*arrays, late)


def rel(index):
    return lax.rem(index + PARTS, PARTS)


def manual(body, place, ins, outs, scratch, flops, name, late=()):
    moved = sum(a.size * a.dtype.itemsize for a in ins)
    moved += sum(o.size * o.dtype.itemsize for o in outs)
    n = 1 + len(ins)
    far_off = pl.BlockSpec(memory_space=pltpu.HBM)

    def run(*refs):
        body(*refs[:n], *refs[n + len(late) :])

    return pl.pallas_call(
        run,
        out_shape=outs,
        in_specs=[pl.BlockSpec(memory_space=pltpu.SMEM)] + [far_off] * (len(ins) + len(late)),
        out_specs=[far_off] * len(outs),
        scratch_shapes=scratch,
        compiler_params=pltpu.CompilerParams(vmem_limit_bytes=VMEM),
        cost_estimate=pl.CostEstimate(flops=flops, bytes_accessed=moved, transcendentals=0),
        name=name,
    )(place, *ins, *late)


def start(src, dst, sem):
    copy = pltpu.make_async_copy(src, dst, sem)
    copy.start()
    return copy


def columns(weight, place):
    own = weight.shape[1] // 2
    return weight.at[:, pl.ds(pl.multiple_of(place[0] * own, own), own)]


def project(x_ref, half, weight, kind, out, place, base=0):
    seqs, rows, width = x_ref.shape
    lanes = 2 * HEAD
    pairs = weight.shape[1] // lanes
    group = rows // PARTS
    x = x_ref[...].reshape(seqs * rows, width)
    got = jnp.dot(x, weight[...], preferred_element_type=F32).astype(BF16)
    for s in range(seqs):
        at = (half * seqs + s) * lanes
        for p in range(pairs):
            part = got[s * rows : (s + 1) * rows, p * lanes : (p + 1) * lanes]
            if kind != "q":
                out[p, base : base + rows, at : at + lanes] = part
                continue
            first = lax.broadcasted_iota(jnp.int32, part.shape, 1) < HEAD
            for h in range(2):
                kept = jnp.where(first == (h == 0), part, jnp.zeros_like(part))
                for a in range(PARTS):
                    out[p, rel(a - place[1]), h, :, at : at + lanes] = kept[
                        a * group : (a + 1) * group
                    ]


def write_logits(queries, keys, held, outs, sems):
    half = held.shape[3]
    copies = []
    for p in range(keys.shape[0]):
        k = keys[p]
        for i, ref in enumerate(queries):
            q = ref[p].reshape(PARTS * half, -1)
            got = lax.dot_general(q, k, (((1,), (1,)), ((), ())), preferred_element_type=F32)
            for d in range(PARTS):
                held[d, i, p] = got[d * half : (d + 1) * half].astype(BF16)
        for d, out in enumerate(outs):
            copies.append(start(held.at[d, :, p], out.at[:, p], sems.at[p, d]))
    return copies


def wait_all(copies):
    for copy in copies:
        copy.wait()


def own_body(place, x0, x1, wq, wk, wv, oq, ok, ov, bx, bw, bq, bk, bv, ins, outs):
    loads = [start(x, bx.at[i], ins.at[i]) for i, x in enumerate((x0, x1))]
    loads += [start(columns(w, place), bw.at[i], ins.at[2 + i]) for i, w in enumerate((wq, wk, wv))]
    stores = []
    for i, (kind, out, held) in enumerate((("q", oq, bq), ("k", ok, bk), ("v", ov, bv))):
        loads[2 + i].wait()
        for half in range(2):
            if i == 0:
                loads[half].wait()
            project(bx.at[half], half, bw.at[i], kind, held, place)
        stores.append(start(held, out, outs.at[i]))
    wait_all(stores)


def near_body(place, q0, k0, *refs):
    xs, (wq, wk, oq), ls = refs[:6], refs[6:9], refs[9:13]
    bx, bw, bq, bk, held, ins, outs, sems = refs[13:]
    rows = k0.shape[1]
    q_in = start(q0, bq.at[0], ins.at[8])
    k_in = start(k0, bk.at[:, pl.ds(0, rows), :], ins.at[9])
    w_in = [start(columns(w, place), bw.at[i], ins.at[6 + i]) for i, w in enumerate((wq, wk))]
    x_in = [start(x, bx.at[i], ins.at[i]) for i, x in enumerate(xs)]
    w_in[0].wait()
    for half in range(2):
        x_in[half].wait()
        project(bx.at[half], half, bw.at[0], "q", bq.at[1], place)
    stored = start(bq.at[1], oq, outs.at[0])
    w_in[1].wait()
    for i in range(2, 6):
        x_in[i].wait()
        project(bx.at[i], i % 2, bw.at[1], "k", bk, place, i // 2 * rows)
    q_in.wait()
    k_in.wait()
    wait_all(write_logits([bq.at[0], bq.at[1]], bk, held, ls, sems))
    stored.wait()


def far_body(place, q0, q1, x0, x1, wk, *refs):
    ls, (bx, bw, bq, bk, held, ins, sems) = refs[:PARTS], refs[PARTS:]
    w_in = start(columns(wk, place), bw, ins.at[0])
    x_in = [start(x, bx.at[i], ins.at[1 + i]) for i, x in enumerate((x0, x1))]
    q_in = [start(q, bq.at[i], ins.at[3 + i]) for i, q in enumerate((q0, q1))]
    w_in.wait()
    for half in range(2):
        x_in[half].wait()
        project(bx.at[half], half, bw, "k", bk, place)
    wait_all(q_in)
    wait_all(write_logits([bq.at[0], bq.at[1]], bk, held, ls, sems))


def values_body(blocks, ready, place, *refs):
    n = 2 * blocks
    xs, made, wv, out = refs[:n], refs[n : n + sum(ready)], refs[n + sum(ready)], refs[n + sum(ready) + 1]
    bx, bw, held, ins, outs, moves = refs[n + sum(ready) + 2 :]
    rows = xs[0].shape[1]
    w_in = start(columns(wv, place), bw, ins.at[n])
    x_in = [start(x, bx.at[i], ins.at[i]) for i, x in enumerate(xs)]
    copies, made, block = [], list(made), 0
    for at, there in enumerate(ready):
        if there:
            copies.append(start(made.pop(0), out.at[:, pl.ds(at * rows, rows), :], moves.at[at]))
    w_in.wait()
    for at, there in enumerate(ready):
        if not there:
            for half in range(2):
                x_in[2 * block + half].wait()
                project(bx.at[2 * block + half], half, bw, "v", held.at[block], place)
            copies.append(
                start(held.at[block], out.at[:, pl.ds(at * rows, rows), :], outs.at[block])
            )
            block += 1
    wait_all(copies)


def make_values(place, blocks, made, ready, weight, name, late=()):
    seqs, rows, width = blocks[0][0].shape
    own = width // 2
    pairs, span = HEADS // 4, 2 * seqs * 2 * HEAD
    n = len(blocks)
    dma = pltpu.SemaphoreType.DMA
    return manual(
        functools.partial(values_body, n, ready),
        place,
        [*(a for b in blocks for a in b), *made, weight],
        [jax.ShapeDtypeStruct((pairs, rows * len(ready), span), BF16)],
        [
            pltpu.VMEM((2 * n, seqs, rows, width), BF16),
            pltpu.VMEM((width, own), BF16),
            pltpu.VMEM((n, pairs, rows, span), BF16),
            dma((2 * n + 1,)),
            dma((n,)),
            dma((len(ready),)),
        ],
        n * 4 * seqs * rows * width * own,
        name,
        late,
    )[0]


def add_body(count, place, *refs):
    out, parts = refs[-1], refs[:-1]
    z_lo = place[3]
    sums = []
    for n in range(0, len(parts), count):
        total = parts[n][...].astype(F32)
        for ref in parts[n + 1 : n + count]:
            total += ref[...].astype(F32)
        sums.append(total)
    total = jnp.concatenate(sums, axis=-1).astype(BF16)
    share = out.shape[2]
    for i in range(2):
        for z in range(PARTS):
            out[z, i ^ z_lo] = total[i, z * share : (z + 1) * share]


def add_parts(place, groups):
    parts = [a for g in groups for a in g]
    rows = parts[0].shape[1]
    cols = sum(g[0].shape[2] for g in groups)
    shape = (PARTS, 2, rows // PARTS, cols)
    return call(
        functools.partial(add_body, PARTS),
        place,
        parts,
        [whole(a.shape) for a in parts],
        [jax.ShapeDtypeStruct(shape, BF16)],
        [whole(shape)],
        (1,),
        sum(a.size for a in parts),
        "add_over_y",
    )[0]


def softmax_body(scale, place, parts, other, out, same):
    z_lo = place[3]
    sides = []
    for side in (z_lo, 1 - z_lo):
        total = parts[0, side].astype(F32)
        for z in range(1, PARTS):
            total += parts[z, side].astype(F32)
        sides.append(total)
    scaled = jnp.concatenate(sides, axis=-1) * scale
    expo = jnp.exp(scaled - jnp.max(scaled, axis=-1, keepdims=True))
    out[...] = (expo / jnp.sum(expo, axis=-1, keepdims=True)).astype(BF16)


def softmax(place, parts, scale, other):
    shape = (parts.shape[2], 2 * parts.shape[3])
    free = pl.BlockSpec(memory_space=pl.ANY)
    return pl.pallas_call(
        functools.partial(softmax_body, scale),
        out_shape=[
            jax.ShapeDtypeStruct(shape, BF16),
            jax.ShapeDtypeStruct(other.shape, other.dtype),
        ],
        in_specs=[pl.BlockSpec(memory_space=pltpu.SMEM), pl.BlockSpec(memory_space=pltpu.VMEM), free],
        out_specs=[pl.BlockSpec(memory_space=pltpu.VMEM), free],
        input_output_aliases={2: 1},
        compiler_params=pltpu.CompilerParams(vmem_limit_bytes=VMEM),
        cost_estimate=pl.CostEstimate(
            flops=parts.size * 8, bytes_accessed=parts.size * 4, transcendentals=parts.size // 4
        ),
        name="softmax",
    )(place, parts, other)


def order_body(place, *refs):
    out, parts = refs[-1], refs[:-1]
    for d, ref in enumerate(parts):
        out[rel(place[2] - d)] = ref[...]


def order(place, parts):
    shape = (PARTS, *parts[0].shape)
    return call(
        order_body,
        place,
        parts,
        [whole(a.shape) for a in parts],
        [jax.ShapeDtypeStruct(shape, BF16)],
        [whole(shape)],
        (1,),
        0,
        "order",
    )[0]


def mix_body(place, *refs):
    probs, values, outs = refs[:PARTS], refs[PARTS], refs[-2:]
    y = place[1]
    group = probs[0].shape[1] // 2
    lanes = 2 * HEAD
    seqs = outs[0].shape[0]
    p = jnp.concatenate([ref[0] for ref in probs], axis=0)
    got = jnp.dot(p, values[0], preferred_element_type=F32)
    first = lax.broadcasted_iota(jnp.int32, (group, lanes), 1) < HEAD
    for d in range(PARTS):
        at = pl.multiple_of(rel(y - d) * group, group)
        for s in range(2 * seqs):
            one, two = (
                got[(2 * d + h) * group : (2 * d + h + 1) * group, s * lanes : (s + 1) * lanes]
                for h in range(2)
            )
            outs[s // seqs][s % seqs, pl.ds(at, group), :] = jnp.where(first, one, two).astype(BF16)


def mix(place, probs, values, seqs):
    pairs, half, cols = probs[0].shape
    span = values.shape[2]
    rows = PARTS * half // 2
    lanes = 2 * HEAD
    shape = jax.ShapeDtypeStruct((seqs, rows, pairs * lanes), BF16)
    return call(
        mix_body,
        place,
        [*probs, values],
        [pl.BlockSpec((1, half, cols), lambda p, s: (p, 0, 0))] * PARTS
        + [pl.BlockSpec((1, cols, span), lambda p, s: (p, 0, 0))],
        [shape] * 2,
        [pl.BlockSpec((seqs, rows, lanes), lambda p, s: (0, 0, p))] * 2,
        (pairs,),
        2 * pairs * PARTS * half * cols * span,
        "mix",
    )


def finish_body(mine, theirs, weight_mine, weight_theirs, out):
    seqs, rows, own = mine.shape
    got = jnp.dot(mine[...].reshape(seqs * rows, own), weight_mine[...], preferred_element_type=F32)
    got += jnp.dot(
        theirs[...].reshape(seqs * rows, own), weight_theirs[...], preferred_element_type=F32
    )
    out[...] = got.astype(BF16).reshape(out.shape)


def finish(mine, theirs, weight_mine, weight_theirs):
    seqs, rows, own = mine.shape
    width = weight_mine.shape[1]
    part = seqs // 2
    return pl.pallas_call(
        finish_body,
        out_shape=jax.ShapeDtypeStruct((seqs, rows, width), BF16),
        grid=(seqs // part,),
        in_specs=[pl.BlockSpec((part, rows, own), lambda r: (r, 0, 0))] * 2
        + [pl.BlockSpec((own, width), lambda r: (0, 0))] * 2,
        out_specs=pl.BlockSpec((part, rows, width), lambda r: (r, 0, 0)),
        compiler_params=pltpu.CompilerParams(vmem_limit_bytes=VMEM),
        cost_estimate=pl.CostEstimate(
            flops=2 * seqs * rows * width * width,
            bytes_accessed=4 * seqs * rows * width + 2 * width * width,
            transcendentals=0,
        ),
        name="finish",
    )(mine, theirs, weight_mine, weight_theirs)


def ring_table(axis_of):
    return [
        (c * SIZE["x"] + i, c * SIZE["x"] + (i + (1 if c == axis_of else -1)) % SIZE["x"])
        for c in range(2)
        for i in range(SIZE["x"])
    ]


def send_x(arr, way):
    return lax.ppermute(arr, ("core", "x"), ring_table(way))


def per_device(data, query_matrix, key_matrix, value_matrix, output_matrix):
    seqs, rows, width = data.shape
    place = jnp.stack([lax.axis_index(a) for a in ("core", "y", "z_hi", "z_lo")])
    place = place.astype(jnp.int32)

    core = lax.axis_index("core")
    half = width // 2

    def swap(arr):
        return shift(arr, "core", 1)

    output_mine, output_theirs = (
        lax.dynamic_slice_in_dim(output_matrix, c * half, half, 0) for c in (core, 1 - core)
    )

    pairs, span, group = HEADS // 4, 4 * seqs * HEAD, rows // PARTS
    q_shape, k_shape = (pairs, PARTS, 2, group, span), (pairs, rows, span)
    dma = pltpu.SemaphoreType.DMA

    def logits_shape(n):
        return jax.ShapeDtypeStruct((2, pairs, 2 * group, n * rows), BF16)

    def bf(*shape):
        return pltpu.VMEM(shape, BF16)

    first, second = send_x(data, 0), send_x(data, 1)
    partner = shift(data, "z_lo", 1)
    queries, keys, values = manual(
        own_body,
        place,
        [data, swap(data), query_matrix, key_matrix, value_matrix],
        [jax.ShapeDtypeStruct(s, BF16) for s in (q_shape, k_shape, k_shape)],
        [bf(2, *data.shape), bf(3, width, half), bf(*q_shape), bf(*k_shape), bf(*k_shape)]
        + [dma((5,)), dma((3,))],
        12 * seqs * rows * width * half,
        "own",
    )
    first, second, partner = tie([first, second, partner], queries)
    far = send_x(first, 0)
    near = [(first, swap(second)), (second, swap(first))]
    partner2 = (partner, swap(partner))
    partner_queries, *near_logits = manual(
        near_body,
        place,
        [queries, keys, *partner2, *near[0], *near[1], query_matrix, key_matrix],
        [jax.ShapeDtypeStruct(q_shape, BF16)] + [logits_shape(3)] * PARTS,
        [bf(6, *data.shape), bf(2, width, half), bf(2, *q_shape), bf(pairs, 3 * rows, span)]
        + [bf(PARTS, 2, pairs, 2 * group, 3 * rows), dma((10,)), dma((1,)), dma((pairs, PARTS))],
        12 * seqs * rows * width * half,
        "near",
    )
    (far,) = tie([far], partner_queries)
    far2 = (far, swap(far))
    far_logits = manual(
        far_body,
        place,
        [queries, partner_queries, *far2, key_matrix],
        [logits_shape(1)] * PARTS,
        [bf(2, *data.shape), bf(width, half), bf(2, *q_shape), bf(*k_shape)]
        + [bf(PARTS, 2, pairs, 2 * group, rows), dma((5,)), dma((pairs, PARTS))],
        4 * seqs * rows * width * half,
        "far",
    )

    def over_y(parts):
        parts = [a.reshape(2, -1, a.shape[-1]) for a in parts]
        return [parts[0]] + [shift(parts[d], "y", d) for d in range(1, PARTS)]

    groups = [over_y(near_logits), over_y(far_logits)]
    z_own = make_values(
        place, [partner2], [], [False], value_matrix, "values_partner", far_logits[:1]
    )
    z_first, z_second = send_x(z_own, 0), send_x(z_own, 1)
    sent = add_parts(place, groups)

    sent = sent.reshape(2 * PARTS, *sent.shape[2:])
    got = lax.all_to_all(sent, ("z_hi", "z_lo"), 0, 0, tiled=True)
    got = got.reshape(PARTS, 2, *got.shape[1:])
    all_rows = seqs * lax.axis_size(("z_hi", "y", "core"))
    probs, z_first = softmax(place, got, HEAD ** (-0.5) * all_rows ** (-0.5), z_first)
    z_far = send_x(z_first, 0)
    probs = order(place, [probs] + [shift(probs, "z_hi", d) for d in range(1, PARTS)])
    probs = probs.reshape(pairs, 2 * group, probs.shape[-1])
    values = make_values(
        place,
        [*near, far2],
        [values, z_own, z_first, z_second, z_far],
        [True, False, False, False, True, True, True, True],
        value_matrix,
        "values",
    )
    probs = [probs] + [shift(probs, "y", d) for d in range(1, PARTS)]
    mine, theirs = mix(place, probs, values, seqs)
    return finish(mine, swap(theirs), output_mine, output_theirs)


def solution(mesh):
    fine = Mesh(mesh.devices.reshape(SIZES), AXES)
    spec = P(("z_hi", "y", "core"), ("x", "z_lo"), None)
    return jax.shard_map(
        per_device,
        mesh=fine,
        in_specs=(spec, P(), P(), P(), P()),
        out_specs=spec,
        check_vma=False,
    )
```

time: 136 us -> 129 us (0.949)
  local copies, waits for them, and re-layouts: 21.4 us -> 8.45 us
  waiting for transfers between devices: 47.7 us -> 50.1 us
  Pallas kernels: 30.1 us -> 32.4 us
    pallas_call x0 -> x7, Pallas kernels: none -> 27.5 us  [the longest x5 24.3 us: manual(): pl.pallas_call(run, out_shape=outs, in_specs=[pl.BlockSpec(memory_space=p...]
    pallas_call x13 -> x3, Pallas kernels: 30.1 us -> 4.92 us  [call(): pl.pallas_call(run, out_shape=outs, grid_spec=pltpu.PrefetchScalarGridSpe...]
    unnamed x86 -> x32, local copies, waits for them, and re-layouts: 21.4 us -> 8.37 us
    ppermute x6, waiting for transfers between devices: 7.29 us -> 9.29 us  [send_x(): return lax.ppermute(arr, ('core', 'x'), ring_table(way))]
  transfers between devices with their start and end apart: 26 -> 26, of which waited for: 13 -> 14; matrix products, arithmetic and copies ran while one was open for 0% -> 0% of each run, Pallas kernels for 16% -> 22%
where the time goes in v2:
time: 129 us; the launch traced here: 128 us
  waiting for transfers between devices  50.1 us (39%)
  starting transfers between devices  36.9 us (29%)
  Pallas kernels  32.4 us (25%)
  local copies, waits for them, and re-layouts  8.45 us (7%)
    ppermute x19, waiting for transfers between devices, shift(): return lax.ppermute(arr, axis, [(i, (i + step) % n) for i in range(n)])  27.2 us
    ppermute x19, starting transfers between devices, shift(): return lax.ppermute(arr, axis, [(i, (i + step) % n) for i in range(n)])  24.4 us
    pallas_call x5, Pallas kernels, manual(): pl.pallas_call(run, out_shape=outs, in_specs=[pl.BlockSpec(memory_space=p...  24.3 us
    all_to_all x1, waiting for transfers between devices, per_device(): got = lax.all_to_all(sent, ('z_hi', 'z_lo'), 0, 0, tiled=True)  13.6 us
    ppermute x6, waiting for transfers between devices, send_x(): return lax.ppermute(arr, ('core', 'x'), ring_table(way))  9.29 us
    unnamed x32, local copies, waits for them, and re-layouts  8.37 us
    all_to_all x1, starting transfers between devices, per_device(): got = lax.all_to_all(sent, ('z_hi', 'z_lo'), 0, 0, tiled=True)  7.95 us
    pallas_call x3, Pallas kernels, call(): pl.pallas_call(run, out_shape=outs, grid_spec=pltpu.PrefetchScalarGridSpe...  4.92 us
  transfers between devices with their start and end apart: 26, of which 14 were waited for; matrix products, arithmetic and copies ran while one was open for 0% of the time, Pallas kernels for 22%

profile of v2, /device:TPU:1, one launch (start us, length us, event | category | flops | bytes accessed | tf_op | source)
XLA Modules:
  0.0 128.1 jit_solution(9559733188939986005)
XLA Ops:
  0.0 3.2 %collective-permute-start = (bf16[4,128,768]{2,1,0:T(8,128)(2,1)}, bf16[4,128,768]{2,1,0:T(8,128)(2,1)S(1)}, u32[]{:S(2)}, u32[]{:S(2)}) collective-permute-start(bf16[4,128,768]{2,1,0:T(8,128)(2,1)} %refs_1_.1), channel_id=1, source_target_pairs={{0,8},{8,0},{1,9},{9,1},{2,10},{10,2},{3,11},{11,3},{4,12},{12,4},... | collective-permute-start | bytes 2359304 | tf_op jit(solution)/shard_map/ppermute | solution.py:23
  5.7 1.3 copy-done
  7.0 1.3 copy-done.1
  8.3 1.3 copy-done.10
  10.7 4.5 %own.1 = (bf16[3,4,2,32,1024]{4,3,2,1,0:T(8,128)(2,1)S(1)}, bf16[3,128,1024]{2,1,0:T(8,128)(2,1)S(1)}, bf16[3,128,1024]{2,1,0:T(8,128)(2,1)S(1)}) custom-call(s32[4]{0:T(128)S(1)} %pad_add_fusion.refs_0_.place, bf16[4,128,768]{2,1,0:T(8,128)(2,1)S(1)} %copy-done.14, bf16[4,128,768]{2,1,0:T(8,128)(2,1)S(1)} %collective-permute-done.refs_2_, ...), custom_call_target="tpu_custom_call" | custom-call | flops 1811939328 | bytes 8257536 | tf_op jit(solution)/shard_map/own/pallas_call | solution.py:78
  15.1 7.5 %collective-permute-done.1.refs_0_ = bf16[4,128,768]{2,1,0:T(8,128)(2,1)S(1)} collective-permute-done((bf16[4,128,768]{2,1,0:T(8,128)(2,1)}, bf16[4,128,768]{2,1,0:T(8,128)(2,1)S(1)}, u32[]{:S(2)}, u32[]{:S(2)}) %collective-permute-start.1) | collective-permute-done | bytes 786464 | tf_op jit(solution)/shard_map/ppermute | solution.py:409
  22.6 1.8 %collective-permute-done.2.refs_1_ = bf16[4,128,768]{2,1,0:T(8,128)(2,1)S(1)} collective-permute-done((bf16[4,128,768]{2,1,0:T(8,128)(2,1)}, bf16[4,128,768]{2,1,0:T(8,128)(2,1)S(1)}, u32[]{:S(2)}, u32[]{:S(2)}) %collective-permute-start.2) | collective-permute-done | bytes 786464 | tf_op jit(solution)/shard_map/ppermute | solution.py:409
  25.4 1.7 %collective-permute-start.10 = (bf16[4,128,768]{2,1,0:T(8,128)(2,1)S(1)}, bf16[4,128,768]{2,1,0:T(8,128)(2,1)S(1)}, u32[]{:S(2)}, u32[]{:S(2)}) collective-permute-start(bf16[4,128,768]{2,1,0:T(8,128)(2,1)S(1)} %get-tuple-element.27.refs_5_.refs_1_), channel_id=1, source_target_pairs={{0,2},{2,4},{4,6},{6,0},{8,14},{10,8},{12,10},{14,12},{1,3},{3,5},... | collective-permute-start | bytes 2359304 | tf_op jit(solution)/shard_map/ppermute | solution.py:409
  29.1 8.1 %near.1 = (bf16[3,4,2,32,1024]{4,3,2,1,0:T(8,128)(2,1)S(1)}, bf16[2,3,64,384]{3,2,1,0:T(8,128)(2,1)S(1)}, bf16[2,3,64,384]{3,2,1,0:T(8,128)(2,1)S(1)}, bf16[2,3,...) custom-call(s32[4]{0:T(128)S(1)} %pad_add_fusion.refs_0_.place, ...), custom_call_target="tpu_custom_call" | custom-call | flops 1811939328 | bytes 12189696 | tf_op jit(solution)/shard_map/near/pallas_call | solution.py:78
  37.3 1.5 %collective-permute-start.11 = (bf16[4,128,768]{2,1,0:T(8,128)(2,1)S(1)}, bf16[4,128,768]{2,1,0:T(8,128)(2,1)S(1)}, u32[]{:S(2)}, u32[]{:S(2)}) collective-permute-start(bf16[4,128,768]{2,1,0:T(8,128)(2,1)S(1)} %tie.3.refs_3_.refs_5_), channel_id=1, source_target_pairs={{0,8},{8,0},{1,9},{9,1},{2,10},{10,2},{3,11},{11,3},{4,12},{12,4},... | collective-permute-start | bytes 2359304 | tf_op jit(solution)/shard_map/ppermute | solution.py:23
  39.5 2.6 %collective-permute-start.8 = (bf16[2,192,384]{2,1,0:T(8,128)(2,1)S(1)}, bf16[2,192,384]{2,1,0:T(8,128)(2,1)S(1)}, u32[]{:S(2)}, u32[]{:S(2)}) collective-permute-start(bf16[2,192,384]{2,1,0:T(8,128)(2,1)S(1)} %bitcast.22), channel_id=1, source_target_pairs={{0,32},{16,48},{32,0},{48,16},{1,33},{17,49},{33,1},{49,17},{2,34}... | collective-permute-start | bytes 884744 | tf_op jit(solution)/shard_map/ppermute | solution.py:23
  43.2 3.8 %far.1 = (bf16[2,3,64,128]{3,2,1,0:T(8,128)(2,1)S(1)}, bf16[2,3,64,128]{3,2,1,0:T(8,128)(2,1)S(1)}, bf16[2,3,64,128]{3,2,1,0:T(8,128)(2,1)S(1)}, bf16[2,3,64,128]{3,2,1,0:T(8,128)(2,1)S(1)}) custom-call(s32[4]{0:T(128)S(1)} %pad_add_fusion.refs_0_.place, bf16[3,4,2,32,1024]{4,3,2,1,0:T(8,128)(2,1)S(1)} %get-tuple-element.24.refs_3_.refs_1_, ...), custom_call_target="tpu_custom_call" | custom-call | flops 603979776 | bytes 6291456 | tf_op jit(solution)/shard_map/far/pallas_call | solution.py:78
  48.6 1.4 %collective-permute-start.14 = (bf16[2,192,128]{2,1,0:T(8,128)(2,1)S(1)}, bf16[2,192,128]{2,1,0:T(8,128)(2,1)S(1)}, u32[]{:S(2)}, u32[]{:S(2)}) collective-permute-start(bf16[2,192,128]{2,1,0:T(8,128)(2,1)S(1)} %bitcast.24), channel_id=1, source_target_pairs={{0,48},{16,0},{32,16},{48,32},{1,49},{17,1},{33,17},{49,33},{2,50}... | collective-permute-start | bytes 294920 | tf_op jit(solution)/shard_map/ppermute | solution.py:23
  50.0 2.8 %values_partner.1.refs_8_ = bf16[3,128,1024]{2,1,0:T(8,128)(2,1)} custom-call(s32[4]{0:T(128)S(1)} %pad_add_fusion.refs_0_.place, bf16[4,128,768]{2,1,0:T(8,128)(2,1)S(1)} %get-tuple-element.26.refs_3_.refs_1_, bf16[4,128,768]{2,1,0:T(8,128)(2,1)S(1)} %collective-permute-done.4.refs_4_.refs_2_, bf16[768,768]{1,0:T(8,128)(2,1)S(1)} %copy-done.2, ...), custom_call_target="tpu_custom_call" | custom-call | flops 603979776 | bytes 3538944 | tf_op jit(solution)/shard_map/values_partner/pallas_call | solution.py:78
  52.8 2.9 %collective-permute-done.8.refs_3_ = bf16[2,192,384]{2,1,0:T(8,128)(2,1)S(1)} collective-permute-done((bf16[2,192,384]{2,1,0:T(8,128)(2,1)S(1)}, bf16[2,192,384]{2,1,0:T(8,128)(2,1)S(1)}, u32[]{:S(2)}, u32[]{:S(2)}) %collective-permute-start.8) | collective-permute-done | bytes 294944 | tf_op jit(solution)/shard_map/ppermute | solution.py:23
  56.3 2.0 %collective-permute-done.12.refs_6_ = bf16[2,192,128]{2,1,0:T(8,128)(2,1)S(1)} collective-permute-done((bf16[2,192,128]{2,1,0:T(8,128)(2,1)S(1)}, bf16[2,192,128]{2,1,0:T(8,128)(2,1)S(1)}, u32[]{:S(2)}, u32[]{:S(2)}) %collective-permute-start.12) | collective-permute-done | bytes 98336 | tf_op jit(solution)/shard_map/ppermute | solution.py:23
  58.3 1.6 %collective-permute-done.13.refs_7_ = bf16[2,192,128]{2,1,0:T(8,128)(2,1)S(1)} collective-permute-done((bf16[2,192,128]{2,1,0:T(8,128)(2,1)S(1)}, bf16[2,192,128]{2,1,0:T(8,128)(2,1)S(1)}, u32[]{:S(2)}, u32[]{:S(2)}) %collective-permute-start.13) | collective-permute-done | bytes 98336 | tf_op jit(solution)/shard_map/ppermute | solution.py:23
  59.9 1.5 %add_over_y.1 = bf16[4,2,48,512]{3,2,1,0:T(8,128)(2,1)} custom-call(s32[4]{0:T(128)S(1)} %pad_add_fusion.refs_0_.place, bf16[2,192,384]{2,1,0:T(8,128)(2,1)S(1)} %bitcast.20, bf16[2,192,384]{2,1,0:T(8,128)(2,1)S(1)} %collective-permute-done.7.refs_2_, bf16[2,192,384]{2,1,0:T(8,128)(2,1)S(1)} %collective-permute-done.8.refs_3_, ...), custom_call_target="tpu_custom_call" | custom-call | flops 786432 | bytes 1966080 | tf_op jit(solution)/shard_map/add_over_y/pallas_call | solution.py:39
  61.4 7.9 %all-to-all-start = ((bf16[8,48,512]{2,1,0:T(8,128)(2,1)}), bf16[8,48,512]{2,1,0:T(8,128)(2,1)}, u32[]{:S(2)}, u32[]{:S(2)}) async-start(bf16[8,48,512]{2,1,0:T(8,128)(2,1)} %bitcast.12), calls=%async_computation | async-start | bytes 786432 | tf_op jit(solution)/shard_map/all_to_all | solution.py:488
  69.4 13.6 %all-to-all-done = bf16[8,48,512]{2,1,0:T(8,128)(2,1)} async-done(((bf16[8,48,512]{2,1,0:T(8,128)(2,1)}), bf16[8,48,512]{2,1,0:T(8,128)(2,1)}, u32[]{:S(2)}, u32[]{:S(2)}) %all-to-all-start) | async-done | bytes 393248 | tf_op jit(solution)/shard_map/all_to_all | solution.py:488
  83.0 1.3 %softmax.1 = (bf16[48,1024]{1,0:T(8,128)(2,1)S(1)}, bf16[3,128,1024]{2,1,0:T(8,128)(2,1)}) custom-call(s32[4]{0:T(128)S(1)} %pad_add_fusion.refs_0_.place, bf16[4,2,48,512]{3,2,1,0:T(8,128)(2,1)} %bitcast.13.parts, bf16[3,128,1024]{2,1,0:T(8,128)(2,1)} %collective-permute-done.15.other), custom_call_target="tpu_custom_call", output_to_operand_aliasing={{1}: (2, {})} | custom-call | flops 1572864 | bytes 786432 | tf_op jit(solution)/shard_map/softmax/pallas_call | solution.py:293
  85.0 3.2 %collective-permute-start.17 = (bf16[48,1024]{1,0:T(8,128)(2,1)S(1)}, bf16[48,1024]{1,0:T(8,128)(2,1)S(1)}, u32[]{:S(2)}, u32[]{:S(2)}) collective-permute-start(bf16[48,1024]{1,0:T(8,128)(2,1)S(1)} %get-tuple-element.38.refs_1_), channel_id=1, source_target_pairs={{0,128},{64,192},{128,0},{192,64},{1,129},{65,193},{129,1},{193,65... | collective-permute-start | bytes 294920 | tf_op jit(solution)/shard_map/ppermute | solution.py:23
  89.2 1.4 %collective-permute-done.16.refs_2_ = bf16[48,1024]{1,0:T(8,128)(2,1)S(1)} collective-permute-done((bf16[48,1024]{1,0:T(8,128)(2,1)S(1)}, bf16[48,1024]{1,0:T(8,128)(2,1)S(1)}, u32[]{:S(2)}, u32[]{:S(2)}) %collective-permute-start.16) | collective-permute-done | bytes 98336 | tf_op jit(solution)/shard_map/ppermute | solution.py:23
  90.6 3.1 %collective-permute-done.17.refs_3_ = bf16[48,1024]{1,0:T(8,128)(2,1)S(1)} collective-permute-done((bf16[48,1024]{1,0:T(8,128)(2,1)S(1)}, bf16[48,1024]{1,0:T(8,128)(2,1)S(1)}, u32[]{:S(2)}, u32[]{:S(2)}) %collective-permute-start.17) | collective-permute-done | bytes 98336 | tf_op jit(solution)/shard_map/ppermute | solution.py:23
  93.6 4.1 %collective-permute-done.18.refs_4_ = bf16[48,1024]{1,0:T(8,128)(2,1)S(1)} collective-permute-done((bf16[48,1024]{1,0:T(8,128)(2,1)S(1)}, bf16[48,1024]{1,0:T(8,128)(2,1)S(1)}, u32[]{:S(2)}, u32[]{:S(2)}) %collective-permute-start.18) | collective-permute-done | bytes 98336 | tf_op jit(solution)/shard_map/ppermute | solution.py:23
  98.4 5.0 %collective-permute-start.20 = (bf16[3,64,1024]{2,1,0:T(8,128)(2,1)S(1)}, bf16[3,64,1024]{2,1,0:T(8,128)(2,1)S(1)}, u32[]{:S(2)}, u32[]{:S(2)}) collective-permute-start(bf16[3,64,1024]{2,1,0:T(8,128)(2,1)S(1)} %bitcast.16), channel_id=1, source_target_pairs={{0,32},{16,48},{32,0},{48,16},{1,33},{17,49},{33,1},{49,17},{2,34}... | collective-permute-start | bytes 1179656 | tf_op jit(solution)/shard_map/ppermute | solution.py:23
  106.9 5.2 %values.1.refs_5_ = bf16[3,1024,1024]{2,1,0:T(8,128)(2,1)S(1)} custom-call(s32[4]{0:T(128)S(1)} %pad_add_fusion.refs_0_.place, bf16[4,128,768]{2,1,0:T(8,128)(2,1)S(1)} %get-tuple-element.27.refs_5_.refs_1_, bf16[4,128,768]{2,1,0:T(8,128)(2,1)S(1)} %copy-done.7, bf16[4,128,768]{2,1,0:T(8,128)(2,1)S(1)} %get-tuple-element.28.refs_7_.refs_3_, ...), custom_call_target="tpu_custom_call" | custom-call | flops 1811939328 | bytes 16121856 | tf_op jit(solution)/shard_map/values/pallas_call | solution.py:78
  112.1 8.6 %collective-permute-done.20.refs_3_ = bf16[3,64,1024]{2,1,0:T(8,128)(2,1)S(1)} collective-permute-done((bf16[3,64,1024]{2,1,0:T(8,128)(2,1)S(1)}, bf16[3,64,1024]{2,1,0:T(8,128)(2,1)S(1)}, u32[]{:S(2)}, u32[]{:S(2)}) %collective-permute-start.20) | collective-permute-done | bytes 393248 | tf_op jit(solution)/shard_map/ppermute | solution.py:23
  120.7 2.9 %mix.1 = (bf16[4,128,384]{2,1,0:T(8,128)(2,1)S(1)}, bf16[4,128,384]{2,1,0:T(8,128)(2,1)S(1)}) custom-call(s32[4]{0:T(128)S(1)} %pad_add_fusion.refs_0_.place, bf16[3,64,1024]{2,1,0:T(8,128)(2,1)S(1)} %bitcast.18, bf16[3,64,1024]{2,1,0:T(8,128)(2,1)S(1)} %collective-permute-done.19.refs_2_, bf16[3,64,1024]{2,1,0:T(8,128)(2,1)S(1)} %collective-permute-done.20.refs_3_, ...), custom_call_target="tpu_custom_call" | custom-call | flops 1610612736 | bytes 8650752 | tf_op jit(solution)/shard_map/mix/pallas_call | solution.py:39
  123.6 1.3 %collective-permute-start.24 = (bf16[4,128,384]{2,1,0:T(8,128)(2,1)S(1)}, bf16[4,128,384]{2,1,0:T(8,128)(2,1)S(1)}, u32[]{:S(2)}, u32[]{:S(2)}) collective-permute-start(bf16[4,128,384]{2,1,0:T(8,128)(2,1)S(1)} %get-tuple-element.42), channel_id=1, source_target_pairs={{0,8},{8,0},{1,9},{9,1},{2,10},{10,2},{3,11},{11,3},{4,12},{12,4},... | collective-permute-start | bytes 1179656 | tf_op jit(solution)/shard_map/ppermute | solution.py:23
  125.0 1.3 collective-permute-done.24.theirs
  126.2 1.9 %finish.1 = bf16[4,128,768]{2,1,0:T(8,128)(2,1)} custom-call(bf16[4,128,384]{2,1,0:T(8,128)(2,1)S(1)} %get-tuple-element.41.mine, bf16[4,128,384]{2,1,0:T(8,128)(2,1)S(1)} %collective-permute-done.24.theirs, bf16[384,768]{1,0:T(8,128)(2,1)S(1)} %get-tuple-element.44.weight_mine, bf16[384,768]{1,0:T(8,128)(2,1)S(1)} %get-tuple-element.43.weight_theirs), custom_call_target="tpu_custom_call" | custom-call | flops 603979776 | bytes 2752512 | tf_op jit(solution)/shard_map/finish/pallas_call | solution.py:383
  (66 shorter events, 16.5 us)
Async XLA Ops:
  0.0 5.7 %collective-permute-start = (bf16[4,128,768]{2,1,0:T(8,128)(2,1)}, bf16[4,128,768]{2,1,0:T(8,128)(2,1)S(1)}, u32[]{:S(2)}, u32[]{:S(2)}) collective-permute-start(bf16[4,128,768]{2,1,0:T(8,128)(2,1)} %refs_1_.1), channel_id=1, source_target_pairs={{0,8},{8,0},{1,9},{9,1},{2,10},{10,2},{3,11},{11,3},{4,12},{12,4},... | collective-permute-start | bytes 2359304 | tf_op jit(solution)/shard_map/ppermute | solution.py:23
  3.2 19.4 %collective-permute-start.1 = (bf16[4,128,768]{2,1,0:T(8,128)(2,1)}, bf16[4,128,768]{2,1,0:T(8,128)(2,1)S(1)}, u32[]{:S(2)}, u32[]{:S(2)}) collective-permute-start(bf16[4,128,768]{2,1,0:T(8,128)(2,1)} %refs_1_.1), channel_id=1, source_target_pairs={{0,2},{2,4},{4,6},{6,0},{8,14},{10,8},{12,10},{14,12},{1,3},{3,5},... | collective-permute-start | bytes 2359304 | tf_op jit(solution)/shard_map/ppermute | solution.py:409
  4.0 20.4 %collective-permute-start.2 = (bf16[4,128,768]{2,1,0:T(8,128)(2,1)}, bf16[4,128,768]{2,1,0:T(8,128)(2,1)S(1)}, u32[]{:S(2)}, u32[]{:S(2)}) collective-permute-start(bf16[4,128,768]{2,1,0:T(8,128)(2,1)} %refs_1_.1), channel_id=1, source_target_pairs={{0,6},{2,0},{4,2},{6,4},{8,10},{10,12},{12,14},{14,8},{1,7},{3,1},... | collective-permute-start | bytes 2359304 | tf_op jit(solution)/shard_map/ppermute | solution.py:409
  4.7 19.7 %collective-permute-start.3 = (bf16[4,128,768]{2,1,0:T(8,128)(2,1)}, bf16[4,128,768]{2,1,0:T(8,128)(2,1)S(1)}, u32[]{:S(2)}, u32[]{:S(2)}) collective-permute-start(bf16[4,128,768]{2,1,0:T(8,128)(2,1)} %refs_1_.1), channel_id=1, source_target_pairs={{0,1},{1,0},{2,3},{3,2},{4,5},{5,4},{6,7},{7,6},{8,9},{9,8},{10,11... | collective-permute-start | bytes 2359304 | tf_op jit(solution)/shard_map/ppermute | solution.py:23
  15.1 9.3 %copy-start.12 = (bf16[3,128,1024]{2,1,0:T(8,128)(2,1)}, bf16[3,128,1024]{2,1,0:T(8,128)(2,1)S(1)}, u32[]{:S(2)}) copy-start(bf16[3,128,1024]{2,1,0:T(8,128)(2,1)S(1)} %get-tuple-element.39.refs_7_) | copy-start | bytes 2359300
  24.4 2.7 %collective-permute-start.6 = (bf16[4,128,768]{2,1,0:T(8,128)(2,1)S(1)}, bf16[4,128,768]{2,1,0:T(8,128)(2,1)S(1)}, u32[]{:S(2)}, u32[]{:S(2)}) collective-permute-start(bf16[4,128,768]{2,1,0:T(8,128)(2,1)S(1)} %get-tuple-element.27.refs_5_.refs_1_), channel_id=1, source_target_pairs={{0,8},{8,0},{1,9},{9,1},{2,10},{10,2},{3,11},{11,3},{4,12},{12,4},... | collective-permute-start | bytes 2359304 | tf_op jit(solution)/shard_map/ppermute | solution.py:23
  24.9 3.0 %collective-permute-start.4 = (bf16[4,128,768]{2,1,0:T(8,128)(2,1)S(1)}, bf16[4,128,768]{2,1,0:T(8,128)(2,1)S(1)}, u32[]{:S(2)}, u32[]{:S(2)}) collective-permute-start(bf16[4,128,768]{2,1,0:T(8,128)(2,1)S(1)} %get-tuple-element.26.refs_3_.refs_1_), channel_id=1, source_target_pairs={{0,8},{8,0},{1,9},{9,1},{2,10},{10,2},{3,11},{11,3},{4,12},{12,4},... | collective-permute-start | bytes 2359304 | tf_op jit(solution)/shard_map/ppermute | solution.py:23
  25.0 4.1 %collective-permute-start.5 = (bf16[4,128,768]{2,1,0:T(8,128)(2,1)S(1)}, bf16[4,128,768]{2,1,0:T(8,128)(2,1)S(1)}, u32[]{:S(2)}, u32[]{:S(2)}) collective-permute-start(bf16[4,128,768]{2,1,0:T(8,128)(2,1)S(1)} %get-tuple-element.28.refs_7_.refs_3_), channel_id=1, source_target_pairs={{0,8},{8,0},{1,9},{9,1},{2,10},{10,2},{3,11},{11,3},{4,12},{12,4},... | collective-permute-start | bytes 2359304 | tf_op jit(solution)/shard_map/ppermute | solution.py:23
  25.4 11.8 %collective-permute-start.10 = (bf16[4,128,768]{2,1,0:T(8,128)(2,1)S(1)}, bf16[4,128,768]{2,1,0:T(8,128)(2,1)S(1)}, u32[]{:S(2)}, u32[]{:S(2)}) collective-permute-start(bf16[4,128,768]{2,1,0:T(8,128)(2,1)S(1)} %get-tuple-element.27.refs_5_.refs_1_), channel_id=1, source_target_pairs={{0,2},{2,4},{4,6},{6,0},{8,14},{10,8},{12,10},{14,12},{1,3},{3,5},... | collective-permute-start | bytes 2359304 | tf_op jit(solution)/shard_map/ppermute | solution.py:409
  27.1 10.1 %copy-start.4 = (bf16[4,128,768]{2,1,0:T(8,128)(2,1)}, bf16[4,128,768]{2,1,0:T(8,128)(2,1)S(1)}, u32[]{:S(2)}) copy-start(bf16[4,128,768]{2,1,0:T(8,128)(2,1)S(1)} %collective-permute-done.6.refs_8_.refs_4_) | copy-start | bytes 2359300
  29.1 8.2 %copy-start.6 = (bf16[4,128,768]{2,1,0:T(8,128)(2,1)}, bf16[4,128,768]{2,1,0:T(8,128)(2,1)S(1)}, u32[]{:S(2)}) copy-start(bf16[4,128,768]{2,1,0:T(8,128)(2,1)S(1)} %collective-permute-done.5.refs_6_.refs_2_) | copy-start | bytes 2359300
  37.3 5.9 %collective-permute-start.11 = (bf16[4,128,768]{2,1,0:T(8,128)(2,1)S(1)}, bf16[4,128,768]{2,1,0:T(8,128)(2,1)S(1)}, u32[]{:S(2)}, u32[]{:S(2)}) collective-permute-start(bf16[4,128,768]{2,1,0:T(8,128)(2,1)S(1)} %tie.3.refs_3_.refs_5_), channel_id=1, source_target_pairs={{0,8},{8,0},{1,9},{9,1},{2,10},{10,2},{3,11},{11,3},{4,12},{12,4},... | collective-permute-start | bytes 2359304 | tf_op jit(solution)/shard_map/ppermute | solution.py:23
  38.7 9.8 %collective-permute-start.7 = (bf16[2,192,384]{2,1,0:T(8,128)(2,1)S(1)}, bf16[2,192,384]{2,1,0:T(8,128)(2,1)S(1)}, u32[]{:S(2)}, u32[]{:S(2)}) collective-permute-start(bf16[2,192,384]{2,1,0:T(8,128)(2,1)S(1)} %bitcast.23), channel_id=1, source_target_pairs={{0,16},{16,32},{32,48},{48,0},{1,17},{17,33},{33,49},{49,1},{2,18}... | collective-permute-start | bytes 884744 | tf_op jit(solution)/shard_map/ppermute | solution.py:23
  39.5 16.2 %collective-permute-start.8 = (bf16[2,192,384]{2,1,0:T(8,128)(2,1)S(1)}, bf16[2,192,384]{2,1,0:T(8,128)(2,1)S(1)}, u32[]{:S(2)}, u32[]{:S(2)}) collective-permute-start(bf16[2,192,384]{2,1,0:T(8,128)(2,1)S(1)} %bitcast.22), channel_id=1, source_target_pairs={{0,32},{16,48},{32,0},{48,16},{1,33},{17,49},{33,1},{49,17},{2,34}... | collective-permute-start | bytes 884744 | tf_op jit(solution)/shard_map/ppermute | solution.py:23
  42.1 14.2 %collective-permute-start.9 = (bf16[2,192,384]{2,1,0:T(8,128)(2,1)S(1)}, bf16[2,192,384]{2,1,0:T(8,128)(2,1)S(1)}, u32[]{:S(2)}, u32[]{:S(2)}) collective-permute-start(bf16[2,192,384]{2,1,0:T(8,128)(2,1)S(1)} %bitcast.21), channel_id=1, source_target_pairs={{0,48},{16,0},{32,16},{48,32},{1,49},{17,1},{33,17},{49,33},{2,50}... | collective-permute-start | bytes 884744 | tf_op jit(solution)/shard_map/ppermute | solution.py:23
  47.0 11.3 %collective-permute-start.12 = (bf16[2,192,128]{2,1,0:T(8,128)(2,1)S(1)}, bf16[2,192,128]{2,1,0:T(8,128)(2,1)S(1)}, u32[]{:S(2)}, u32[]{:S(2)}) collective-permute-start(bf16[2,192,128]{2,1,0:T(8,128)(2,1)S(1)} %bitcast.26), channel_id=1, source_target_pairs={{0,16},{16,32},{32,48},{48,0},{1,17},{17,33},{33,49},{49,1},{2,18}... | collective-permute-start | bytes 294920 | tf_op jit(solution)/shard_map/ppermute | solution.py:23
  47.5 12.4 %collective-permute-start.13 = (bf16[2,192,128]{2,1,0:T(8,128)(2,1)S(1)}, bf16[2,192,128]{2,1,0:T(8,128)(2,1)S(1)}, u32[]{:S(2)}, u32[]{:S(2)}) collective-permute-start(bf16[2,192,128]{2,1,0:T(8,128)(2,1)S(1)} %bitcast.25), channel_id=1, source_target_pairs={{0,32},{16,48},{32,0},{48,16},{1,33},{17,49},{33,1},{49,17},{2,34}... | collective-permute-start | bytes 294920 | tf_op jit(solution)/shard_map/ppermute | solution.py:23
  48.6 11.3 %collective-permute-start.14 = (bf16[2,192,128]{2,1,0:T(8,128)(2,1)S(1)}, bf16[2,192,128]{2,1,0:T(8,128)(2,1)S(1)}, u32[]{:S(2)}, u32[]{:S(2)}) collective-permute-start(bf16[2,192,128]{2,1,0:T(8,128)(2,1)S(1)} %bitcast.24), channel_id=1, source_target_pairs={{0,48},{16,0},{32,16},{48,32},{1,49},{17,1},{33,17},{49,33},{2,50}... | collective-permute-start | bytes 294920 | tf_op jit(solution)/shard_map/ppermute | solution.py:23
  55.7 13.8 %collective-permute-start.15 = (bf16[3,128,1024]{2,1,0:T(8,128)(2,1)}, bf16[3,128,1024]{2,1,0:T(8,128)(2,1)}, u32[]{:S(2)}, u32[]{:S(2)}) collective-permute-start(bf16[3,128,1024]{2,1,0:T(8,128)(2,1)} %values_partner.1.refs_8_), channel_id=1, source_target_pairs={{0,2},{2,4},{4,6},{6,0},{8,14},{10,8},{12,10},{14,12},{1,3},{3,5},... | collective-permute-start | bytes 2359304 | tf_op jit(solution)/shard_map/ppermute | solution.py:409
  61.4 21.6 %all-to-all-start = ((bf16[8,48,512]{2,1,0:T(8,128)(2,1)}), bf16[8,48,512]{2,1,0:T(8,128)(2,1)}, u32[]{:S(2)}, u32[]{:S(2)}) async-start(bf16[8,48,512]{2,1,0:T(8,128)(2,1)} %bitcast.12), calls=%async_computation | async-start | bytes 786432 | tf_op jit(solution)/shard_map/all_to_all | solution.py:488
  69.3 34.1 %copy-start.3 = (bf16[768,768]{1,0:T(8,128)(2,1)S(1)}, bf16[768,768]{1,0:T(8,128)(2,1)}, u32[]{:S(2)}) copy-start(bf16[768,768]{1,0:T(8,128)(2,1)} %refs_12_.1) | copy-start | bytes 3538948
  69.3 34.1 %collective-permute-start.22 = (bf16[3,128,1024]{2,1,0:T(8,128)(2,1)}, bf16[3,128,1024]{2,1,0:T(8,128)(2,1)}, u32[]{:S(2)}, u32[]{:S(2)}) collective-permute-start(bf16[3,128,1024]{2,1,0:T(8,128)(2,1)} %values_partner.1.refs_8_), channel_id=1, source_target_pairs={{0,6},{2,0},{4,2},{6,4},{8,10},{10,12},{12,14},{14,8},{1,7},{3,1},... | collective-permute-start | bytes 2359304 | tf_op jit(solution)/shard_map/ppermute | solution.py:409
  83.0 20.5 %copy-start.5 = (bf16[4,128,768]{2,1,0:T(8,128)(2,1)S(1)}, bf16[4,128,768]{2,1,0:T(8,128)(2,1)}, u32[]{:S(2)}) copy-start(bf16[4,128,768]{2,1,0:T(8,128)(2,1)} %copy-done.4) | copy-start | bytes 2359300
  84.3 19.1 %collective-permute-start.23 = (bf16[3,128,1024]{2,1,0:T(8,128)(2,1)}, bf16[3,128,1024]{2,1,0:T(8,128)(2,1)S(1)}, u32[]{:S(2)}, u32[]{:S(2)}) collective-permute-start(bf16[3,128,1024]{2,1,0:T(8,128)(2,1)} %get-tuple-element.40.refs_9_), channel_id=1, source_target_pairs={{0,2},{2,4},{4,6},{6,0},{8,14},{10,8},{12,10},{14,12},{1,3},{3,5},... | collective-permute-start | bytes 2359304 | tf_op jit(solution)/shard_map/ppermute | solution.py:409
  85.0 5.6 %collective-permute-start.16 = (bf16[48,1024]{1,0:T(8,128)(2,1)S(1)}, bf16[48,1024]{1,0:T(8,128)(2,1)S(1)}, u32[]{:S(2)}, u32[]{:S(2)}) collective-permute-start(bf16[48,1024]{1,0:T(8,128)(2,1)S(1)} %get-tuple-element.38.refs_1_), channel_id=1, source_target_pairs={{0,64},{64,128},{128,192},{192,0},{1,65},{65,129},{129,193},{193,1... | collective-permute-start | bytes 294920 | tf_op jit(solution)/shard_map/ppermute | solution.py:23
  85.0 8.6 %collective-permute-start.17 = (bf16[48,1024]{1,0:T(8,128)(2,1)S(1)}, bf16[48,1024]{1,0:T(8,128)(2,1)S(1)}, u32[]{:S(2)}, u32[]{:S(2)}) collective-permute-start(bf16[48,1024]{1,0:T(8,128)(2,1)S(1)} %get-tuple-element.38.refs_1_), channel_id=1, source_target_pairs={{0,128},{64,192},{128,0},{192,64},{1,129},{65,193},{129,1},{193,65... | collective-permute-start | bytes 294920 | tf_op jit(solution)/shard_map/ppermute | solution.py:23
  88.3 9.5 %collective-permute-start.18 = (bf16[48,1024]{1,0:T(8,128)(2,1)S(1)}, bf16[48,1024]{1,0:T(8,128)(2,1)S(1)}, u32[]{:S(2)}, u32[]{:S(2)}) collective-permute-start(bf16[48,1024]{1,0:T(8,128)(2,1)S(1)} %get-tuple-element.38.refs_1_), channel_id=1, source_target_pairs={{0,192},{64,0},{128,64},{192,128},{1,193},{65,1},{129,65},{193,129... | collective-permute-start | bytes 294920 | tf_op jit(solution)/shard_map/ppermute | solution.py:23
  98.3 13.7 %collective-permute-start.19 = (bf16[3,64,1024]{2,1,0:T(8,128)(2,1)S(1)}, bf16[3,64,1024]{2,1,0:T(8,128)(2,1)S(1)}, u32[]{:S(2)}, u32[]{:S(2)}) collective-permute-start(bf16[3,64,1024]{2,1,0:T(8,128)(2,1)S(1)} %bitcast.15), channel_id=1, source_target_pairs={{0,16},{16,32},{32,48},{48,0},{1,17},{17,33},{33,49},{49,1},{2,18}... | collective-permute-start | bytes 1179656 | tf_op jit(solution)/shard_map/ppermute | solution.py:23
  98.4 22.3 %collective-permute-start.20 = (bf16[3,64,1024]{2,1,0:T(8,128)(2,1)S(1)}, bf16[3,64,1024]{2,1,0:T(8,128)(2,1)S(1)}, u32[]{:S(2)}, u32[]{:S(2)}) collective-permute-start(bf16[3,64,1024]{2,1,0:T(8,128)(2,1)S(1)} %bitcast.16), channel_id=1, source_target_pairs={{0,32},{16,48},{32,0},{48,16},{1,33},{17,49},{33,1},{49,17},{2,34}... | collective-permute-start | bytes 1179656 | tf_op jit(solution)/shard_map/ppermute | solution.py:23
  103.4 17.3 %collective-permute-start.21 = (bf16[3,64,1024]{2,1,0:T(8,128)(2,1)S(1)}, bf16[3,64,1024]{2,1,0:T(8,128)(2,1)S(1)}, u32[]{:S(2)}, u32[]{:S(2)}) collective-permute-start(bf16[3,64,1024]{2,1,0:T(8,128)(2,1)S(1)} %bitcast.17), channel_id=1, source_target_pairs={{0,48},{16,0},{32,16},{48,32},{1,49},{17,1},{33,17},{49,33},{2,50}... | collective-permute-start | bytes 1179656 | tf_op jit(solution)/shard_map/ppermute | solution.py:23
  112.1 12.8 %copy-start.15 = (bf16[768,768]{1,0:T(8,128)(2,1)S(1)}, bf16[768,768]{1,0:T(8,128)(2,1)}, u32[]{:S(2)}) copy-start(bf16[768,768]{1,0:T(8,128)(2,1)} %param.9) | copy-start | bytes 3538948
  123.6 2.7 %collective-permute-start.24 = (bf16[4,128,384]{2,1,0:T(8,128)(2,1)S(1)}, bf16[4,128,384]{2,1,0:T(8,128)(2,1)S(1)}, u32[]{:S(2)}, u32[]{:S(2)}) collective-permute-start(bf16[4,128,384]{2,1,0:T(8,128)(2,1)S(1)} %get-tuple-element.42), channel_id=1, source_target_pairs={{0,8},{8,0},{1,9},{9,1},{2,10},{10,2},{3,11},{11,3},{4,12},{12,4},... | collective-permute-start | bytes 1179656 | tf_op jit(solution)/shard_map/ppermute | solution.py:23
  (10 other events, 24.7 us)

commit v3 on v2

--- a/solution.py
+++ b/solution.py
@@ -78,9 +78,32 @@
     return pl.pallas_call(
         run,
         out_shape=outs,
-        in_specs=[pl.BlockSpec(memory_space=pltpu.SMEM)] + [far_off] * (len(ins) + len(late)),
+        in_specs=[pl.BlockSpec(memory_space=pltpu.SMEM)]
+        + [far_off] * len(ins)
+        + [pl.BlockSpec(memory_space=pl.ANY)] * len(late),
         out_specs=[far_off] * len(outs),
         scratch_shapes=scratch,
+        compiler_params=pltpu.CompilerParams(vmem_limit_bytes=VMEM),
+        cost_estimate=pl.CostEstimate(flops=flops, bytes_accessed=moved, transcendentals=0),
+        name=name,
+    )(place, *ins, *late)
+
+
+def local(body, place, ins, outs, flops, name, late=()):
+    here = pl.BlockSpec(memory_space=pltpu.VMEM)
+    moved = sum(a.size * a.dtype.itemsize for a in ins)
+    moved += sum(o.size * o.dtype.itemsize for o in outs)
+    n = 1 + len(ins)
+
+    def run(*refs):
+        body(*refs[:n], *refs[n + len(late) :])
+
+    return pl.pallas_call(
+        run,
+        out_shape=outs,
+        in_specs=[pl.BlockSpec(memory_space=pltpu.SMEM)] + [here] * len(ins)
+        + [pl.BlockSpec(memory_space=pl.ANY)] * len(late),
+        out_specs=[here] * len(outs),
         compiler_params=pltpu.CompilerParams(vmem_limit_bytes=VMEM),
         cost_estimate=pl.CostEstimate(flops=flops, bytes_accessed=moved, transcendentals=0),
         name=name,
@@ -121,19 +144,15 @@
                     ]
 
 
-def write_logits(queries, keys, held, outs, sems):
-    half = held.shape[3]
-    copies = []
-    for p in range(keys.shape[0]):
-        k = keys[p]
-        for i, ref in enumerate(queries):
-            q = ref[p].reshape(PARTS * half, -1)
+def write_logits(queries, keys, outs):
+    half = outs[0].shape[2]
+    for p in range(outs[0].shape[1]):
+        k = jnp.concatenate([ref[p] for ref in keys], axis=0)
+        for i, refs in enumerate(queries):
+            q = jnp.concatenate([ref[p].reshape(PARTS * half, -1) for ref in refs], axis=-1)
             got = lax.dot_general(q, k, (((1,), (1,)), ((), ())), preferred_element_type=F32)
-            for d in range(PARTS):
-                held[d, i, p] = got[d * half : (d + 1) * half].astype(BF16)
-        for d, out in enumerate(outs):
-            copies.append(start(held.at[d, :, p], out.at[:, p], sems.at[p, d]))
-    return copies
+            for d, out in enumerate(outs):
+                out[i, p] = got[d * half : (d + 1) * half].astype(BF16)
 
 
 def wait_all(copies):
@@ -155,89 +174,41 @@
     wait_all(stores)
 
 
-def near_body(place, q0, k0, *refs):
-    xs, (wq, wk, oq), ls = refs[:6], refs[6:9], refs[9:13]
-    bx, bw, bq, bk, held, ins, outs, sems = refs[13:]
-    rows = k0.shape[1]
-    q_in = start(q0, bq.at[0], ins.at[8])
-    k_in = start(k0, bk.at[:, pl.ds(0, rows), :], ins.at[9])
-    w_in = [start(columns(w, place), bw.at[i], ins.at[6 + i]) for i, w in enumerate((wq, wk))]
-    x_in = [start(x, bx.at[i], ins.at[i]) for i, x in enumerate(xs)]
-    w_in[0].wait()
-    for half in range(2):
-        x_in[half].wait()
-        project(bx.at[half], half, bw.at[0], "q", bq.at[1], place)
-    stored = start(bq.at[1], oq, outs.at[0])
-    w_in[1].wait()
-    for i in range(2, 6):
-        x_in[i].wait()
-        project(bx.at[i], i % 2, bw.at[1], "k", bk, place, i // 2 * rows)
-    q_in.wait()
-    k_in.wait()
-    wait_all(write_logits([bq.at[0], bq.at[1]], bk, held, ls, sems))
-    stored.wait()
-
-
-def far_body(place, q0, q1, x0, x1, wk, *refs):
-    ls, (bx, bw, bq, bk, held, ins, sems) = refs[:PARTS], refs[PARTS:]
-    w_in = start(columns(wk, place), bw, ins.at[0])
-    x_in = [start(x, bx.at[i], ins.at[1 + i]) for i, x in enumerate((x0, x1))]
-    q_in = [start(q, bq.at[i], ins.at[3 + i]) for i, q in enumerate((q0, q1))]
-    w_in.wait()
-    for half in range(2):
-        x_in[half].wait()
-        project(bx.at[half], half, bw, "k", bk, place)
-    wait_all(q_in)
-    wait_all(write_logits([bq.at[0], bq.at[1]], bk, held, ls, sems))
-
-
-def values_body(blocks, ready, place, *refs):
-    n = 2 * blocks
-    xs, made, wv, out = refs[:n], refs[n : n + sum(ready)], refs[n + sum(ready)], refs[n + sum(ready) + 1]
-    bx, bw, held, ins, outs, moves = refs[n + sum(ready) + 2 :]
-    rows = xs[0].shape[1]
-    w_in = start(columns(wv, place), bw, ins.at[n])
-    x_in = [start(x, bx.at[i], ins.at[i]) for i, x in enumerate(xs)]
-    copies, made, block = [], list(made), 0
-    for at, there in enumerate(ready):
-        if there:
-            copies.append(start(made.pop(0), out.at[:, pl.ds(at * rows, rows), :], moves.at[at]))
-    w_in.wait()
-    for at, there in enumerate(ready):
-        if not there:
-            for half in range(2):
-                x_in[2 * block + half].wait()
-                project(bx.at[2 * block + half], half, bw, "v", held.at[block], place)
-            copies.append(
-                start(held.at[block], out.at[:, pl.ds(at * rows, rows), :], outs.at[block])
-            )
-            block += 1
-    wait_all(copies)
-
-
-def make_values(place, blocks, made, ready, weight, name, late=()):
-    seqs, rows, width = blocks[0][0].shape
-    own = width // 2
-    pairs, span = HEADS // 4, 2 * seqs * 2 * HEAD
-    n = len(blocks)
-    dma = pltpu.SemaphoreType.DMA
-    return manual(
-        functools.partial(values_body, n, ready),
-        place,
-        [*(a for b in blocks for a in b), *made, weight],
-        [jax.ShapeDtypeStruct((pairs, rows * len(ready), span), BF16)],
-        [
-            pltpu.VMEM((2 * n, seqs, rows, width), BF16),
-            pltpu.VMEM((width, own), BF16),
-            pltpu.VMEM((n, pairs, rows, span), BF16),
-            dma((2 * n + 1,)),
-            dma((n,)),
-            dma((len(ready),)),
-        ],
-        n * 4 * seqs * rows * width * own,
-        name,
-        late,
-    )[0]
+def near_body(place, first, second, partner, wq, wk, qa, k1, k2):
+    project(first, 0, columns(wk, place), "k", k1, place)
+    project(second, 0, columns(wk, place), "k", k2, place)
+    project(partner, 0, columns(wq, place), "q", qa, place)
+
+
+def near_keys_body(place, a1, a2, first, second, wk, k1, k2):
+    half = a1.shape[2]
+    for a, x, k in ((a1, first, k1), (a2, second, k2)):
+        k[:, :, :half] = a[...]
+        project(x, 1, columns(wk, place), "k", k, place)
+
+
+def near_logits_body(place, q0, qa, k0, k1, k2, partner, wq, qb, *outs):
+    project(partner, 0, columns(wq, place), "q", qb, place)
+    write_logits([[q0], [qa, qb]], [k0, k1, k2], outs)
+
+
+def far_logits_body(place, q0, qa, qb, k, *outs):
+    write_logits([[q0], [qa, qb]], [k], outs)
+
+
+def values_body(place, *refs):
+    *xs, weight = refs[: len(refs) * 2 // 3 + 1]
+    for i, out in enumerate(refs[len(xs) + 1 :]):
+        for half in range(2):
+            project(xs[2 * i + half], half, columns(weight, place), "v", out, place)
+
+
+def gather_body(place, *refs):
+    out, at = refs[-1], 0
+    for ref in refs[:-1]:
+        rows = ref.shape[1]
+        out[:, at : at + rows, :] = ref[...]
+        at += rows
 
 
 def add_body(count, place, *refs):
@@ -260,21 +231,18 @@
     parts = [a for g in groups for a in g]
     rows = parts[0].shape[1]
     cols = sum(g[0].shape[2] for g in groups)
-    shape = (PARTS, 2, rows // PARTS, cols)
-    return call(
+    return local(
         functools.partial(add_body, PARTS),
         place,
         parts,
-        [whole(a.shape) for a in parts],
-        [jax.ShapeDtypeStruct(shape, BF16)],
-        [whole(shape)],
-        (1,),
+        [jax.ShapeDtypeStruct((PARTS, 2, rows // PARTS, cols), BF16)],
         sum(a.size for a in parts),
         "add_over_y",
     )[0]
 
 
-def softmax_body(scale, place, parts, other, out, same):
+def softmax_body(scale, place, parts, *refs):
+    out = refs[len(refs) // 2]
     z_lo = place[3]
     sides = []
     for side in (z_lo, 1 - z_lo):
@@ -287,24 +255,23 @@
     out[...] = (expo / jnp.sum(expo, axis=-1, keepdims=True)).astype(BF16)
 
 
-def softmax(place, parts, scale, other):
+def softmax(place, parts, scale, others):
     shape = (parts.shape[2], 2 * parts.shape[3])
-    free = pl.BlockSpec(memory_space=pl.ANY)
+    free = [pl.BlockSpec(memory_space=pl.ANY)] * len(others)
+    here = pl.BlockSpec(memory_space=pltpu.VMEM)
     return pl.pallas_call(
         functools.partial(softmax_body, scale),
-        out_shape=[
-            jax.ShapeDtypeStruct(shape, BF16),
-            jax.ShapeDtypeStruct(other.shape, other.dtype),
-        ],
-        in_specs=[pl.BlockSpec(memory_space=pltpu.SMEM), pl.BlockSpec(memory_space=pltpu.VMEM), free],
-        out_specs=[pl.BlockSpec(memory_space=pltpu.VMEM), free],
-        input_output_aliases={2: 1},
+        out_shape=[jax.ShapeDtypeStruct(shape, BF16)]
+        + [jax.ShapeDtypeStruct(a.shape, a.dtype) for a in others],
+        in_specs=[pl.BlockSpec(memory_space=pltpu.SMEM), here, *free],
+        out_specs=[here, *free],
+        input_output_aliases={2 + i: 1 + i for i in range(len(others))},
         compiler_params=pltpu.CompilerParams(vmem_limit_bytes=VMEM),
         cost_estimate=pl.CostEstimate(
             flops=parts.size * 8, bytes_accessed=parts.size * 4, transcendentals=parts.size // 4
         ),
         name="softmax",
-    )(place, parts, other)
+    )(place, parts, *others)
 
 
 def order_body(place, *refs):
@@ -331,38 +298,35 @@
 def mix_body(place, *refs):
     probs, values, outs = refs[:PARTS], refs[PARTS], refs[-2:]
     y = place[1]
-    group = probs[0].shape[1] // 2
+    pairs, half, _ = probs[0].shape
+    group = half // 2
     lanes = 2 * HEAD
     seqs = outs[0].shape[0]
-    p = jnp.concatenate([ref[0] for ref in probs], axis=0)
-    got = jnp.dot(p, values[0], preferred_element_type=F32)
     first = lax.broadcasted_iota(jnp.int32, (group, lanes), 1) < HEAD
-    for d in range(PARTS):
-        at = pl.multiple_of(rel(y - d) * group, group)
-        for s in range(2 * seqs):
-            one, two = (
-                got[(2 * d + h) * group : (2 * d + h + 1) * group, s * lanes : (s + 1) * lanes]
-                for h in range(2)
-            )
-            outs[s // seqs][s % seqs, pl.ds(at, group), :] = jnp.where(first, one, two).astype(BF16)
+    for pair in range(pairs):
+        p = jnp.concatenate([ref[pair] for ref in probs], axis=0)
+        got = jnp.dot(p, values[pair], preferred_element_type=F32)
+        for d in range(PARTS):
+            at = pl.multiple_of(rel(y - d) * group, group)
+            for s in range(2 * seqs):
+                one, two = (
+                    got[(2 * d + h) * group : (2 * d + h + 1) * group, s * lanes : (s + 1) * lanes]
+                    for h in range(2)
+                )
+                outs[s // seqs][
+                    s % seqs, pl.ds(at, group), pair * lanes : (pair + 1) * lanes
+                ] = jnp.where(first, one, two).astype(BF16)
 
 
 def mix(place, probs, values, seqs):
     pairs, half, cols = probs[0].shape
-    span = values.shape[2]
     rows = PARTS * half // 2
-    lanes = 2 * HEAD
-    shape = jax.ShapeDtypeStruct((seqs, rows, pairs * lanes), BF16)
-    return call(
+    return local(
         mix_body,
         place,
         [*probs, values],
-        [pl.BlockSpec((1, half, cols), lambda p, s: (p, 0, 0))] * PARTS
-        + [pl.BlockSpec((1, cols, span), lambda p, s: (p, 0, 0))],
-        [shape] * 2,
-        [pl.BlockSpec((seqs, rows, lanes), lambda p, s: (0, 0, p))] * 2,
-        (pairs,),
-        2 * pairs * PARTS * half * cols * span,
+        [jax.ShapeDtypeStruct((seqs, rows, pairs * 2 * HEAD), BF16)] * 2,
+        2 * pairs * PARTS * half * cols * values.shape[2],
         "mix",
     )
 
@@ -446,60 +410,89 @@
         12 * seqs * rows * width * half,
         "own",
     )
-    first, second, partner = tie([first, second, partner], queries)
-    far = send_x(first, 0)
+    first, second, partner = (tie([a], queries)[0] for a in (first, second, partner))
     near = [(first, swap(second)), (second, swap(first))]
     partner2 = (partner, swap(partner))
-    partner_queries, *near_logits = manual(
+    qa_shape, ka_shape = (*q_shape[:-1], span // 2), (*k_shape[:-1], span // 2)
+
+    def of(*shapes):
+        return [jax.ShapeDtypeStruct(s, BF16) for s in shapes]
+
+    work = 4 * seqs * rows * width * half
+    qa, ka1, ka2 = local(
         near_body,
         place,
-        [queries, keys, *partner2, *near[0], *near[1], query_matrix, key_matrix],
-        [jax.ShapeDtypeStruct(q_shape, BF16)] + [logits_shape(3)] * PARTS,
-        [bf(6, *data.shape), bf(2, width, half), bf(2, *q_shape), bf(pairs, 3 * rows, span)]
-        + [bf(PARTS, 2, pairs, 2 * group, 3 * rows), dma((10,)), dma((1,)), dma((pairs, PARTS))],
-        12 * seqs * rows * width * half,
+        [first, second, partner, query_matrix, key_matrix],
+        of(qa_shape, ka_shape, ka_shape),
+        3 * work // 2,
         "near",
     )
-    (far,) = tie([far], partner_queries)
-    far2 = (far, swap(far))
-    far_logits = manual(
-        far_body,
-        place,
-        [queries, partner_queries, *far2, key_matrix],
+    k1, k2 = local(
+        near_keys_body,
+        place,
+        [ka1, ka2, near[0][1], near[1][1], key_matrix],
+        of(k_shape, k_shape),
+        work,
+        "near_keys",
+    )
+    far_keys = send_x(k1, 0)
+    qb, *near_logits = local(
+        near_logits_body,
+        place,
+        [queries, qa, keys, k1, k2, partner2[1], query_matrix],
+        of(qa_shape) + [logits_shape(3)] * PARTS,
+        2 * work,
+        "near_logits",
+    )
+    (z_own,) = local(
+        values_body,
+        place,
+        [*partner2, value_matrix],
+        of(k_shape),
+        work,
+        "values_partner",
+        [qb],
+    )
+    z_first, z_second = send_x(z_own, 0), send_x(z_own, 1)
+    far_logits = local(
+        far_logits_body,
+        place,
+        [queries, qa, qb, far_keys],
         [logits_shape(1)] * PARTS,
-        [bf(2, *data.shape), bf(width, half), bf(2, *q_shape), bf(*k_shape)]
-        + [bf(PARTS, 2, pairs, 2 * group, rows), dma((5,)), dma((pairs, PARTS))],
-        4 * seqs * rows * width * half,
-        "far",
-    )
-
+        work // 2,
+        "far_logits",
+        [z_own],
+    )
     def over_y(parts):
         parts = [a.reshape(2, -1, a.shape[-1]) for a in parts]
         return [parts[0]] + [shift(parts[d], "y", d) for d in range(1, PARTS)]
 
     groups = [over_y(near_logits), over_y(far_logits)]
-    z_own = make_values(
-        place, [partner2], [], [False], value_matrix, "values_partner", far_logits[:1]
-    )
-    z_first, z_second = send_x(z_own, 0), send_x(z_own, 1)
     sent = add_parts(place, groups)
+    first_values, second_values = local(
+        values_body,
+        place,
+        [*near[0], *near[1], value_matrix],
+        of(k_shape, k_shape),
+        2 * work,
+        "values_near",
+        [far_logits[0]],
+    )
 
     sent = sent.reshape(2 * PARTS, *sent.shape[2:])
     got = lax.all_to_all(sent, ("z_hi", "z_lo"), 0, 0, tiled=True)
     got = got.reshape(PARTS, 2, *got.shape[1:])
     all_rows = seqs * lax.axis_size(("z_hi", "y", "core"))
-    probs, z_first = softmax(place, got, HEAD ** (-0.5) * all_rows ** (-0.5), z_first)
+    scale = HEAD ** (-0.5) * all_rows ** (-0.5)
+    probs, z_first, z_second, first_values = softmax(
+        place, got, scale, [z_first, z_second, first_values]
+    )
     z_far = send_x(z_first, 0)
+    far_values = send_x(first_values, 0)
     probs = order(place, [probs] + [shift(probs, "z_hi", d) for d in range(1, PARTS)])
     probs = probs.reshape(pairs, 2 * group, probs.shape[-1])
-    values = make_values(
-        place,
-        [*near, far2],
-        [values, z_own, z_first, z_second, z_far],
-        [True, False, False, False, True, True, True, True],
-        value_matrix,
-        "values",
-    )
+    parts = [values, first_values, second_values, far_values, z_own, z_first, z_second, z_far]
+    (values,) = local(gather_body, place, parts, of((pairs, 8 * rows, span)), 0, "gather_values")
     probs = [probs] + [shift(probs, "y", d) for d in range(1, PARTS)]
     mine, theirs = mix(place, probs, values, seqs)
     return finish(mine, swap(theirs), output_mine, output_theirs)

time: 129 us -> 123 us (0.953)
  Pallas kernels: 32.4 us -> 24.8 us
  local copies, waits for them, and re-layouts: 8.45 us -> 11.5 us
  waiting for transfers between devices: 50.1 us -> 48.5 us
    pallas_call x5 -> x1, Pallas kernels: 24.3 us -> 4.45 us  [manual(): pl.pallas_call(run, out_shape=outs, in_specs=[pl.BlockSpec(memory_space=p...]
    pallas_call x0 -> x9, Pallas kernels: none -> 17.1 us  [local(): pl.pallas_call(run, out_shape=outs, in_specs=[pl.BlockSpec(memory_space=p...]
    ppermute x19 -> x18, waiting for transfers between devices: 27.2 us -> 34.7 us  [shift(): return lax.ppermute(arr, axis, [(i, (i + step) % n) for i in range(n)])]
    all_to_all x1, waiting for transfers between devices: 13.6 us -> 6.33 us  [per_device(): got = lax.all_to_all(sent, ('z_hi', 'z_lo'), 0, 0, tiled=True)]
    pallas_call x3 -> x1, Pallas kernels: 4.92 us -> 0.57 us  [call(): pl.pallas_call(run, out_shape=outs, grid_spec=pltpu.PrefetchScalarGridSpe...]
    unnamed x32 -> x42, local copies, waits for them, and re-layouts: 8.37 us -> 11.4 us
    ppermute x6 -> x7, waiting for transfers between devices: 9.29 us -> 7.51 us  [send_x(): return lax.ppermute(arr, ('core', 'x'), ring_table(way))]
    ppermute x6 -> x7, starting transfers between devices: 4.57 us -> 5.36 us  [send_x(): return lax.ppermute(arr, ('core', 'x'), ring_table(way))]
  transfers between devices with their start and end apart: 26 -> 26, of which waited for: 14 -> 16; matrix products, arithmetic and copies ran while one was open for 0% -> 0% of each run, Pallas kernels for 22% -> 16%
where the time goes in v3:
time: 123 us; the launch traced here: 122 us
  waiting for transfers between devices  48.5 us (39%)
  starting transfers between devices  37.2 us (30%)
  Pallas kernels  24.8 us (20%)
  local copies, waits for them, and re-layouts  11.5 us (9%)
    ppermute x18, waiting for transfers between devices, shift(): return lax.ppermute(arr, axis, [(i, (i + step) % n) for i in range(n)])  34.7 us
    ppermute x18, starting transfers between devices, shift(): return lax.ppermute(arr, axis, [(i, (i + step) % n) for i in range(n)])  25.1 us
    pallas_call x9, Pallas kernels, local(): pl.pallas_call(run, out_shape=outs, in_specs=[pl.BlockSpec(memory_space=p...  17.1 us
    unnamed x42, local copies, waits for them, and re-layouts  11.4 us
    ppermute x7, waiting for transfers between devices, send_x(): return lax.ppermute(arr, ('core', 'x'), ring_table(way))  7.51 us
    all_to_all x1, starting transfers between devices, per_device(): got = lax.all_to_all(sent, ('z_hi', 'z_lo'), 0, 0, tiled=True)  6.78 us
    all_to_all x1, waiting for transfers between devices, per_device(): got = lax.all_to_all(sent, ('z_hi', 'z_lo'), 0, 0, tiled=True)  6.33 us
    ppermute x7, starting transfers between devices, send_x(): return lax.ppermute(arr, ('core', 'x'), ring_table(way))  5.36 us
  transfers between devices with their start and end apart: 26, of which 16 were waited for; matrix products, arithmetic and copies ran while one was open for 0% of the time, Pallas kernels for 16%

profile of v3, /device:TPU:1, one launch (start us, length us, event | category | flops | bytes accessed | tf_op | source)
XLA Modules:
  0.0 122.3 jit_solution(5600531887582518590)
XLA Ops:
  0.0 3.2 %collective-permute-start = (bf16[4,128,768]{2,1,0:T(8,128)(2,1)}, bf16[4,128,768]{2,1,0:T(8,128)(2,1)S(1)}, u32[]{:S(2)}, u32[]{:S(2)}) collective-permute-start(bf16[4,128,768]{2,1,0:T(8,128)(2,1)} %refs_1_.1), channel_id=1, source_target_pairs={{0,8},{8,0},{1,9},{9,1},{2,10},{10,2},{3,11},{11,3},{4,12},{12,4},... | collective-permute-start | bytes 2359304 | tf_op jit(solution)/shard_map/ppermute | solution.py:23
  3.2 2.7 %collective-permute-start.1 = (bf16[4,128,768]{2,1,0:T(8,128)(2,1)}, bf16[4,128,768]{2,1,0:T(8,128)(2,1)S(1)}, u32[]{:S(2)}, u32[]{:S(2)}) collective-permute-start(bf16[4,128,768]{2,1,0:T(8,128)(2,1)} %refs_1_.1), channel_id=1, source_target_pairs={{0,2},{2,4},{4,6},{6,0},{8,14},{10,8},{12,10},{14,12},{1,3},{3,5},... | collective-permute-start | bytes 2359304 | tf_op jit(solution)/shard_map/ppermute | solution.py:373
  11.0 4.5 %own.1 = (bf16[3,4,2,32,1024]{4,3,2,1,0:T(8,128)(2,1)S(1)}, bf16[3,128,1024]{2,1,0:T(8,128)(2,1)S(1)}, bf16[3,128,1024]{2,1,0:T(8,128)(2,1)S(1)}) custom-call(s32[4]{0:T(128)S(1)} %pad_add_fusion.refs_0_.place, bf16[4,128,768]{2,1,0:T(8,128)(2,1)S(1)} %copy-done.19, bf16[4,128,768]{2,1,0:T(8,128)(2,1)S(1)} %collective-permute-done.refs_2_, ...), custom_call_target="tpu_custom_call" | custom-call | flops 1811939328 | bytes 8257536 | tf_op jit(solution)/shard_map/own/pallas_call | solution.py:78
  15.4 7.2 %collective-permute-done.2.refs_0_ = bf16[4,128,768]{2,1,0:T(8,128)(2,1)S(1)} collective-permute-done((bf16[4,128,768]{2,1,0:T(8,128)(2,1)}, bf16[4,128,768]{2,1,0:T(8,128)(2,1)S(1)}, u32[]{:S(2)}, u32[]{:S(2)}) %collective-permute-start.2) | collective-permute-done | bytes 786464 | tf_op jit(solution)/shard_map/ppermute | solution.py:373
  25.7 2.0 %near.1 = (bf16[3,4,2,32,512]{4,3,2,1,0:T(8,128)(2,1)S(1)}, bf16[3,128,512]{2,1,0:T(8,128)(2,1)S(1)}, bf16[3,128,512]{2,1,0:T(8,128)(2,1)S(1)}) custom-call(s32[4]{0:T(128)S(1)} %pad_add_fusion.refs_0_.place, bf16[4,128,768]{2,1,0:T(8,128)(2,1)S(1)} %tie.3.refs_1_, bf16[4,128,768]{2,1,0:T(8,128)(2,1)S(1)} %tie.4.refs_2_.refs_3_, ...), custom_call_target="tpu_custom_call" | custom-call | flops 905969664 | bytes 6291456 | tf_op jit(solution)/shard_map/near/pallas_call | solution.py:101
  27.7 1.6 %near_keys.1 = (bf16[3,128,1024]{2,1,0:T(8,128)(2,1)S(1)}, bf16[3,128,1024]{2,1,0:T(8,128)(2,1)S(1)}) custom-call(s32[4]{0:T(128)S(1)} %pad_add_fusion.refs_0_.place, bf16[3,128,512]{2,1,0:T(8,128)(2,1)S(1)} %get-tuple-element.33.refs_1_, bf16[3,128,512]{2,1,0:T(8,128)(2,1)S(1)} %get-tuple-element.34.refs_2_, ...), custom_call_target="tpu_custom_call" | custom-call | flops 603979776 | bytes 5111808 | tf_op jit(solution)/shard_map/near_keys/pallas_call | solution.py:101
  30.4 2.8 %near_logits.1 = (bf16[3,4,2,32,512]{4,3,2,1,0:T(8,128)(2,1)S(1)}, bf16[2,3,64,384]{3,2,1,0:T(8,128)(2,1)S(1)}, bf16[2,3,64,384]{3,2,1,0:T(8,128)(2,1)S(1)}, bf1...) custom-call(s32[4]{0:T(128)S(1)} %pad_add_fusion.refs_0_.place, ...), custom_call_target="tpu_custom_call" | custom-call | flops 1207959552 | bytes 8650752 | tf_op jit(solution)/shard_map/near_logits/pallas_call | solution.py:101
  33.2 1.8 %collective-permute-start.7 = (bf16[2,192,384]{2,1,0:T(8,128)(2,1)S(1)}, bf16[2,192,384]{2,1,0:T(8,128)(2,1)S(1)}, u32[]{:S(2)}, u32[]{:S(2)}) collective-permute-start(bf16[2,192,384]{2,1,0:T(8,128)(2,1)S(1)} %bitcast.24), channel_id=1, source_target_pairs={{0,16},{16,32},{32,48},{48,0},{1,17},{17,33},{33,49},{49,1},{2,18}... | collective-permute-start | bytes 884744 | tf_op jit(solution)/shard_map/ppermute | solution.py:23
  35.0 2.6 %collective-permute-start.8 = (bf16[2,192,384]{2,1,0:T(8,128)(2,1)S(1)}, bf16[2,192,384]{2,1,0:T(8,128)(2,1)S(1)}, u32[]{:S(2)}, u32[]{:S(2)}) collective-permute-start(bf16[2,192,384]{2,1,0:T(8,128)(2,1)S(1)} %bitcast.23), channel_id=1, source_target_pairs={{0,32},{16,48},{32,0},{48,16},{1,33},{17,49},{33,1},{49,17},{2,34}... | collective-permute-start | bytes 884744 | tf_op jit(solution)/shard_map/ppermute | solution.py:23
  38.7 1.5 %values_partner.1.refs_5_ = bf16[3,128,1024]{2,1,0:T(8,128)(2,1)S(1)} custom-call(s32[4]{0:T(128)S(1)} %pad_add_fusion.refs_0_.place, bf16[4,128,768]{2,1,0:T(8,128)(2,1)S(1)} %tie.5.refs_3_.refs_1_, bf16[4,128,768]{2,1,0:T(8,128)(2,1)S(1)} %collective-permute-done.6.refs_6_.refs_2_, bf16[768,768]{1,0:T(8,128)(2,1)S(1)} %copy-done.7, ...), custom_call_target="tpu_custom_call" | custom-call | flops 603979776 | bytes 3538944 | tf_op jit(solution)/shard_map/values_partner/pallas_call | solution.py:101
  40.5 1.5 %far_logits.1 = (bf16[2,3,64,128]{3,2,1,0:T(8,128)(2,1)S(1)}, bf16[2,3,64,128]{3,2,1,0:T(8,128)(2,1)S(1)}, bf16[2,3,64,128]{3,2,1,0:T(8,128)(2,1)S(1)}, bf16[2,3,64,128]{3,2,1,0:T(8,128)(2,1)S(1)}) custom-call(s32[4]{0:T(128)S(1)} %pad_add_fusion.refs_0_.place, bf16[3,4,2,32,1024]{4,3,2,1,0:T(8,128)(2,1)S(1)} %get-tuple-element.30.refs_1_, ...), custom_call_target="tpu_custom_call" | custom-call | flops 301989888 | bytes 4325376 | tf_op jit(solution)/shard_map/far_logits/pallas_call | solution.py:101
  42.7 2.6 %collective-permute-start.12 = (bf16[2,192,128]{2,1,0:T(8,128)(2,1)S(1)}, bf16[2,192,128]{2,1,0:T(8,128)(2,1)S(1)}, u32[]{:S(2)}, u32[]{:S(2)}) collective-permute-start(bf16[2,192,128]{2,1,0:T(8,128)(2,1)S(1)} %bitcast.26), channel_id=1, source_target_pairs={{0,32},{16,48},{32,0},{48,16},{1,33},{17,49},{33,1},{49,17},{2,34}... | collective-permute-start | bytes 294920 | tf_op jit(solution)/shard_map/ppermute | solution.py:23
  45.3 3.4 %collective-permute-done.7.refs_2_ = bf16[2,192,384]{2,1,0:T(8,128)(2,1)S(1)} collective-permute-done((bf16[2,192,384]{2,1,0:T(8,128)(2,1)S(1)}, bf16[2,192,384]{2,1,0:T(8,128)(2,1)S(1)}, u32[]{:S(2)}, u32[]{:S(2)}) %collective-permute-start.7) | collective-permute-done | bytes 294944 | tf_op jit(solution)/shard_map/ppermute | solution.py:23
  48.7 1.7 %collective-permute-done.8.refs_3_ = bf16[2,192,384]{2,1,0:T(8,128)(2,1)S(1)} collective-permute-done((bf16[2,192,384]{2,1,0:T(8,128)(2,1)S(1)}, bf16[2,192,384]{2,1,0:T(8,128)(2,1)S(1)}, u32[]{:S(2)}, u32[]{:S(2)}) %collective-permute-start.8) | collective-permute-done | bytes 294944 | tf_op jit(solution)/shard_map/ppermute | solution.py:23
  55.0 1.5 %add_over_y.1 = bf16[4,2,48,512]{3,2,1,0:T(8,128)(2,1)} custom-call(s32[4]{0:T(128)S(1)} %pad_add_fusion.refs_0_.place, bf16[2,192,384]{2,1,0:T(8,128)(2,1)S(1)} %bitcast.20, bf16[2,192,384]{2,1,0:T(8,128)(2,1)S(1)} %collective-permute-done.7.refs_2_, bf16[2,192,384]{2,1,0:T(8,128)(2,1)S(1)} %collective-permute-done.8.refs_3_, ...), custom_call_target="tpu_custom_call" | custom-call | flops 786432 | bytes 1966080 | tf_op jit(solution)/shard_map/add_over_y/pallas_call | solution.py:101
  56.5 6.8 %all-to-all-start = ((bf16[8,48,512]{2,1,0:T(8,128)(2,1)}), bf16[8,48,512]{2,1,0:T(8,128)(2,1)S(1)}, u32[]{:S(2)}, u32[]{:S(2)}) async-start(bf16[8,48,512]{2,1,0:T(8,128)(2,1)} %bitcast.12), calls=%async_computation | async-start | bytes 786432 | tf_op jit(solution)/shard_map/all_to_all | solution.py:483
  68.8 2.4 %values_near.1 = (bf16[3,128,1024]{2,1,0:T(8,128)(2,1)}, bf16[3,128,1024]{2,1,0:T(8,128)(2,1)S(1)}) custom-call(s32[4]{0:T(128)S(1)} %pad_add_fusion.refs_0_.place, bf16[4,128,768]{2,1,0:T(8,128)(2,1)S(1)} %tie.3.refs_1_, bf16[4,128,768]{2,1,0:T(8,128)(2,1)S(1)} %copy-done.14, bf16[4,128,768]{2,1,0:T(8,128)(2,1)S(1)} %copy-done.5, ...), custom_call_target="tpu_custom_call" | custom-call | flops 1207959552 | bytes 5898240 | tf_op jit(solution)/shard_map/values_near/pallas_call | solution.py:101
  72.1 6.3 %all-to-all-done = bf16[8,48,512]{2,1,0:T(8,128)(2,1)S(1)} async-done(((bf16[8,48,512]{2,1,0:T(8,128)(2,1)}), bf16[8,48,512]{2,1,0:T(8,128)(2,1)S(1)}, u32[]{:S(2)}, u32[]{:S(2)}) %all-to-all-start) | async-done | bytes 393248 | tf_op jit(solution)/shard_map/all_to_all | solution.py:483
  79.5 2.7 %collective-permute-start.17 = (bf16[48,1024]{1,0:T(8,128)(2,1)S(1)}, bf16[48,1024]{1,0:T(8,128)(2,1)S(1)}, u32[]{:S(2)}, u32[]{:S(2)}) collective-permute-start(bf16[48,1024]{1,0:T(8,128)(2,1)S(1)} %get-tuple-element.47.refs_1_), channel_id=1, source_target_pairs={{0,128},{64,192},{128,0},{192,64},{1,129},{65,193},{129,1},{193,65... | collective-permute-start | bytes 294920 | tf_op jit(solution)/shard_map/ppermute | solution.py:23
  82.2 1.4 %collective-permute-start.18 = (bf16[48,1024]{1,0:T(8,128)(2,1)S(1)}, bf16[48,1024]{1,0:T(8,128)(2,1)S(1)}, u32[]{:S(2)}, u32[]{:S(2)}) collective-permute-start(bf16[48,1024]{1,0:T(8,128)(2,1)S(1)} %get-tuple-element.47.refs_1_), channel_id=1, source_target_pairs={{0,192},{64,0},{128,64},{192,128},{1,193},{65,1},{129,65},{193,129... | collective-permute-start | bytes 294920 | tf_op jit(solution)/shard_map/ppermute | solution.py:23
  83.6 2.5 %collective-permute-done.16.refs_2_ = bf16[48,1024]{1,0:T(8,128)(2,1)S(1)} collective-permute-done((bf16[48,1024]{1,0:T(8,128)(2,1)S(1)}, bf16[48,1024]{1,0:T(8,128)(2,1)S(1)}, u32[]{:S(2)}, u32[]{:S(2)}) %collective-permute-start.16) | collective-permute-done | bytes 98336 | tf_op jit(solution)/shard_map/ppermute | solution.py:23
  86.1 3.4 %collective-permute-done.17.refs_3_ = bf16[48,1024]{1,0:T(8,128)(2,1)S(1)} collective-permute-done((bf16[48,1024]{1,0:T(8,128)(2,1)S(1)}, bf16[48,1024]{1,0:T(8,128)(2,1)S(1)}, u32[]{:S(2)}, u32[]{:S(2)}) %collective-permute-start.17) | collective-permute-done | bytes 98336 | tf_op jit(solution)/shard_map/ppermute | solution.py:23
  89.5 4.7 %collective-permute-done.18.refs_4_ = bf16[48,1024]{1,0:T(8,128)(2,1)S(1)} collective-permute-done((bf16[48,1024]{1,0:T(8,128)(2,1)S(1)}, bf16[48,1024]{1,0:T(8,128)(2,1)S(1)}, u32[]{:S(2)}, u32[]{:S(2)}) %collective-permute-start.18) | collective-permute-done | bytes 98336 | tf_op jit(solution)/shard_map/ppermute | solution.py:23
  94.8 1.6 %collective-permute-start.19 = (bf16[3,64,1024]{2,1,0:T(8,128)(2,1)S(1)}, bf16[3,64,1024]{2,1,0:T(8,128)(2,1)S(1)}, u32[]{:S(2)}, u32[]{:S(2)}) collective-permute-start(bf16[3,64,1024]{2,1,0:T(8,128)(2,1)S(1)} %bitcast.15), channel_id=1, source_target_pairs={{0,16},{16,32},{32,48},{48,0},{1,17},{17,33},{33,49},{49,1},{2,18}... | collective-permute-start | bytes 1179656 | tf_op jit(solution)/shard_map/ppermute | solution.py:23
  96.4 1.6 %collective-permute-start.20 = (bf16[3,64,1024]{2,1,0:T(8,128)(2,1)S(1)}, bf16[3,64,1024]{2,1,0:T(8,128)(2,1)S(1)}, u32[]{:S(2)}, u32[]{:S(2)}) collective-permute-start(bf16[3,64,1024]{2,1,0:T(8,128)(2,1)S(1)} %bitcast.16), channel_id=1, source_target_pairs={{0,32},{16,48},{32,0},{48,16},{1,33},{17,49},{33,1},{49,17},{2,34}... | collective-permute-start | bytes 1179656 | tf_op jit(solution)/shard_map/ppermute | solution.py:23
  98.0 2.0 %collective-permute-start.21 = (bf16[3,64,1024]{2,1,0:T(8,128)(2,1)S(1)}, bf16[3,64,1024]{2,1,0:T(8,128)(2,1)S(1)}, u32[]{:S(2)}, u32[]{:S(2)}) collective-permute-start(bf16[3,64,1024]{2,1,0:T(8,128)(2,1)S(1)} %bitcast.17), channel_id=1, source_target_pairs={{0,48},{16,0},{32,16},{48,32},{1,49},{17,1},{33,17},{49,33},{2,50}... | collective-permute-start | bytes 1179656 | tf_op jit(solution)/shard_map/ppermute | solution.py:23
  100.0 1.6 %gather_values.1.refs_5_ = bf16[3,1024,1024]{2,1,0:T(8,128)(2,1)S(1)} custom-call(s32[4]{0:T(128)S(1)} %pad_add_fusion.refs_0_.place, bf16[3,128,1024]{2,1,0:T(8,128)(2,1)S(1)} %copy-done.10, bf16[3,128,1024]{2,1,0:T(8,128)(2,1)} %get-tuple-element.49.refs_2_, bf16[3,128,1024]{2,1,0:T(8,128)(2,1)S(1)} %copy-done.12, ...), custom_call_target="tpu_custom_call" | custom-call | bytes 12582912 | tf_op jit(solution)/shard_map/gather_values/pallas_call | solution.py:101
  101.6 4.7 %collective-permute-done.19.refs_2_ = bf16[3,64,1024]{2,1,0:T(8,128)(2,1)S(1)} collective-permute-done((bf16[3,64,1024]{2,1,0:T(8,128)(2,1)S(1)}, bf16[3,64,1024]{2,1,0:T(8,128)(2,1)S(1)}, u32[]{:S(2)}, u32[]{:S(2)}) %collective-permute-start.19) | collective-permute-done | bytes 393248 | tf_op jit(solution)/shard_map/ppermute | solution.py:23
  106.3 9.1 %collective-permute-done.20.refs_3_ = bf16[3,64,1024]{2,1,0:T(8,128)(2,1)S(1)} collective-permute-done((bf16[3,64,1024]{2,1,0:T(8,128)(2,1)S(1)}, bf16[3,64,1024]{2,1,0:T(8,128)(2,1)S(1)}, u32[]{:S(2)}, u32[]{:S(2)}) %collective-permute-start.20) | collective-permute-done | bytes 393248 | tf_op jit(solution)/shard_map/ppermute | solution.py:23
  115.4 2.4 %mix.1 = (bf16[4,128,384]{2,1,0:T(8,128)(2,1)S(1)}, bf16[4,128,384]{2,1,0:T(8,128)(2,1)S(1)}) custom-call(s32[4]{0:T(128)S(1)} %pad_add_fusion.refs_0_.place, bf16[3,64,1024]{2,1,0:T(8,128)(2,1)S(1)} %bitcast.18, bf16[3,64,1024]{2,1,0:T(8,128)(2,1)S(1)} %collective-permute-done.19.refs_2_, bf16[3,64,1024]{2,1,0:T(8,128)(2,1)S(1)} %collective-permute-done.20.refs_3_, ...), custom_call_target="tpu_custom_call" | custom-call | flops 1610612736 | bytes 8650752 | tf_op jit(solution)/shard_map/mix/pallas_call | solution.py:101
  117.8 1.3 %collective-permute-start.24 = (bf16[4,128,384]{2,1,0:T(8,128)(2,1)S(1)}, bf16[4,128,384]{2,1,0:T(8,128)(2,1)S(1)}, u32[]{:S(2)}, u32[]{:S(2)}) collective-permute-start(bf16[4,128,384]{2,1,0:T(8,128)(2,1)S(1)} %get-tuple-element.54), channel_id=1, source_target_pairs={{0,8},{8,0},{1,9},{9,1},{2,10},{10,2},{3,11},{11,3},{4,12},{12,4},... | collective-permute-start | bytes 1179656 | tf_op jit(solution)/shard_map/ppermute | solution.py:23
  120.4 1.9 %finish.1 = bf16[4,128,768]{2,1,0:T(8,128)(2,1)} custom-call(bf16[4,128,384]{2,1,0:T(8,128)(2,1)S(1)} %get-tuple-element.53.mine, bf16[4,128,384]{2,1,0:T(8,128)(2,1)S(1)} %collective-permute-done.24.theirs, bf16[384,768]{1,0:T(8,128)(2,1)S(1)} %get-tuple-element.56.weight_mine, bf16[384,768]{1,0:T(8,128)(2,1)S(1)} %get-tuple-element.55.weight_theirs), custom_call_target="tpu_custom_call" | custom-call | flops 603979776 | bytes 2752512 | tf_op jit(solution)/shard_map/finish/pallas_call | solution.py:347
  (80 shorter events, 25.2 us)
Async XLA Ops:
  0.0 6.0 %collective-permute-start = (bf16[4,128,768]{2,1,0:T(8,128)(2,1)}, bf16[4,128,768]{2,1,0:T(8,128)(2,1)S(1)}, u32[]{:S(2)}, u32[]{:S(2)}) collective-permute-start(bf16[4,128,768]{2,1,0:T(8,128)(2,1)} %refs_1_.1), channel_id=1, source_target_pairs={{0,8},{8,0},{1,9},{9,1},{2,10},{10,2},{3,11},{11,3},{4,12},{12,4},... | collective-permute-start | bytes 2359304 | tf_op jit(solution)/shard_map/ppermute | solution.py:23
  3.2 19.4 %collective-permute-start.2 = (bf16[4,128,768]{2,1,0:T(8,128)(2,1)}, bf16[4,128,768]{2,1,0:T(8,128)(2,1)S(1)}, u32[]{:S(2)}, u32[]{:S(2)}) collective-permute-start(bf16[4,128,768]{2,1,0:T(8,128)(2,1)} %refs_1_.1), channel_id=1, source_target_pairs={{0,6},{2,0},{4,2},{6,4},{8,10},{10,12},{12,14},{14,8},{1,7},{3,1},... | collective-permute-start | bytes 2359304 | tf_op jit(solution)/shard_map/ppermute | solution.py:373
  3.2 20.2 %collective-permute-start.1 = (bf16[4,128,768]{2,1,0:T(8,128)(2,1)}, bf16[4,128,768]{2,1,0:T(8,128)(2,1)S(1)}, u32[]{:S(2)}, u32[]{:S(2)}) collective-permute-start(bf16[4,128,768]{2,1,0:T(8,128)(2,1)} %refs_1_.1), channel_id=1, source_target_pairs={{0,2},{2,4},{4,6},{6,0},{8,14},{10,8},{12,10},{14,12},{1,3},{3,5},... | collective-permute-start | bytes 2359304 | tf_op jit(solution)/shard_map/ppermute | solution.py:373
  5.9 19.4 %collective-permute-start.3 = (bf16[4,128,768]{2,1,0:T(8,128)(2,1)}, bf16[4,128,768]{2,1,0:T(8,128)(2,1)S(1)}, u32[]{:S(2)}, u32[]{:S(2)}) collective-permute-start(bf16[4,128,768]{2,1,0:T(8,128)(2,1)} %refs_1_.1), channel_id=1, source_target_pairs={{0,1},{1,0},{2,3},{3,2},{4,5},{5,4},{6,7},{7,6},{8,9},{9,8},{10,11... | collective-permute-start | bytes 2359304 | tf_op jit(solution)/shard_map/ppermute | solution.py:23
  15.4 7.3 %copy-start.9 = (bf16[3,128,1024]{2,1,0:T(8,128)(2,1)}, bf16[3,128,1024]{2,1,0:T(8,128)(2,1)S(1)}, u32[]{:S(2)}) copy-start(bf16[3,128,1024]{2,1,0:T(8,128)(2,1)S(1)} %get-tuple-element.48.refs_1_) | copy-start | bytes 2359300
  22.7 5.0 %collective-permute-start.4 = (bf16[4,128,768]{2,1,0:T(8,128)(2,1)S(1)}, bf16[4,128,768]{2,1,0:T(8,128)(2,1)S(1)}, u32[]{:S(2)}, u32[]{:S(2)}) collective-permute-start(bf16[4,128,768]{2,1,0:T(8,128)(2,1)S(1)} %tie.4.refs_2_.refs_3_), channel_id=1, source_target_pairs={{0,8},{8,0},{1,9},{9,1},{2,10},{10,2},{3,11},{11,3},{4,12},{12,4},... | collective-permute-start | bytes 2359304 | tf_op jit(solution)/shard_map/ppermute | solution.py:23
  23.4 4.3 %collective-permute-start.5 = (bf16[4,128,768]{2,1,0:T(8,128)(2,1)S(1)}, bf16[4,128,768]{2,1,0:T(8,128)(2,1)S(1)}, u32[]{:S(2)}, u32[]{:S(2)}) collective-permute-start(bf16[4,128,768]{2,1,0:T(8,128)(2,1)S(1)} %tie.3.refs_1_), channel_id=1, source_target_pairs={{0,8},{8,0},{1,9},{9,1},{2,10},{10,2},{3,11},{11,3},{4,12},{12,4},... | collective-permute-start | bytes 2359304 | tf_op jit(solution)/shard_map/ppermute | solution.py:23
  25.3 5.1 %collective-permute-start.6 = (bf16[4,128,768]{2,1,0:T(8,128)(2,1)S(1)}, bf16[4,128,768]{2,1,0:T(8,128)(2,1)S(1)}, u32[]{:S(2)}, u32[]{:S(2)}) collective-permute-start(bf16[4,128,768]{2,1,0:T(8,128)(2,1)S(1)} %tie.5.refs_3_.refs_1_), channel_id=1, source_target_pairs={{0,8},{8,0},{1,9},{9,1},{2,10},{10,2},{3,11},{11,3},{4,12},{12,4},... | collective-permute-start | bytes 2359304 | tf_op jit(solution)/shard_map/ppermute | solution.py:23
  29.3 11.2 %collective-permute-start.10 = (bf16[3,128,1024]{2,1,0:T(8,128)(2,1)S(1)}, bf16[3,128,1024]{2,1,0:T(8,128)(2,1)S(1)}, u32[]{:S(2)}, u32[]{:S(2)}) collective-permute-start(bf16[3,128,1024]{2,1,0:T(8,128)(2,1)S(1)} %get-tuple-element.35.refs_4_), channel_id=1, source_target_pairs={{0,2},{2,4},{4,6},{6,0},{8,14},{10,8},{12,10},{14,12},{1,3},{3,5},... | collective-permute-start | bytes 2359304 | tf_op jit(solution)/shard_map/ppermute | solution.py:373
  30.4 8.3 %copy-start.7 = (bf16[768,768]{1,0:T(8,128)(2,1)S(1)}, bf16[768,768]{1,0:T(8,128)(2,1)}, u32[]{:S(2)}) copy-start(bf16[768,768]{1,0:T(8,128)(2,1)} %refs_5_.7) | copy-start | bytes 3538948
  33.2 15.5 %collective-permute-start.7 = (bf16[2,192,384]{2,1,0:T(8,128)(2,1)S(1)}, bf16[2,192,384]{2,1,0:T(8,128)(2,1)S(1)}, u32[]{:S(2)}, u32[]{:S(2)}) collective-permute-start(bf16[2,192,384]{2,1,0:T(8,128)(2,1)S(1)} %bitcast.24), channel_id=1, source_target_pairs={{0,16},{16,32},{32,48},{48,0},{1,17},{17,33},{33,49},{49,1},{2,18}... | collective-permute-start | bytes 884744 | tf_op jit(solution)/shard_map/ppermute | solution.py:23
  35.0 15.3 %collective-permute-start.8 = (bf16[2,192,384]{2,1,0:T(8,128)(2,1)S(1)}, bf16[2,192,384]{2,1,0:T(8,128)(2,1)S(1)}, u32[]{:S(2)}, u32[]{:S(2)}) collective-permute-start(bf16[2,192,384]{2,1,0:T(8,128)(2,1)S(1)} %bitcast.23), channel_id=1, source_target_pairs={{0,32},{16,48},{32,0},{48,16},{1,33},{17,49},{33,1},{49,17},{2,34}... | collective-permute-start | bytes 884744 | tf_op jit(solution)/shard_map/ppermute | solution.py:23
  37.7 13.3 %collective-permute-start.9 = (bf16[2,192,384]{2,1,0:T(8,128)(2,1)S(1)}, bf16[2,192,384]{2,1,0:T(8,128)(2,1)S(1)}, u32[]{:S(2)}, u32[]{:S(2)}) collective-permute-start(bf16[2,192,384]{2,1,0:T(8,128)(2,1)S(1)} %bitcast.22), channel_id=1, source_target_pairs={{0,48},{16,0},{32,16},{48,32},{1,49},{17,1},{33,17},{49,33},{2,50}... | collective-permute-start | bytes 884744 | tf_op jit(solution)/shard_map/ppermute | solution.py:23
  42.0 14.4 %copy-start.17 = (bf16[2,3,64,128]{3,2,1,0:T(8,128)(2,1)}, bf16[2,3,64,128]{3,2,1,0:T(8,128)(2,1)S(1)}, u32[]{:S(2)}) copy-start(bf16[2,3,64,128]{3,2,1,0:T(8,128)(2,1)S(1)} %get-tuple-element.42.refs_6_) | copy-start | bytes 294916
  42.0 10.9 %collective-permute-start.11 = (bf16[2,192,128]{2,1,0:T(8,128)(2,1)S(1)}, bf16[2,192,128]{2,1,0:T(8,128)(2,1)S(1)}, u32[]{:S(2)}, u32[]{:S(2)}) collective-permute-start(bf16[2,192,128]{2,1,0:T(8,128)(2,1)S(1)} %bitcast.27), channel_id=1, source_target_pairs={{0,16},{16,32},{32,48},{48,0},{1,17},{17,33},{33,49},{49,1},{2,18}... | collective-permute-start | bytes 294920 | tf_op jit(solution)/shard_map/ppermute | solution.py:23
  42.7 11.0 %collective-permute-start.12 = (bf16[2,192,128]{2,1,0:T(8,128)(2,1)S(1)}, bf16[2,192,128]{2,1,0:T(8,128)(2,1)S(1)}, u32[]{:S(2)}, u32[]{:S(2)}) collective-permute-start(bf16[2,192,128]{2,1,0:T(8,128)(2,1)S(1)} %bitcast.26), channel_id=1, source_target_pairs={{0,32},{16,48},{32,0},{48,16},{1,33},{17,49},{33,1},{49,17},{2,34}... | collective-permute-start | bytes 294920 | tf_op jit(solution)/shard_map/ppermute | solution.py:23
  48.7 6.3 %collective-permute-start.13 = (bf16[2,192,128]{2,1,0:T(8,128)(2,1)S(1)}, bf16[2,192,128]{2,1,0:T(8,128)(2,1)S(1)}, u32[]{:S(2)}, u32[]{:S(2)}) collective-permute-start(bf16[2,192,128]{2,1,0:T(8,128)(2,1)S(1)} %bitcast.25), channel_id=1, source_target_pairs={{0,48},{16,0},{32,16},{48,32},{1,49},{17,1},{33,17},{49,33},{2,50}... | collective-permute-start | bytes 294920 | tf_op jit(solution)/shard_map/ppermute | solution.py:23
  50.4 21.8 %collective-permute-start.14 = (bf16[3,128,1024]{2,1,0:T(8,128)(2,1)S(1)}, bf16[3,128,1024]{2,1,0:T(8,128)(2,1)S(1)}, u32[]{:S(2)}, u32[]{:S(2)}) collective-permute-start(bf16[3,128,1024]{2,1,0:T(8,128)(2,1)S(1)} %values_partner.1.refs_5_), channel_id=1, source_target_pairs={{0,2},{2,4},{4,6},{6,0},{8,14},{10,8},{12,10},{14,12},{1,3},{3,5},... | collective-permute-start | bytes 2359304 | tf_op jit(solution)/shard_map/ppermute | solution.py:373
  51.0 21.1 %collective-permute-start.15 = (bf16[3,128,1024]{2,1,0:T(8,128)(2,1)S(1)}, bf16[3,128,1024]{2,1,0:T(8,128)(2,1)S(1)}, u32[]{:S(2)}, u32[]{:S(2)}) collective-permute-start(bf16[3,128,1024]{2,1,0:T(8,128)(2,1)S(1)} %values_partner.1.refs_5_), channel_id=1, source_target_pairs={{0,6},{2,0},{4,2},{6,4},{8,10},{10,12},{12,14},{14,8},{1,7},{3,1},... | collective-permute-start | bytes 2359304 | tf_op jit(solution)/shard_map/ppermute | solution.py:373
  56.5 22.0 %all-to-all-start = ((bf16[8,48,512]{2,1,0:T(8,128)(2,1)}), bf16[8,48,512]{2,1,0:T(8,128)(2,1)S(1)}, u32[]{:S(2)}, u32[]{:S(2)}) async-start(bf16[8,48,512]{2,1,0:T(8,128)(2,1)} %bitcast.12), calls=%async_computation | async-start | bytes 786432 | tf_op jit(solution)/shard_map/all_to_all | solution.py:483
  78.5 21.5 %copy-start.10 = (bf16[3,128,1024]{2,1,0:T(8,128)(2,1)S(1)}, bf16[3,128,1024]{2,1,0:T(8,128)(2,1)}, u32[]{:S(2)}) copy-start(bf16[3,128,1024]{2,1,0:T(8,128)(2,1)} %copy-done.9) | copy-start | bytes 2359300
  78.5 21.5 %copy-start.12 = (bf16[3,128,1024]{2,1,0:T(8,128)(2,1)S(1)}, bf16[3,128,1024]{2,1,0:T(8,128)(2,1)}, u32[]{:S(2)}) copy-start(bf16[3,128,1024]{2,1,0:T(8,128)(2,1)} %copy-done.11) | copy-start | bytes 2359300
  79.2 20.7 %collective-permute-start.22 = (bf16[3,128,1024]{2,1,0:T(8,128)(2,1)}, bf16[3,128,1024]{2,1,0:T(8,128)(2,1)S(1)}, u32[]{:S(2)}, u32[]{:S(2)}) collective-permute-start(bf16[3,128,1024]{2,1,0:T(8,128)(2,1)} %get-tuple-element.49.refs_2_), channel_id=1, source_target_pairs={{0,2},{2,4},{4,6},{6,0},{8,14},{10,8},{12,10},{14,12},{1,3},{3,5},... | collective-permute-start | bytes 2359304 | tf_op jit(solution)/shard_map/ppermute | solution.py:373
  79.3 20.7 %collective-permute-start.23 = (bf16[3,128,1024]{2,1,0:T(8,128)(2,1)S(1)}, bf16[3,128,1024]{2,1,0:T(8,128)(2,1)S(1)}, u32[]{:S(2)}, u32[]{:S(2)}) collective-permute-start(bf16[3,128,1024]{2,1,0:T(8,128)(2,1)S(1)} %get-tuple-element.51.refs_6_), channel_id=1, source_target_pairs={{0,2},{2,4},{4,6},{6,0},{8,14},{10,8},{12,10},{14,12},{1,3},{3,5},... | collective-permute-start | bytes 2359304 | tf_op jit(solution)/shard_map/ppermute | solution.py:373
  79.4 6.7 %collective-permute-start.16 = (bf16[48,1024]{1,0:T(8,128)(2,1)S(1)}, bf16[48,1024]{1,0:T(8,128)(2,1)S(1)}, u32[]{:S(2)}, u32[]{:S(2)}) collective-permute-start(bf16[48,1024]{1,0:T(8,128)(2,1)S(1)} %get-tuple-element.47.refs_1_), channel_id=1, source_target_pairs={{0,64},{64,128},{128,192},{192,0},{1,65},{65,129},{129,193},{193,1... | collective-permute-start | bytes 294920 | tf_op jit(solution)/shard_map/ppermute | solution.py:23
  79.5 9.9 %collective-permute-start.17 = (bf16[48,1024]{1,0:T(8,128)(2,1)S(1)}, bf16[48,1024]{1,0:T(8,128)(2,1)S(1)}, u32[]{:S(2)}, u32[]{:S(2)}) collective-permute-start(bf16[48,1024]{1,0:T(8,128)(2,1)S(1)} %get-tuple-element.47.refs_1_), channel_id=1, source_target_pairs={{0,128},{64,192},{128,0},{192,64},{1,129},{65,193},{129,1},{193,65... | collective-permute-start | bytes 294920 | tf_op jit(solution)/shard_map/ppermute | solution.py:23
  82.2 12.0 %collective-permute-start.18 = (bf16[48,1024]{1,0:T(8,128)(2,1)S(1)}, bf16[48,1024]{1,0:T(8,128)(2,1)S(1)}, u32[]{:S(2)}, u32[]{:S(2)}) collective-permute-start(bf16[48,1024]{1,0:T(8,128)(2,1)S(1)} %get-tuple-element.47.refs_1_), channel_id=1, source_target_pairs={{0,192},{64,0},{128,64},{192,128},{1,193},{65,1},{129,65},{193,129... | collective-permute-start | bytes 294920 | tf_op jit(solution)/shard_map/ppermute | solution.py:23
  94.8 11.5 %collective-permute-start.19 = (bf16[3,64,1024]{2,1,0:T(8,128)(2,1)S(1)}, bf16[3,64,1024]{2,1,0:T(8,128)(2,1)S(1)}, u32[]{:S(2)}, u32[]{:S(2)}) collective-permute-start(bf16[3,64,1024]{2,1,0:T(8,128)(2,1)S(1)} %bitcast.15), channel_id=1, source_target_pairs={{0,16},{16,32},{32,48},{48,0},{1,17},{17,33},{33,49},{49,1},{2,18}... | collective-permute-start | bytes 1179656 | tf_op jit(solution)/shard_map/ppermute | solution.py:23
  96.4 19.0 %collective-permute-start.20 = (bf16[3,64,1024]{2,1,0:T(8,128)(2,1)S(1)}, bf16[3,64,1024]{2,1,0:T(8,128)(2,1)S(1)}, u32[]{:S(2)}, u32[]{:S(2)}) collective-permute-start(bf16[3,64,1024]{2,1,0:T(8,128)(2,1)S(1)} %bitcast.16), channel_id=1, source_target_pairs={{0,32},{16,48},{32,0},{48,16},{1,33},{17,49},{33,1},{49,17},{2,34}... | collective-permute-start | bytes 1179656 | tf_op jit(solution)/shard_map/ppermute | solution.py:23
  98.0 17.4 %collective-permute-start.21 = (bf16[3,64,1024]{2,1,0:T(8,128)(2,1)S(1)}, bf16[3,64,1024]{2,1,0:T(8,128)(2,1)S(1)}, u32[]{:S(2)}, u32[]{:S(2)}) collective-permute-start(bf16[3,64,1024]{2,1,0:T(8,128)(2,1)S(1)} %bitcast.17), channel_id=1, source_target_pairs={{0,48},{16,0},{32,16},{48,32},{1,49},{17,1},{33,17},{49,33},{2,50}... | collective-permute-start | bytes 1179656 | tf_op jit(solution)/shard_map/ppermute | solution.py:23
  101.6 17.5 %copy-start.20 = (bf16[768,768]{1,0:T(8,128)(2,1)S(1)}, bf16[768,768]{1,0:T(8,128)(2,1)}, u32[]{:S(2)}) copy-start(bf16[768,768]{1,0:T(8,128)(2,1)} %param.9) | copy-start | bytes 3538948
  117.8 2.7 %collective-permute-start.24 = (bf16[4,128,384]{2,1,0:T(8,128)(2,1)S(1)}, bf16[4,128,384]{2,1,0:T(8,128)(2,1)S(1)}, u32[]{:S(2)}, u32[]{:S(2)}) collective-permute-start(bf16[4,128,384]{2,1,0:T(8,128)(2,1)S(1)} %get-tuple-element.54), channel_id=1, source_target_pairs={{0,8},{8,0},{1,9},{9,1},{2,10},{10,2},{3,11},{11,3},{4,12},{12,4},... | collective-permute-start | bytes 1179656 | tf_op jit(solution)/shard_map/ppermute | solution.py:23
  (15 other events, 22.2 us)

commit v4 on v3

--- a/solution.py
+++ b/solution.py
@@ -121,38 +121,64 @@
     return weight.at[:, pl.ds(pl.multiple_of(place[0] * own, own), own)]
 
 
-def project(x_ref, half, weight, kind, out, place, base=0):
+def project(x_ref, half, weight, out, place):
     seqs, rows, width = x_ref.shape
     lanes = 2 * HEAD
-    pairs = weight.shape[1] // lanes
-    group = rows // PARTS
-    x = x_ref[...].reshape(seqs * rows, width)
-    got = jnp.dot(x, weight[...], preferred_element_type=F32).astype(BF16)
+    got = jnp.dot(
+        x_ref[...].reshape(seqs * rows, width), weight[...], preferred_element_type=F32
+    ).astype(BF16)
     for s in range(seqs):
         at = (half * seqs + s) * lanes
-        for p in range(pairs):
-            part = got[s * rows : (s + 1) * rows, p * lanes : (p + 1) * lanes]
-            if kind != "q":
-                out[p, base : base + rows, at : at + lanes] = part
-                continue
-            first = lax.broadcasted_iota(jnp.int32, part.shape, 1) < HEAD
+        for p in range(out.shape[0]):
+            out[p, :, at : at + lanes] = got[s * rows : (s + 1) * rows, p * lanes : (p + 1) * lanes]
+
+
+def project_heads(x_ref, half, weights, out, place):
+    seqs, rows, width = x_ref.shape
+    lanes, some = 2 * HEAD, seqs // 2
+    group = rows // PARTS
+    sides = [
+        jnp.dot(
+            x_ref[i * some : (i + 1) * some].reshape(some * rows, width),
+            weights[i],
+            preferred_element_type=F32,
+        ).astype(BF16)
+        for i in range(2)
+    ]
+    first = lax.broadcasted_iota(jnp.int32, (rows, lanes), 1) < HEAD
+    for s in range(some):
+        at = (half * some + s) * lanes
+        for p in range(out.shape[0] // 2):
+            one, two = (a[s * rows : (s + 1) * rows, p * lanes : (p + 1) * lanes] for a in sides)
             for h in range(2):
-                kept = jnp.where(first == (h == 0), part, jnp.zeros_like(part))
+                part = jnp.where(first, two, one) if h else jnp.where(first, one, two)
+                if len(out.shape) == 3:
+                    out[2 * p + h, :, at : at + lanes] = part
+                    continue
                 for a in range(PARTS):
-                    out[p, rel(a - place[1]), h, :, at : at + lanes] = kept[
+                    out[2 * p + h, rel(a - place[1]), :, at : at + lanes] = part[
                         a * group : (a + 1) * group
                     ]
 
 
 def write_logits(queries, keys, outs):
-    half = outs[0].shape[2]
-    for p in range(outs[0].shape[1]):
-        k = jnp.concatenate([ref[p] for ref in keys], axis=0)
-        for i, refs in enumerate(queries):
-            q = jnp.concatenate([ref[p].reshape(PARTS * half, -1) for ref in refs], axis=-1)
-            got = lax.dot_general(q, k, (((1,), (1,)), ((), ())), preferred_element_type=F32)
+    group = outs[0].shape[2] // 2
+    for head in range(keys[0].shape[0]):
+        k = jnp.concatenate([ref[head] for ref in keys], axis=0)
+        q = jnp.concatenate(
+            [
+                jnp.concatenate([ref[head].reshape(PARTS * group, -1) for ref in refs], axis=-1)
+                for refs in queries
+            ],
+            axis=0,
+        )
+        got = lax.dot_general(q, k, (((1,), (1,)), ((), ())), preferred_element_type=F32)
+        at = head % 2 * group
+        for i in range(len(queries)):
             for d, out in enumerate(outs):
-                out[i, p] = got[d * half : (d + 1) * half].astype(BF16)
+                out[i, head // 2, at : at + group] = got[
+                    (i * PARTS + d) * group : (i * PARTS + d + 1) * group
+                ].astype(BF16)
 
 
 def wait_all(copies):
@@ -160,35 +186,46 @@
         copy.wait()
 
 
-def own_body(place, x0, x1, wq, wk, wv, oq, ok, ov, bx, bw, bq, bk, bv, ins, outs):
+def own_body(place, x0, x1, wq, wk, wv, oq, ok, ov, oqw, okw, bx, bw, bq, bk, bv, bs, ins, outs):
     loads = [start(x, bx.at[i], ins.at[i]) for i, x in enumerate((x0, x1))]
     loads += [start(columns(w, place), bw.at[i], ins.at[2 + i]) for i, w in enumerate((wq, wk, wv))]
+    lanes = 2 * HEAD
     stores = []
-    for i, (kind, out, held) in enumerate((("q", oq, bq), ("k", ok, bk), ("v", ov, bv))):
+    for i, out in enumerate((oqw, okw)):
         loads[2 + i].wait()
+        bs[i, 0] = bw[i]
+        for p in range(bw.shape[2] // lanes):
+            at = slice(p * lanes, (p + 1) * lanes)
+            bs[i, 1, :, at] = pltpu.roll(bw[i, :, at].astype(F32), HEAD, 1).astype(BF16)
+        stores.append(start(bs.at[i], out, outs.at[3 + i]))
+    for load in loads[:2]:
+        load.wait()
+    for i, (out, held) in enumerate(((oq, bq), (ok, bk))):
         for half in range(2):
-            if i == 0:
-                loads[half].wait()
-            project(bx.at[half], half, bw.at[i], kind, held, place)
+            project_heads(bx.at[half], half, bs.at[i], held, place)
         stores.append(start(held, out, outs.at[i]))
+    loads[4].wait()
+    for half in range(2):
+        project(bx.at[half], half, bw.at[2], bv, place)
+    stores.append(start(bv, ov, outs.at[2]))
     wait_all(stores)
 
 
 def near_body(place, first, second, partner, wq, wk, qa, k1, k2):
-    project(first, 0, columns(wk, place), "k", k1, place)
-    project(second, 0, columns(wk, place), "k", k2, place)
-    project(partner, 0, columns(wq, place), "q", qa, place)
+    project_heads(first, 0, wk, k1, place)
+    project_heads(second, 0, wk, k2, place)
+    project_heads(partner, 0, wq, qa, place)
 
 
 def near_keys_body(place, a1, a2, first, second, wk, k1, k2):
     half = a1.shape[2]
     for a, x, k in ((a1, first, k1), (a2, second, k2)):
         k[:, :, :half] = a[...]
-        project(x, 1, columns(wk, place), "k", k, place)
+        project_heads(x, 1, wk, k, place)
 
 
 def near_logits_body(place, q0, qa, k0, k1, k2, partner, wq, qb, *outs):
-    project(partner, 0, columns(wq, place), "q", qb, place)
+    project_heads(partner, 0, wq, qb, place)
     write_logits([[q0], [qa, qb]], [k0, k1, k2], outs)
 
 
@@ -200,15 +237,22 @@
     *xs, weight = refs[: len(refs) * 2 // 3 + 1]
     for i, out in enumerate(refs[len(xs) + 1 :]):
         for half in range(2):
-            project(xs[2 * i + half], half, columns(weight, place), "v", out, place)
-
-
-def gather_body(place, *refs):
-    out, at = refs[-1], 0
-    for ref in refs[:-1]:
-        rows = ref.shape[1]
-        out[:, at : at + rows, :] = ref[...]
-        at += rows
+            project(xs[2 * i + half], half, columns(weight, place), out, place)
+
+
+def near_values_body(place, x0, x1, x2, x3, z_first, weight, both, second):
+    for half, x in enumerate((x0, x1)):
+        project(x, half, columns(weight, place), both.at[0], place)
+    for half, x in enumerate((x2, x3)):
+        project(x, half, columns(weight, place), second, place)
+    both[1] = z_first[...]
+
+
+def gather_body(place, own, both, second, far, z_own, z_second, out):
+    blocks = (own, both.at[0], second, far.at[0], z_own, both.at[1], z_second, far.at[1])
+    rows = own.shape[1]
+    for i, ref in enumerate(blocks):
+        out[:, i * rows : (i + 1) * rows, :] = ref[...]
 
 
 def add_body(count, place, *refs):
@@ -389,7 +433,10 @@
     )
 
     pairs, span, group = HEADS // 4, 4 * seqs * HEAD, rows // PARTS
-    q_shape, k_shape = (pairs, PARTS, 2, group, span), (pairs, rows, span)
+    heads, v_shape = 2 * pairs, (pairs, rows, span)
+    q_shape, k_shape = (heads, PARTS, group, span // 2), (heads, rows, span // 2)
+    qa_shape, ka_shape = (*q_shape[:-1], span // 4), (*k_shape[:-1], span // 4)
+    w_shape = (2, width, half)
     dma = pltpu.SemaphoreType.DMA
 
     def logits_shape(n):
@@ -400,21 +447,19 @@
 
     first, second = send_x(data, 0), send_x(data, 1)
     partner = shift(data, "z_lo", 1)
-    queries, keys, values = manual(
+    queries, keys, values, query_pair, key_pair = manual(
         own_body,
         place,
         [data, swap(data), query_matrix, key_matrix, value_matrix],
-        [jax.ShapeDtypeStruct(s, BF16) for s in (q_shape, k_shape, k_shape)],
-        [bf(2, *data.shape), bf(3, width, half), bf(*q_shape), bf(*k_shape), bf(*k_shape)]
-        + [dma((5,)), dma((3,))],
+        [jax.ShapeDtypeStruct(s, BF16) for s in (q_shape, k_shape, v_shape, w_shape, w_shape)],
+        [bf(2, *data.shape), bf(3, width, half), bf(*q_shape), bf(*k_shape), bf(*v_shape)]
+        + [bf(2, *w_shape), dma((5,)), dma((5,))],
         12 * seqs * rows * width * half,
         "own",
     )
     first, second, partner = (tie([a], queries)[0] for a in (first, second, partner))
     near = [(first, swap(second)), (second, swap(first))]
     partner2 = (partner, swap(partner))
-    qa_shape, ka_shape = (*q_shape[:-1], span // 2), (*k_shape[:-1], span // 2)
-
     def of(*shapes):
         return [jax.ShapeDtypeStruct(s, BF16) for s in shapes]
 
@@ -422,7 +467,7 @@
     qa, ka1, ka2 = local(
         near_body,
         place,
-        [first, second, partner, query_matrix, key_matrix],
+        [first, second, partner, query_pair, key_pair],
         of(qa_shape, ka_shape, ka_shape),
         3 * work // 2,
         "near",
@@ -430,7 +475,7 @@
     k1, k2 = local(
         near_keys_body,
         place,
-        [ka1, ka2, near[0][1], near[1][1], key_matrix],
+        [ka1, ka2, near[0][1], near[1][1], key_pair],
         of(k_shape, k_shape),
         work,
         "near_keys",
@@ -439,7 +484,7 @@
     qb, *near_logits = local(
         near_logits_body,
         place,
-        [queries, qa, keys, k1, k2, partner2[1], query_matrix],
+        [queries, qa, keys, k1, k2, partner2[1], query_pair],
         of(qa_shape) + [logits_shape(3)] * PARTS,
         2 * work,
         "near_logits",
@@ -448,7 +493,7 @@
         values_body,
         place,
         [*partner2, value_matrix],
-        of(k_shape),
+        of(v_shape),
         work,
         "values_partner",
         [qb],
@@ -469,29 +514,25 @@
 
     groups = [over_y(near_logits), over_y(far_logits)]
     sent = add_parts(place, groups)
-    first_values, second_values = local(
-        values_body,
-        place,
-        [*near[0], *near[1], value_matrix],
-        of(k_shape, k_shape),
+    both_values, second_values = local(
+        near_values_body,
+        place,
+        [*near[0], *near[1], z_first, value_matrix],
+        of((2, *v_shape), v_shape),
         2 * work,
         "values_near",
-        [far_logits[0]],
-    )
-
+        [sent],
+    )
     sent = sent.reshape(2 * PARTS, *sent.shape[2:])
     got = lax.all_to_all(sent, ("z_hi", "z_lo"), 0, 0, tiled=True)
     got = got.reshape(PARTS, 2, *got.shape[1:])
     all_rows = seqs * lax.axis_size(("z_hi", "y", "core"))
     scale = HEAD ** (-0.5) * all_rows ** (-0.5)
-    probs, z_first, z_second, first_values = softmax(
-        place, got, scale, [z_first, z_second, first_values]
-    )
-    z_far = send_x(z_first, 0)
-    far_values = send_x(first_values, 0)
+    probs, z_second, both_values = softmax(place, got, scale, [z_second, both_values])
+    far_values = send_x(both_values, 0)
     probs = order(place, [probs] + [shift(probs, "z_hi", d) for d in range(1, PARTS)])
     probs = probs.reshape(pairs, 2 * group, probs.shape[-1])
-    parts = [values, first_values, second_values, far_values, z_own, z_first, z_second, z_far]
+    parts = [values, both_values, second_values, far_values, z_own, z_second]
     (values,) = local(gather_body, place, parts, of((pairs, 8 * rows, span)), 0, "gather_values")
     probs = [probs] + [shift(probs, "y", d) for d in range(1, PARTS)]
     mine, theirs = mix(place, probs, values, seqs)

time: 123 us -> 122 us (level)
  waiting for transfers between devices: 48.5 us -> 45.1 us
  Pallas kernels: 24.8 us -> 26.3 us
    ppermute x18, waiting for transfers between devices: 34.7 us -> 32.3 us  [shift(): return lax.ppermute(arr, axis, [(i, (i + step) % n) for i in range(n)])]
    ppermute x18, starting transfers between devices: 25.1 us -> 26.9 us  [shift(): return lax.ppermute(arr, axis, [(i, (i + step) % n) for i in range(n)])]
    ppermute x7 -> x6, starting transfers between devices: 5.36 us -> 3.84 us  [send_x(): return lax.ppermute(arr, ('core', 'x'), ring_table(way))]
    ppermute x7 -> x6, waiting for transfers between devices: 7.51 us -> 6.18 us  [send_x(): return lax.ppermute(arr, ('core', 'x'), ring_table(way))]
    unnamed x42 -> x34, local copies, waits for them, and re-layouts: 11.4 us -> 11.4 us
  transfers between devices with their start and end apart: 26 -> 25, of which waited for: 16 -> 18; matrix products, arithmetic and copies ran while one was open for 0% -> 0% of each run, Pallas kernels for 16% -> 18%
where the time goes in v4:
time: 122 us; the launch traced here: 121 us
  waiting for transfers between devices  45.1 us (37%)
  starting transfers between devices  38 us (31%)
  Pallas kernels  26.3 us (22%)
  local copies, waits for them, and re-layouts  11.5 us (9%)
    ppermute x18, waiting for transfers between devices, shift(): return lax.ppermute(arr, axis, [(i, (i + step) % n) for i in range(n)])  32.3 us
    ppermute x18, starting transfers between devices, shift(): return lax.ppermute(arr, axis, [(i, (i + step) % n) for i in range(n)])  26.9 us
    pallas_call x9, Pallas kernels, local(): pl.pallas_call(run, out_shape=outs, in_specs=[pl.BlockSpec(memory_space=p...  17.9 us
    unnamed x34, local copies, waits for them, and re-layouts  11.4 us
    all_to_all x1, starting transfers between devices, per_device(): got = lax.all_to_all(sent, ('z_hi', 'z_lo'), 0, 0, tiled=True)  7.3 us
    all_to_all x1, waiting for transfers between devices, per_device(): got = lax.all_to_all(sent, ('z_hi', 'z_lo'), 0, 0, tiled=True)  6.62 us
    ppermute x6, waiting for transfers between devices, send_x(): return lax.ppermute(arr, ('core', 'x'), ring_table(way))  6.18 us
    pallas_call x1, Pallas kernels, manual(): pl.pallas_call(run, out_shape=outs, in_specs=[pl.BlockSpec(memory_space=p...  5.13 us
  transfers between devices with their start and end apart: 25, of which 18 were waited for; matrix products, arithmetic and copies ran while one was open for 0% of the time, Pallas kernels for 18%

profile of v4, /device:TPU:1, one launch (start us, length us, event | category | flops | bytes accessed | tf_op | source)
XLA Modules:
  0.0 121.2 jit_solution(8762443647479185340)
XLA Ops:
  0.0 3.2 %collective-permute-start = (bf16[4,128,768]{2,1,0:T(8,128)(2,1)}, bf16[4,128,768]{2,1,0:T(8,128)(2,1)S(1)}, u32[]{:S(2)}, u32[]{:S(2)}) collective-permute-start(bf16[4,128,768]{2,1,0:T(8,128)(2,1)} %refs_1_.1), channel_id=1, source_target_pairs={{0,8},{8,0},{1,9},{9,1},{2,10},{10,2},{3,11},{11,3},{4,12},{12,4},... | collective-permute-start | bytes 2359304 | tf_op jit(solution)/shard_map/ppermute | solution.py:23
  3.2 2.7 %collective-permute-start.1 = (bf16[4,128,768]{2,1,0:T(8,128)(2,1)}, bf16[4,128,768]{2,1,0:T(8,128)(2,1)S(1)}, u32[]{:S(2)}, u32[]{:S(2)}) collective-permute-start(bf16[4,128,768]{2,1,0:T(8,128)(2,1)} %refs_1_.1), channel_id=1, source_target_pairs={{0,2},{2,4},{4,6},{6,0},{8,14},{10,8},{12,10},{14,12},{1,3},{3,5},... | collective-permute-start | bytes 2359304 | tf_op jit(solution)/shard_map/ppermute | solution.py:417
  13.0 5.1 %own.1 = (bf16[6,4,32,512]{3,2,1,0:T(8,128)(2,1)S(1)}, bf16[6,128,512]{2,1,0:T(8,128)(2,1)S(1)}, bf16[3,128,1024]{2,1,0:T(8,128)(2,1)S(1)}, bf16[2,768,384]{2,1,0:T(8,128)(2,1)S(1)}, bf16[2,768,384]{2,1,0:T(8,128)(2,1)S(1)}) custom-call(s32[4]{0:T(128)S(1)} %pad_add_fusion.refs_0_.place, bf16[4,128,768]{2,1,0:T(8,128)(2,1)S(1)} %copy-done.13, ...), custom_call_target="tpu_custom_call" | custom-call | flops 1811939328 | bytes 9830400 | tf_op jit(solution)/shard_map/own/pallas_call | solution.py:78
  18.1 4.6 %collective-permute-done.2.refs_0_ = bf16[4,128,768]{2,1,0:T(8,128)(2,1)S(1)} collective-permute-done((bf16[4,128,768]{2,1,0:T(8,128)(2,1)}, bf16[4,128,768]{2,1,0:T(8,128)(2,1)S(1)}, u32[]{:S(2)}, u32[]{:S(2)}) %collective-permute-start.2) | collective-permute-done | bytes 786464 | tf_op jit(solution)/shard_map/ppermute | solution.py:417
  25.7 2.0 %near.1 = (bf16[6,4,32,256]{3,2,1,0:T(8,128)(2,1)S(1)}, bf16[6,128,256]{2,1,0:T(8,128)(2,1)S(1)}, bf16[6,128,256]{2,1,0:T(8,128)(2,1)S(1)}) custom-call(s32[4]{0:T(128)S(1)} %pad_add_fusion.refs_0_.place, bf16[4,128,768]{2,1,0:T(8,128)(2,1)S(1)} %tie.3.refs_1_, bf16[4,128,768]{2,1,0:T(8,128)(2,1)S(1)} %tie.4.refs_2_.refs_3_, ...), custom_call_target="tpu_custom_call" | custom-call | flops 905969664 | bytes 5898240 | tf_op jit(solution)/shard_map/near/pallas_call | solution.py:101
  27.7 1.6 %near_keys.1 = (bf16[6,128,512]{2,1,0:T(8,128)(2,1)S(1)}, bf16[6,128,512]{2,1,0:T(8,128)(2,1)S(1)}) custom-call(s32[4]{0:T(128)S(1)} %pad_add_fusion.refs_0_.place, bf16[6,128,256]{2,1,0:T(8,128)(2,1)S(1)} %get-tuple-element.36.refs_1_, bf16[6,128,256]{2,1,0:T(8,128)(2,1)S(1)} %get-tuple-element.37.refs_2_, ...), custom_call_target="tpu_custom_call" | custom-call | flops 603979776 | bytes 5111808 | tf_op jit(solution)/shard_map/near_keys/pallas_call | solution.py:101
  30.0 2.0 %near_logits.1 = (bf16[6,4,32,256]{3,2,1,0:T(8,128)(2,1)S(1)}, bf16[2,3,64,384]{3,2,1,0:T(8,128)(2,1)S(1)}, bf16[2,3,64,384]{3,2,1,0:T(8,128)(2,1)S(1)}, bf16[2,...) custom-call(s32[4]{0:T(128)S(1)} %pad_add_fusion.refs_0_.place, ...), custom_call_target="tpu_custom_call" | custom-call | flops 1207959552 | bytes 7077888 | tf_op jit(solution)/shard_map/near_logits/pallas_call | solution.py:101
  31.9 1.9 %collective-permute-start.7 = (bf16[2,192,384]{2,1,0:T(8,128)(2,1)S(1)}, bf16[2,192,384]{2,1,0:T(8,128)(2,1)S(1)}, u32[]{:S(2)}, u32[]{:S(2)}) collective-permute-start(bf16[2,192,384]{2,1,0:T(8,128)(2,1)S(1)} %bitcast.24), channel_id=1, source_target_pairs={{0,16},{16,32},{32,48},{48,0},{1,17},{17,33},{33,49},{49,1},{2,18}... | collective-permute-start | bytes 884744 | tf_op jit(solution)/shard_map/ppermute | solution.py:23
  33.8 2.6 %collective-permute-start.8 = (bf16[2,192,384]{2,1,0:T(8,128)(2,1)S(1)}, bf16[2,192,384]{2,1,0:T(8,128)(2,1)S(1)}, u32[]{:S(2)}, u32[]{:S(2)}) collective-permute-start(bf16[2,192,384]{2,1,0:T(8,128)(2,1)S(1)} %bitcast.23), channel_id=1, source_target_pairs={{0,32},{16,48},{32,0},{48,16},{1,33},{17,49},{33,1},{49,17},{2,34}... | collective-permute-start | bytes 884744 | tf_op jit(solution)/shard_map/ppermute | solution.py:23
  37.5 1.5 %values_partner.1.refs_5_ = bf16[3,128,1024]{2,1,0:T(8,128)(2,1)S(1)} custom-call(s32[4]{0:T(128)S(1)} %pad_add_fusion.refs_0_.place, bf16[4,128,768]{2,1,0:T(8,128)(2,1)S(1)} %tie.5.refs_3_.refs_1_, bf16[4,128,768]{2,1,0:T(8,128)(2,1)S(1)} %collective-permute-done.6.refs_6_.refs_2_, bf16[768,768]{1,0:T(8,128)(2,1)S(1)} %copy-done.1, ...), custom_call_target="tpu_custom_call" | custom-call | flops 603979776 | bytes 3538944 | tf_op jit(solution)/shard_map/values_partner/pallas_call | solution.py:101
  39.1 1.6 %collective-permute-done.10.refs_4_ = bf16[6,128,512]{2,1,0:T(8,128)(2,1)S(1)} collective-permute-done((bf16[6,128,512]{2,1,0:T(8,128)(2,1)S(1)}, bf16[6,128,512]{2,1,0:T(8,128)(2,1)S(1)}, u32[]{:S(2)}, u32[]{:S(2)}) %collective-permute-start.10) | collective-permute-done | bytes 786464 | tf_op jit(solution)/shard_map/ppermute | solution.py:417
  42.0 1.6 %collective-permute-done.7.refs_2_ = bf16[2,192,384]{2,1,0:T(8,128)(2,1)S(1)} collective-permute-done((bf16[2,192,384]{2,1,0:T(8,128)(2,1)S(1)}, bf16[2,192,384]{2,1,0:T(8,128)(2,1)S(1)}, u32[]{:S(2)}, u32[]{:S(2)}) %collective-permute-start.7) | collective-permute-done | bytes 294944 | tf_op jit(solution)/shard_map/ppermute | solution.py:23
  43.7 5.4 %collective-permute-start.12 = (bf16[2,192,128]{2,1,0:T(8,128)(2,1)S(1)}, bf16[2,192,128]{2,1,0:T(8,128)(2,1)S(1)}, u32[]{:S(2)}, u32[]{:S(2)}) collective-permute-start(bf16[2,192,128]{2,1,0:T(8,128)(2,1)S(1)} %bitcast.26), channel_id=1, source_target_pairs={{0,32},{16,48},{32,0},{48,16},{1,33},{17,49},{33,1},{49,17},{2,34}... | collective-permute-start | bytes 294920 | tf_op jit(solution)/shard_map/ppermute | solution.py:23
  51.4 1.5 %collective-permute-done.12.refs_7_ = bf16[2,192,128]{2,1,0:T(8,128)(2,1)S(1)} collective-permute-done((bf16[2,192,128]{2,1,0:T(8,128)(2,1)S(1)}, bf16[2,192,128]{2,1,0:T(8,128)(2,1)S(1)}, u32[]{:S(2)}, u32[]{:S(2)}) %collective-permute-start.12) | collective-permute-done | bytes 98336 | tf_op jit(solution)/shard_map/ppermute | solution.py:23
  53.9 1.5 %add_over_y.1.refs_7_ = bf16[4,2,48,512]{3,2,1,0:T(8,128)(2,1)} custom-call(s32[4]{0:T(128)S(1)} %pad_add_fusion.refs_0_.place, bf16[2,192,384]{2,1,0:T(8,128)(2,1)S(1)} %bitcast.20, bf16[2,192,384]{2,1,0:T(8,128)(2,1)S(1)} %collective-permute-done.7.refs_2_, bf16[2,192,384]{2,1,0:T(8,128)(2,1)S(1)} %collective-permute-done.8.refs_3_, ...), custom_call_target="tpu_custom_call" | custom-call | flops 786432 | bytes 1966080 | tf_op jit(solution)/shard_map/add_over_y/pallas_call | solution.py:101
  55.4 7.3 %all-to-all-start = ((bf16[8,48,512]{2,1,0:T(8,128)(2,1)}), bf16[8,48,512]{2,1,0:T(8,128)(2,1)S(1)}, u32[]{:S(2)}, u32[]{:S(2)}) async-start(bf16[8,48,512]{2,1,0:T(8,128)(2,1)} %bitcast.12), calls=%async_computation | async-start | bytes 786432 | tf_op jit(solution)/shard_map/all_to_all | solution.py:527
  66.2 4.1 %values_near.1 = (bf16[2,3,128,1024]{3,2,1,0:T(8,128)(2,1)}, bf16[3,128,1024]{2,1,0:T(8,128)(2,1)S(1)}) custom-call(s32[4]{0:T(128)S(1)} %pad_add_fusion.refs_0_.place, bf16[4,128,768]{2,1,0:T(8,128)(2,1)S(1)} %tie.3.refs_1_, bf16[4,128,768]{2,1,0:T(8,128)(2,1)S(1)} %copy-done.4, bf16[4,128,768]{2,1,0:T(8,128)(2,1)S(1)} %tie.4.refs_2_.refs_3_, ...), custom_call_target="tpu_custom_call" | custom-call | flops 1207959552 | bytes 7471104 | tf_op jit(solution)/shard_map/values_near/pallas_call | solution.py:101
  71.3 6.6 %all-to-all-done = bf16[8,48,512]{2,1,0:T(8,128)(2,1)S(1)} async-done(((bf16[8,48,512]{2,1,0:T(8,128)(2,1)}), bf16[8,48,512]{2,1,0:T(8,128)(2,1)S(1)}, u32[]{:S(2)}, u32[]{:S(2)}) %all-to-all-start) | async-done | bytes 393248 | tf_op jit(solution)/shard_map/all_to_all | solution.py:527
  78.8 2.1 %collective-permute-start.17 = (bf16[48,1024]{1,0:T(8,128)(2,1)S(1)}, bf16[48,1024]{1,0:T(8,128)(2,1)S(1)}, u32[]{:S(2)}, u32[]{:S(2)}) collective-permute-start(bf16[48,1024]{1,0:T(8,128)(2,1)S(1)} %get-tuple-element.50.refs_1_), channel_id=1, source_target_pairs={{0,128},{64,192},{128,0},{192,64},{1,129},{65,193},{129,1},{193,65... | collective-permute-start | bytes 294920 | tf_op jit(solution)/shard_map/ppermute | solution.py:23
  80.9 1.5 %collective-permute-start.18 = (bf16[48,1024]{1,0:T(8,128)(2,1)S(1)}, bf16[48,1024]{1,0:T(8,128)(2,1)S(1)}, u32[]{:S(2)}, u32[]{:S(2)}) collective-permute-start(bf16[48,1024]{1,0:T(8,128)(2,1)S(1)} %get-tuple-element.50.refs_1_), channel_id=1, source_target_pairs={{0,192},{64,0},{128,64},{192,128},{1,193},{65,1},{129,65},{193,129... | collective-permute-start | bytes 294920 | tf_op jit(solution)/shard_map/ppermute | solution.py:23
  82.4 3.1 %collective-permute-done.16.refs_2_ = bf16[48,1024]{1,0:T(8,128)(2,1)S(1)} collective-permute-done((bf16[48,1024]{1,0:T(8,128)(2,1)S(1)}, bf16[48,1024]{1,0:T(8,128)(2,1)S(1)}, u32[]{:S(2)}, u32[]{:S(2)}) %collective-permute-start.16) | collective-permute-done | bytes 98336 | tf_op jit(solution)/shard_map/ppermute | solution.py:23
  85.5 2.7 %collective-permute-done.17.refs_3_ = bf16[48,1024]{1,0:T(8,128)(2,1)S(1)} collective-permute-done((bf16[48,1024]{1,0:T(8,128)(2,1)S(1)}, bf16[48,1024]{1,0:T(8,128)(2,1)S(1)}, u32[]{:S(2)}, u32[]{:S(2)}) %collective-permute-start.17) | collective-permute-done | bytes 98336 | tf_op jit(solution)/shard_map/ppermute | solution.py:23
  88.2 4.9 %collective-permute-done.18.refs_4_ = bf16[48,1024]{1,0:T(8,128)(2,1)S(1)} collective-permute-done((bf16[48,1024]{1,0:T(8,128)(2,1)S(1)}, bf16[48,1024]{1,0:T(8,128)(2,1)S(1)}, u32[]{:S(2)}, u32[]{:S(2)}) %collective-permute-start.18) | collective-permute-done | bytes 98336 | tf_op jit(solution)/shard_map/ppermute | solution.py:23
  93.6 1.5 %collective-permute-start.19 = (bf16[3,64,1024]{2,1,0:T(8,128)(2,1)S(1)}, bf16[3,64,1024]{2,1,0:T(8,128)(2,1)S(1)}, u32[]{:S(2)}, u32[]{:S(2)}) collective-permute-start(bf16[3,64,1024]{2,1,0:T(8,128)(2,1)S(1)} %bitcast.15), channel_id=1, source_target_pairs={{0,16},{16,32},{32,48},{48,0},{1,17},{17,33},{33,49},{49,1},{2,18}... | collective-permute-start | bytes 1179656 | tf_op jit(solution)/shard_map/ppermute | solution.py:23
  95.1 1.4 %collective-permute-start.20 = (bf16[3,64,1024]{2,1,0:T(8,128)(2,1)S(1)}, bf16[3,64,1024]{2,1,0:T(8,128)(2,1)S(1)}, u32[]{:S(2)}, u32[]{:S(2)}) collective-permute-start(bf16[3,64,1024]{2,1,0:T(8,128)(2,1)S(1)} %bitcast.16), channel_id=1, source_target_pairs={{0,32},{16,48},{32,0},{48,16},{1,33},{17,49},{33,1},{49,17},{2,34}... | collective-permute-start | bytes 1179656 | tf_op jit(solution)/shard_map/ppermute | solution.py:23
  96.5 2.0 %collective-permute-start.21 = (bf16[3,64,1024]{2,1,0:T(8,128)(2,1)S(1)}, bf16[3,64,1024]{2,1,0:T(8,128)(2,1)S(1)}, u32[]{:S(2)}, u32[]{:S(2)}) collective-permute-start(bf16[3,64,1024]{2,1,0:T(8,128)(2,1)S(1)} %bitcast.17), channel_id=1, source_target_pairs={{0,48},{16,0},{32,16},{48,32},{1,49},{17,1},{33,17},{49,33},{2,50}... | collective-permute-start | bytes 1179656 | tf_op jit(solution)/shard_map/ppermute | solution.py:23
  98.5 1.8 %gather_values.1.refs_5_ = bf16[3,1024,1024]{2,1,0:T(8,128)(2,1)S(1)} custom-call(s32[4]{0:T(128)S(1)} %pad_add_fusion.refs_0_.place, bf16[3,128,1024]{2,1,0:T(8,128)(2,1)S(1)} %copy-done.8, bf16[2,3,128,1024]{3,2,1,0:T(8,128)(2,1)} %get-tuple-element.52.refs_2_, bf16[3,128,1024]{2,1,0:T(8,128)(2,1)S(1)} %copy-done.10, ...), custom_call_target="tpu_custom_call" | custom-call | bytes 12582912 | tf_op jit(solution)/shard_map/gather_values/pallas_call | solution.py:101
  100.4 4.8 %collective-permute-done.19.refs_2_ = bf16[3,64,1024]{2,1,0:T(8,128)(2,1)S(1)} collective-permute-done((bf16[3,64,1024]{2,1,0:T(8,128)(2,1)S(1)}, bf16[3,64,1024]{2,1,0:T(8,128)(2,1)S(1)}, u32[]{:S(2)}, u32[]{:S(2)}) %collective-permute-start.19) | collective-permute-done | bytes 393248 | tf_op jit(solution)/shard_map/ppermute | solution.py:23
  105.1 8.7 %collective-permute-done.20.refs_3_ = bf16[3,64,1024]{2,1,0:T(8,128)(2,1)S(1)} collective-permute-done((bf16[3,64,1024]{2,1,0:T(8,128)(2,1)S(1)}, bf16[3,64,1024]{2,1,0:T(8,128)(2,1)S(1)}, u32[]{:S(2)}, u32[]{:S(2)}) %collective-permute-start.20) | collective-permute-done | bytes 393248 | tf_op jit(solution)/shard_map/ppermute | solution.py:23
  114.0 2.4 %mix.1 = (bf16[4,128,384]{2,1,0:T(8,128)(2,1)S(1)}, bf16[4,128,384]{2,1,0:T(8,128)(2,1)S(1)}) custom-call(s32[4]{0:T(128)S(1)} %pad_add_fusion.refs_0_.place, bf16[3,64,1024]{2,1,0:T(8,128)(2,1)S(1)} %bitcast.18, bf16[3,64,1024]{2,1,0:T(8,128)(2,1)S(1)} %collective-permute-done.19.refs_2_, bf16[3,64,1024]{2,1,0:T(8,128)(2,1)S(1)} %collective-permute-done.20.refs_3_, ...), custom_call_target="tpu_custom_call" | custom-call | flops 1610612736 | bytes 8650752 | tf_op jit(solution)/shard_map/mix/pallas_call | solution.py:101
  116.3 1.6 %collective-permute-start.23 = (bf16[4,128,384]{2,1,0:T(8,128)(2,1)S(1)}, bf16[4,128,384]{2,1,0:T(8,128)(2,1)S(1)}, u32[]{:S(2)}, u32[]{:S(2)}) collective-permute-start(bf16[4,128,384]{2,1,0:T(8,128)(2,1)S(1)} %get-tuple-element.56), channel_id=1, source_target_pairs={{0,8},{8,0},{1,9},{9,1},{2,10},{10,2},{3,11},{11,3},{4,12},{12,4},... | collective-permute-start | bytes 1179656 | tf_op jit(solution)/shard_map/ppermute | solution.py:23
  119.3 1.9 %finish.1 = bf16[4,128,768]{2,1,0:T(8,128)(2,1)} custom-call(bf16[4,128,384]{2,1,0:T(8,128)(2,1)S(1)} %get-tuple-element.55.mine, bf16[4,128,384]{2,1,0:T(8,128)(2,1)S(1)} %collective-permute-done.23.theirs, bf16[384,768]{1,0:T(8,128)(2,1)S(1)} %get-tuple-element.58.weight_mine, bf16[384,768]{1,0:T(8,128)(2,1)S(1)} %get-tuple-element.57.weight_theirs), custom_call_target="tpu_custom_call" | custom-call | flops 603979776 | bytes 2752512 | tf_op jit(solution)/shard_map/finish/pallas_call | solution.py:391
  (70 shorter events, 24.0 us)
Async XLA Ops:
  0.0 6.0 %collective-permute-start = (bf16[4,128,768]{2,1,0:T(8,128)(2,1)}, bf16[4,128,768]{2,1,0:T(8,128)(2,1)S(1)}, u32[]{:S(2)}, u32[]{:S(2)}) collective-permute-start(bf16[4,128,768]{2,1,0:T(8,128)(2,1)} %refs_1_.1), channel_id=1, source_target_pairs={{0,8},{8,0},{1,9},{9,1},{2,10},{10,2},{3,11},{11,3},{4,12},{12,4},... | collective-permute-start | bytes 2359304 | tf_op jit(solution)/shard_map/ppermute | solution.py:23
  3.2 19.4 %collective-permute-start.2 = (bf16[4,128,768]{2,1,0:T(8,128)(2,1)}, bf16[4,128,768]{2,1,0:T(8,128)(2,1)S(1)}, u32[]{:S(2)}, u32[]{:S(2)}) collective-permute-start(bf16[4,128,768]{2,1,0:T(8,128)(2,1)} %refs_1_.1), channel_id=1, source_target_pairs={{0,6},{2,0},{4,2},{6,4},{8,10},{10,12},{12,14},{14,8},{1,7},{3,1},... | collective-permute-start | bytes 2359304 | tf_op jit(solution)/shard_map/ppermute | solution.py:417
  3.2 20.2 %collective-permute-start.1 = (bf16[4,128,768]{2,1,0:T(8,128)(2,1)}, bf16[4,128,768]{2,1,0:T(8,128)(2,1)S(1)}, u32[]{:S(2)}, u32[]{:S(2)}) collective-permute-start(bf16[4,128,768]{2,1,0:T(8,128)(2,1)} %refs_1_.1), channel_id=1, source_target_pairs={{0,2},{2,4},{4,6},{6,0},{8,14},{10,8},{12,10},{14,12},{1,3},{3,5},... | collective-permute-start | bytes 2359304 | tf_op jit(solution)/shard_map/ppermute | solution.py:417
  5.9 19.4 %collective-permute-start.3 = (bf16[4,128,768]{2,1,0:T(8,128)(2,1)}, bf16[4,128,768]{2,1,0:T(8,128)(2,1)S(1)}, u32[]{:S(2)}, u32[]{:S(2)}) collective-permute-start(bf16[4,128,768]{2,1,0:T(8,128)(2,1)} %refs_1_.1), channel_id=1, source_target_pairs={{0,1},{1,0},{2,3},{3,2},{4,5},{5,4},{6,7},{7,6},{8,9},{9,8},{10,11... | collective-permute-start | bytes 2359304 | tf_op jit(solution)/shard_map/ppermute | solution.py:23
  18.1 4.6 %copy-start.7 = (bf16[3,128,1024]{2,1,0:T(8,128)(2,1)}, bf16[3,128,1024]{2,1,0:T(8,128)(2,1)S(1)}, u32[]{:S(2)}) copy-start(bf16[3,128,1024]{2,1,0:T(8,128)(2,1)S(1)} %get-tuple-element.51.refs_1_) | copy-start | bytes 2359300
  22.7 5.0 %collective-permute-start.4 = (bf16[4,128,768]{2,1,0:T(8,128)(2,1)S(1)}, bf16[4,128,768]{2,1,0:T(8,128)(2,1)S(1)}, u32[]{:S(2)}, u32[]{:S(2)}) collective-permute-start(bf16[4,128,768]{2,1,0:T(8,128)(2,1)S(1)} %tie.4.refs_2_.refs_3_), channel_id=1, source_target_pairs={{0,8},{8,0},{1,9},{9,1},{2,10},{10,2},{3,11},{11,3},{4,12},{12,4},... | collective-permute-start | bytes 2359304 | tf_op jit(solution)/shard_map/ppermute | solution.py:23
  23.4 4.3 %collective-permute-start.5 = (bf16[4,128,768]{2,1,0:T(8,128)(2,1)S(1)}, bf16[4,128,768]{2,1,0:T(8,128)(2,1)S(1)}, u32[]{:S(2)}, u32[]{:S(2)}) collective-permute-start(bf16[4,128,768]{2,1,0:T(8,128)(2,1)S(1)} %tie.3.refs_1_), channel_id=1, source_target_pairs={{0,8},{8,0},{1,9},{9,1},{2,10},{10,2},{3,11},{11,3},{4,12},{12,4},... | collective-permute-start | bytes 2359304 | tf_op jit(solution)/shard_map/ppermute | solution.py:23
  25.3 4.6 %collective-permute-start.6 = (bf16[4,128,768]{2,1,0:T(8,128)(2,1)S(1)}, bf16[4,128,768]{2,1,0:T(8,128)(2,1)S(1)}, u32[]{:S(2)}, u32[]{:S(2)}) collective-permute-start(bf16[4,128,768]{2,1,0:T(8,128)(2,1)S(1)} %tie.5.refs_3_.refs_1_), channel_id=1, source_target_pairs={{0,8},{8,0},{1,9},{9,1},{2,10},{10,2},{3,11},{11,3},{4,12},{12,4},... | collective-permute-start | bytes 2359304 | tf_op jit(solution)/shard_map/ppermute | solution.py:23
  27.7 1.6 %copy-start.3 = (bf16[4,128,768]{2,1,0:T(8,128)(2,1)}, bf16[4,128,768]{2,1,0:T(8,128)(2,1)S(1)}, u32[]{:S(2)}) copy-start(bf16[4,128,768]{2,1,0:T(8,128)(2,1)S(1)} %collective-permute-done.4.refs_3_.refs_2_) | copy-start | bytes 2359300
  27.7 1.6 %copy-start.5 = (bf16[4,128,768]{2,1,0:T(8,128)(2,1)}, bf16[4,128,768]{2,1,0:T(8,128)(2,1)S(1)}, u32[]{:S(2)}) copy-start(bf16[4,128,768]{2,1,0:T(8,128)(2,1)S(1)} %collective-permute-done.5.refs_4_) | copy-start | bytes 2359300
  29.3 11.4 %collective-permute-start.10 = (bf16[6,128,512]{2,1,0:T(8,128)(2,1)S(1)}, bf16[6,128,512]{2,1,0:T(8,128)(2,1)S(1)}, u32[]{:S(2)}, u32[]{:S(2)}) collective-permute-start(bf16[6,128,512]{2,1,0:T(8,128)(2,1)S(1)} %get-tuple-element.38.refs_4_), channel_id=1, source_target_pairs={{0,2},{2,4},{4,6},{6,0},{8,14},{10,8},{12,10},{14,12},{1,3},{3,5},... | collective-permute-start | bytes 2359304 | tf_op jit(solution)/shard_map/ppermute | solution.py:417
  30.0 7.5 %copy-start.1 = (bf16[768,768]{1,0:T(8,128)(2,1)S(1)}, bf16[768,768]{1,0:T(8,128)(2,1)}, u32[]{:S(2)}) copy-start(bf16[768,768]{1,0:T(8,128)(2,1)} %refs_6_.1) | copy-start | bytes 3538948
  31.9 11.7 %collective-permute-start.7 = (bf16[2,192,384]{2,1,0:T(8,128)(2,1)S(1)}, bf16[2,192,384]{2,1,0:T(8,128)(2,1)S(1)}, u32[]{:S(2)}, u32[]{:S(2)}) collective-permute-start(bf16[2,192,384]{2,1,0:T(8,128)(2,1)S(1)} %bitcast.24), channel_id=1, source_target_pairs={{0,16},{16,32},{32,48},{48,0},{1,17},{17,33},{33,49},{49,1},{2,18}... | collective-permute-start | bytes 884744 | tf_op jit(solution)/shard_map/ppermute | solution.py:23
  33.8 15.5 %collective-permute-start.8 = (bf16[2,192,384]{2,1,0:T(8,128)(2,1)S(1)}, bf16[2,192,384]{2,1,0:T(8,128)(2,1)S(1)}, u32[]{:S(2)}, u32[]{:S(2)}) collective-permute-start(bf16[2,192,384]{2,1,0:T(8,128)(2,1)S(1)} %bitcast.23), channel_id=1, source_target_pairs={{0,32},{16,48},{32,0},{48,16},{1,33},{17,49},{33,1},{49,17},{2,34}... | collective-permute-start | bytes 884744 | tf_op jit(solution)/shard_map/ppermute | solution.py:23
  36.4 13.5 %collective-permute-start.9 = (bf16[2,192,384]{2,1,0:T(8,128)(2,1)S(1)}, bf16[2,192,384]{2,1,0:T(8,128)(2,1)S(1)}, u32[]{:S(2)}, u32[]{:S(2)}) collective-permute-start(bf16[2,192,384]{2,1,0:T(8,128)(2,1)S(1)} %bitcast.22), channel_id=1, source_target_pairs={{0,48},{16,0},{32,16},{48,32},{1,49},{17,1},{33,17},{49,33},{2,50}... | collective-permute-start | bytes 884744 | tf_op jit(solution)/shard_map/ppermute | solution.py:23
  39.0 23.7 %collective-permute-start.15 = (bf16[3,128,1024]{2,1,0:T(8,128)(2,1)S(1)}, bf16[3,128,1024]{2,1,0:T(8,128)(2,1)}, u32[]{:S(2)}, u32[]{:S(2)}) collective-permute-start(bf16[3,128,1024]{2,1,0:T(8,128)(2,1)S(1)} %values_partner.1.refs_5_), channel_id=1, source_target_pairs={{0,2},{2,4},{4,6},{6,0},{8,14},{10,8},{12,10},{14,12},{1,3},{3,5},... | collective-permute-start | bytes 2359304 | tf_op jit(solution)/shard_map/ppermute | solution.py:417
  41.8 9.6 %collective-permute-start.11 = (bf16[2,192,128]{2,1,0:T(8,128)(2,1)S(1)}, bf16[2,192,128]{2,1,0:T(8,128)(2,1)S(1)}, u32[]{:S(2)}, u32[]{:S(2)}) collective-permute-start(bf16[2,192,128]{2,1,0:T(8,128)(2,1)S(1)} %bitcast.27), channel_id=1, source_target_pairs={{0,16},{16,32},{32,48},{48,0},{1,17},{17,33},{33,49},{49,1},{2,18}... | collective-permute-start | bytes 294920 | tf_op jit(solution)/shard_map/ppermute | solution.py:23
  43.7 9.3 %collective-permute-start.12 = (bf16[2,192,128]{2,1,0:T(8,128)(2,1)S(1)}, bf16[2,192,128]{2,1,0:T(8,128)(2,1)S(1)}, u32[]{:S(2)}, u32[]{:S(2)}) collective-permute-start(bf16[2,192,128]{2,1,0:T(8,128)(2,1)S(1)} %bitcast.26), channel_id=1, source_target_pairs={{0,32},{16,48},{32,0},{48,16},{1,33},{17,49},{33,1},{49,17},{2,34}... | collective-permute-start | bytes 294920 | tf_op jit(solution)/shard_map/ppermute | solution.py:23
  49.3 4.6 %collective-permute-start.13 = (bf16[2,192,128]{2,1,0:T(8,128)(2,1)S(1)}, bf16[2,192,128]{2,1,0:T(8,128)(2,1)S(1)}, u32[]{:S(2)}, u32[]{:S(2)}) collective-permute-start(bf16[2,192,128]{2,1,0:T(8,128)(2,1)S(1)} %bitcast.25), channel_id=1, source_target_pairs={{0,48},{16,0},{32,16},{48,32},{1,49},{17,1},{33,17},{49,33},{2,50}... | collective-permute-start | bytes 294920 | tf_op jit(solution)/shard_map/ppermute | solution.py:23
  49.9 21.3 %collective-permute-start.14 = (bf16[3,128,1024]{2,1,0:T(8,128)(2,1)S(1)}, bf16[3,128,1024]{2,1,0:T(8,128)(2,1)S(1)}, u32[]{:S(2)}, u32[]{:S(2)}) collective-permute-start(bf16[3,128,1024]{2,1,0:T(8,128)(2,1)S(1)} %values_partner.1.refs_5_), channel_id=1, source_target_pairs={{0,6},{2,0},{4,2},{6,4},{8,10},{10,12},{12,14},{14,8},{1,7},{3,1},... | collective-permute-start | bytes 2359304 | tf_op jit(solution)/shard_map/ppermute | solution.py:417
  55.4 22.5 %all-to-all-start = ((bf16[8,48,512]{2,1,0:T(8,128)(2,1)}), bf16[8,48,512]{2,1,0:T(8,128)(2,1)S(1)}, u32[]{:S(2)}, u32[]{:S(2)}) async-start(bf16[8,48,512]{2,1,0:T(8,128)(2,1)} %bitcast.12), calls=%async_computation | async-start | bytes 786432 | tf_op jit(solution)/shard_map/all_to_all | solution.py:527
  77.9 20.6 %copy-start.8 = (bf16[3,128,1024]{2,1,0:T(8,128)(2,1)S(1)}, bf16[3,128,1024]{2,1,0:T(8,128)(2,1)}, u32[]{:S(2)}) copy-start(bf16[3,128,1024]{2,1,0:T(8,128)(2,1)} %copy-done.7) | copy-start | bytes 2359300
  77.9 20.6 %copy-start.10 = (bf16[3,128,1024]{2,1,0:T(8,128)(2,1)S(1)}, bf16[3,128,1024]{2,1,0:T(8,128)(2,1)}, u32[]{:S(2)}) copy-start(bf16[3,128,1024]{2,1,0:T(8,128)(2,1)} %copy-done.9) | copy-start | bytes 2359300
  78.7 19.8 %collective-permute-start.22 = (bf16[2,3,128,1024]{3,2,1,0:T(8,128)(2,1)}, bf16[2,3,128,1024]{3,2,1,0:T(8,128)(2,1)S(1)}, u32[]{:S(2)}, u32[]{:S(2)}) collective-permute-start(bf16[2,3,128,1024]{3,2,1,0:T(8,128)(2,1)} %get-tuple-element.52.refs_2_), channel_id=1, source_target_pairs={{0,2},{2,4},{4,6},{6,0},{8,14},{10,8},{12,10},{14,12},{1,3},{3,5},... | collective-permute-start | bytes 4718600 | tf_op jit(solution)/shard_map/ppermute | solution.py:417
  78.8 6.7 %collective-permute-start.16 = (bf16[48,1024]{1,0:T(8,128)(2,1)S(1)}, bf16[48,1024]{1,0:T(8,128)(2,1)S(1)}, u32[]{:S(2)}, u32[]{:S(2)}) collective-permute-start(bf16[48,1024]{1,0:T(8,128)(2,1)S(1)} %get-tuple-element.50.refs_1_), channel_id=1, source_target_pairs={{0,64},{64,128},{128,192},{192,0},{1,65},{65,129},{129,193},{193,1... | collective-permute-start | bytes 294920 | tf_op jit(solution)/shard_map/ppermute | solution.py:23
  78.8 9.4 %collective-permute-start.17 = (bf16[48,1024]{1,0:T(8,128)(2,1)S(1)}, bf16[48,1024]{1,0:T(8,128)(2,1)S(1)}, u32[]{:S(2)}, u32[]{:S(2)}) collective-permute-start(bf16[48,1024]{1,0:T(8,128)(2,1)S(1)} %get-tuple-element.50.refs_1_), channel_id=1, source_target_pairs={{0,128},{64,192},{128,0},{192,64},{1,129},{65,193},{129,1},{193,65... | collective-permute-start | bytes 294920 | tf_op jit(solution)/shard_map/ppermute | solution.py:23
  80.9 12.1 %collective-permute-start.18 = (bf16[48,1024]{1,0:T(8,128)(2,1)S(1)}, bf16[48,1024]{1,0:T(8,128)(2,1)S(1)}, u32[]{:S(2)}, u32[]{:S(2)}) collective-permute-start(bf16[48,1024]{1,0:T(8,128)(2,1)S(1)} %get-tuple-element.50.refs_1_), channel_id=1, source_target_pairs={{0,192},{64,0},{128,64},{192,128},{1,193},{65,1},{129,65},{193,129... | collective-permute-start | bytes 294920 | tf_op jit(solution)/shard_map/ppermute | solution.py:23
  93.6 11.5 %collective-permute-start.19 = (bf16[3,64,1024]{2,1,0:T(8,128)(2,1)S(1)}, bf16[3,64,1024]{2,1,0:T(8,128)(2,1)S(1)}, u32[]{:S(2)}, u32[]{:S(2)}) collective-permute-start(bf16[3,64,1024]{2,1,0:T(8,128)(2,1)S(1)} %bitcast.15), channel_id=1, source_target_pairs={{0,16},{16,32},{32,48},{48,0},{1,17},{17,33},{33,49},{49,1},{2,18}... | collective-permute-start | bytes 1179656 | tf_op jit(solution)/shard_map/ppermute | solution.py:23
  95.1 18.8 %collective-permute-start.20 = (bf16[3,64,1024]{2,1,0:T(8,128)(2,1)S(1)}, bf16[3,64,1024]{2,1,0:T(8,128)(2,1)S(1)}, u32[]{:S(2)}, u32[]{:S(2)}) collective-permute-start(bf16[3,64,1024]{2,1,0:T(8,128)(2,1)S(1)} %bitcast.16), channel_id=1, source_target_pairs={{0,32},{16,48},{32,0},{48,16},{1,33},{17,49},{33,1},{49,17},{2,34}... | collective-permute-start | bytes 1179656 | tf_op jit(solution)/shard_map/ppermute | solution.py:23
  96.5 17.5 %collective-permute-start.21 = (bf16[3,64,1024]{2,1,0:T(8,128)(2,1)S(1)}, bf16[3,64,1024]{2,1,0:T(8,128)(2,1)S(1)}, u32[]{:S(2)}, u32[]{:S(2)}) collective-permute-start(bf16[3,64,1024]{2,1,0:T(8,128)(2,1)S(1)} %bitcast.17), channel_id=1, source_target_pairs={{0,48},{16,0},{32,16},{48,32},{1,49},{17,1},{33,17},{49,33},{2,50}... | collective-permute-start | bytes 1179656 | tf_op jit(solution)/shard_map/ppermute | solution.py:23
  100.3 17.6 %copy-start.16 = (bf16[768,768]{1,0:T(8,128)(2,1)S(1)}, bf16[768,768]{1,0:T(8,128)(2,1)}, u32[]{:S(2)}) copy-start(bf16[768,768]{1,0:T(8,128)(2,1)} %param.9) | copy-start | bytes 3538948
  116.3 3.0 %collective-permute-start.23 = (bf16[4,128,384]{2,1,0:T(8,128)(2,1)S(1)}, bf16[4,128,384]{2,1,0:T(8,128)(2,1)S(1)}, u32[]{:S(2)}, u32[]{:S(2)}) collective-permute-start(bf16[4,128,384]{2,1,0:T(8,128)(2,1)S(1)} %get-tuple-element.56), channel_id=1, source_target_pairs={{0,8},{8,0},{1,9},{9,1},{2,10},{10,2},{3,11},{11,3},{4,12},{12,4},... | collective-permute-start | bytes 1179656 | tf_op jit(solution)/shard_map/ppermute | solution.py:23
  (10 other events, 11.4 us)

commit v5 on v4

--- a/solution.py
+++ b/solution.py
@@ -417,6 +417,13 @@
     return lax.ppermute(arr, ("core", "x"), ring_table(way))
 
 
+def send_y(arr, way):
+    table = [
+        (i * 2 + c, (i + (1 if c == way else -1)) % PARTS * 2 + c) for i in range(PARTS) for c in range(2)
+    ]
+    return lax.ppermute(arr, ("y", "core"), table)
+
+
 def per_device(data, query_matrix, key_matrix, value_matrix, output_matrix):
     seqs, rows, width = data.shape
     place = jnp.stack([lax.axis_index(a) for a in ("core", "y", "z_hi", "z_lo")])
@@ -498,7 +505,6 @@
         "values_partner",
         [qb],
     )
-    z_first, z_second = send_x(z_own, 0), send_x(z_own, 1)
     far_logits = local(
         far_logits_body,
         place,
@@ -508,11 +514,19 @@
         "far_logits",
         [z_own],
     )
-    def over_y(parts):
+    (z_own,) = tie([z_own], far_logits[0])
+    z_first, z_second = send_x(z_own, 0), send_x(z_own, 1)
+
+    def over_y(parts, split):
         parts = [a.reshape(2, -1, a.shape[-1]) for a in parts]
-        return [parts[0]] + [shift(parts[d], "y", d) for d in range(1, PARTS)]
-
-    groups = [over_y(near_logits), over_y(far_logits)]
+        if split:
+            (opposite,) = tie([send_y(parts[2], 0)], z_own)
+            opposite = send_y(opposite, 0)
+        else:
+            opposite = shift(parts[2], "y", 2)
+        return [parts[0], shift(parts[1], "y", 1), opposite, shift(parts[3], "y", 3)]
+
+    groups = [over_y(near_logits, True), over_y(far_logits, False)]
     sent = add_parts(place, groups)
     both_values, second_values = local(
         near_values_body,

time: 122 us -> 122 us (level)
  starting transfers between devices: 38 us -> 42.7 us
  waiting for transfers between devices: 45.1 us -> 42.5 us
  local copies, waits for them, and re-layouts: 11.5 us -> 9.46 us
    ppermute x0 -> x2, starting transfers between devices: none -> 6.62 us  [send_y(): return lax.ppermute(arr, ('y', 'core'), table)]
    ppermute x18 -> x17, starting transfers between devices: 26.9 us -> 21.4 us  [shift(): return lax.ppermute(arr, axis, [(i, (i + step) % n) for i in range(n)])]
    ppermute x6, starting transfers between devices: 3.84 us -> 7.21 us  [send_x(): return lax.ppermute(arr, ('core', 'x'), ring_table(way))]
    all_to_all x1, waiting for transfers between devices: 6.62 us -> 3.3 us  [per_device(): got = lax.all_to_all(sent, ('z_hi', 'z_lo'), 0, 0, tiled=True)]
    ppermute x6, waiting for transfers between devices: 6.18 us -> 9.03 us  [send_x(): return lax.ppermute(arr, ('core', 'x'), ring_table(way))]
    ppermute x18 -> x17, waiting for transfers between devices: 32.3 us -> 29.9 us  [shift(): return lax.ppermute(arr, axis, [(i, (i + step) % n) for i in range(n)])]
    unnamed x34 -> x30, local copies, waits for them, and re-layouts: 11.4 us -> 9.39 us
  transfers between devices with their start and end apart: 25 -> 26, of which waited for: 18 -> 13; matrix products, arithmetic and copies ran while one was open for 0% -> 0% of each run, Pallas kernels for 18% -> 18%
where the time goes in v5:
time: 122 us; the launch traced here: 121 us
  starting transfers between devices  42.7 us (35%)
  waiting for transfers between devices  42.5 us (35%)
  Pallas kernels  26.3 us (22%)
  local copies, waits for them, and re-layouts  9.46 us (8%)
    ppermute x17, waiting for transfers between devices, shift(): return lax.ppermute(arr, axis, [(i, (i + step) % n) for i in range(n)])  29.9 us
    ppermute x17, starting transfers between devices, shift(): return lax.ppermute(arr, axis, [(i, (i + step) % n) for i in range(n)])  21.4 us
    pallas_call x9, Pallas kernels, local(): pl.pallas_call(run, out_shape=outs, in_specs=[pl.BlockSpec(memory_space=p...  17.9 us
    unnamed x30, local copies, waits for them, and re-layouts  9.39 us
    ppermute x6, waiting for transfers between devices, send_x(): return lax.ppermute(arr, ('core', 'x'), ring_table(way))  9.03 us
    all_to_all x1, starting transfers between devices, per_device(): got = lax.all_to_all(sent, ('z_hi', 'z_lo'), 0, 0, tiled=True)  7.46 us
    ppermute x6, starting transfers between devices, send_x(): return lax.ppermute(arr, ('core', 'x'), ring_table(way))  7.21 us
    ppermute x2, starting transfers between devices, send_y(): return lax.ppermute(arr, ('y', 'core'), table)  6.62 us
  transfers between devices with their start and end apart: 26, of which 13 were waited for; matrix products, arithmetic and copies ran while one was open for 0% of the time, Pallas kernels for 18%

profile of v5, /device:TPU:1, one launch (start us, length us, event | category | flops | bytes accessed | tf_op | source)
XLA Modules:
  0.0 121.2 jit_solution(10438624915967708793)
XLA Ops:
  0.0 3.2 %collective-permute-start = (bf16[4,128,768]{2,1,0:T(8,128)(2,1)}, bf16[4,128,768]{2,1,0:T(8,128)(2,1)S(1)}, u32[]{:S(2)}, u32[]{:S(2)}) collective-permute-start(bf16[4,128,768]{2,1,0:T(8,128)(2,1)} %refs_1_.1), channel_id=1, source_target_pairs={{0,8},{8,0},{1,9},{9,1},{2,10},{10,2},{3,11},{11,3},{4,12},{12,4},... | collective-permute-start | bytes 2359304 | tf_op jit(solution)/shard_map/ppermute | solution.py:23
  3.2 2.7 %collective-permute-start.1 = (bf16[4,128,768]{2,1,0:T(8,128)(2,1)}, bf16[4,128,768]{2,1,0:T(8,128)(2,1)S(1)}, u32[]{:S(2)}, u32[]{:S(2)}) collective-permute-start(bf16[4,128,768]{2,1,0:T(8,128)(2,1)} %refs_1_.1), channel_id=1, source_target_pairs={{0,2},{2,4},{4,6},{6,0},{8,14},{10,8},{12,10},{14,12},{1,3},{3,5},... | collective-permute-start | bytes 2359304 | tf_op jit(solution)/shard_map/ppermute | solution.py:417
  11.0 5.1 %own.1 = (bf16[6,4,32,512]{3,2,1,0:T(8,128)(2,1)S(1)}, bf16[6,128,512]{2,1,0:T(8,128)(2,1)S(1)}, bf16[3,128,1024]{2,1,0:T(8,128)(2,1)S(1)}, bf16[2,768,384]{2,1,0:T(8,128)(2,1)S(1)}, bf16[2,768,384]{2,1,0:T(8,128)(2,1)S(1)}) custom-call(s32[4]{0:T(128)S(1)} %pad_add_fusion.refs_0_.place, bf16[4,128,768]{2,1,0:T(8,128)(2,1)S(1)} %copy-done.13, ...), custom_call_target="tpu_custom_call" | custom-call | flops 1811939328 | bytes 9830400 | tf_op jit(solution)/shard_map/own/pallas_call | solution.py:78
  16.1 6.6 %collective-permute-done.2.refs_0_ = bf16[4,128,768]{2,1,0:T(8,128)(2,1)S(1)} collective-permute-done((bf16[4,128,768]{2,1,0:T(8,128)(2,1)}, bf16[4,128,768]{2,1,0:T(8,128)(2,1)S(1)}, u32[]{:S(2)}, u32[]{:S(2)}) %collective-permute-start.2) | collective-permute-done | bytes 786464 | tf_op jit(solution)/shard_map/ppermute | solution.py:417
  25.7 2.0 %near.1 = (bf16[6,4,32,256]{3,2,1,0:T(8,128)(2,1)S(1)}, bf16[6,128,256]{2,1,0:T(8,128)(2,1)S(1)}, bf16[6,128,256]{2,1,0:T(8,128)(2,1)S(1)}) custom-call(s32[4]{0:T(128)S(1)} %pad_add_fusion.refs_0_.place, bf16[4,128,768]{2,1,0:T(8,128)(2,1)S(1)} %tie.5.refs_1_, bf16[4,128,768]{2,1,0:T(8,128)(2,1)S(1)} %tie.6.refs_2_.refs_3_, ...), custom_call_target="tpu_custom_call" | custom-call | flops 905969664 | bytes 5898240 | tf_op jit(solution)/shard_map/near/pallas_call | solution.py:101
  27.7 1.6 %near_keys.1 = (bf16[6,128,512]{2,1,0:T(8,128)(2,1)S(1)}, bf16[6,128,512]{2,1,0:T(8,128)(2,1)S(1)}) custom-call(s32[4]{0:T(128)S(1)} %pad_add_fusion.refs_0_.place, bf16[6,128,256]{2,1,0:T(8,128)(2,1)S(1)} %get-tuple-element.36.refs_1_, bf16[6,128,256]{2,1,0:T(8,128)(2,1)S(1)} %get-tuple-element.37.refs_2_, ...), custom_call_target="tpu_custom_call" | custom-call | flops 603979776 | bytes 5111808 | tf_op jit(solution)/shard_map/near_keys/pallas_call | solution.py:101
  29.9 2.0 %near_logits.1 = (bf16[6,4,32,256]{3,2,1,0:T(8,128)(2,1)S(1)}, bf16[2,3,64,384]{3,2,1,0:T(8,128)(2,1)S(1)}, bf16[2,3,64,384]{3,2,1,0:T(8,128)(2,1)S(1)}, bf16[2,...) custom-call(s32[4]{0:T(128)S(1)} %pad_add_fusion.refs_0_.place, ...), custom_call_target="tpu_custom_call" | custom-call | flops 1207959552 | bytes 7077888 | tf_op jit(solution)/shard_map/near_logits/pallas_call | solution.py:101
  31.9 3.3 %collective-permute-start.8 = (bf16[2,192,384]{2,1,0:T(8,128)(2,1)S(1)}, bf16[2,192,384]{2,1,0:T(8,128)(2,1)S(1)}, u32[]{:S(2)}, u32[]{:S(2)}) collective-permute-start(bf16[2,192,384]{2,1,0:T(8,128)(2,1)S(1)} %bitcast.24), channel_id=1, source_target_pairs={{0,16},{8,56},{16,32},{24,8},{32,48},{40,24},{48,0},{56,40},{1,17}... | collective-permute-start | bytes 884744 | tf_op jit(solution)/shard_map/ppermute | solution.py:424
  36.7 1.5 %values_partner.1.refs_5_.refs_0_ = bf16[3,128,1024]{2,1,0:T(8,128)(2,1)S(1)} custom-call(s32[4]{0:T(128)S(1)} %pad_add_fusion.refs_0_.place, bf16[4,128,768]{2,1,0:T(8,128)(2,1)S(1)} %tie.7.refs_3_.refs_1_, bf16[4,128,768]{2,1,0:T(8,128)(2,1)S(1)} %collective-permute-done.6.refs_6_.refs_2_, bf16[768,768]{1,0:T(8,128)(2,1)S(1)} %copy-done.1, ...), custom_call_target="tpu_custom_call" | custom-call | flops 603979776 | bytes 3538944 | tf_op jit(solution)/shard_map/values_partner/pallas_call | solution.py:101
  38.2 2.5 %collective-permute-done.9.refs_4_ = bf16[6,128,512]{2,1,0:T(8,128)(2,1)S(1)} collective-permute-done((bf16[6,128,512]{2,1,0:T(8,128)(2,1)S(1)}, bf16[6,128,512]{2,1,0:T(8,128)(2,1)S(1)}, u32[]{:S(2)}, u32[]{:S(2)}) %collective-permute-start.9) | collective-permute-done | bytes 786464 | tf_op jit(solution)/shard_map/ppermute | solution.py:417
  42.1 3.3 %collective-permute-start.10 = (bf16[2,192,384]{2,1,0:T(8,128)(2,1)S(1)}, bf16[2,192,384]{2,1,0:T(8,128)(2,1)S(1)}, u32[]{:S(2)}, u32[]{:S(2)}) collective-permute-start(bf16[2,192,384]{2,1,0:T(8,128)(2,1)S(1)} %tie.9), channel_id=1, source_target_pairs={{0,16},{8,56},{16,32},{24,8},{32,48},{40,24},{48,0},{56,40},{1,17}... | collective-permute-start | bytes 884744 | tf_op jit(solution)/shard_map/ppermute | solution.py:424
  45.4 1.4 %collective-permute-start.16 = (bf16[3,128,1024]{2,1,0:T(8,128)(2,1)S(1)}, bf16[3,128,1024]{2,1,0:T(8,128)(2,1)}, u32[]{:S(2)}, u32[]{:S(2)}) collective-permute-start(bf16[3,128,1024]{2,1,0:T(8,128)(2,1)S(1)} %tie.8.refs_1_.refs_5_), channel_id=1, source_target_pairs={{0,2},{2,4},{4,6},{6,0},{8,14},{10,8},{12,10},{14,12},{1,3},{3,5},... | collective-permute-start | bytes 2359304 | tf_op jit(solution)/shard_map/ppermute | solution.py:417
  46.8 1.3 %collective-permute-start.13 = (bf16[2,192,128]{2,1,0:T(8,128)(2,1)S(1)}, bf16[2,192,128]{2,1,0:T(8,128)(2,1)S(1)}, u32[]{:S(2)}, u32[]{:S(2)}) collective-permute-start(bf16[2,192,128]{2,1,0:T(8,128)(2,1)S(1)} %bitcast.26), channel_id=1, source_target_pairs={{0,32},{16,48},{32,0},{48,16},{1,33},{17,49},{33,1},{49,17},{2,34}... | collective-permute-start | bytes 294920 | tf_op jit(solution)/shard_map/ppermute | solution.py:23
  48.1 1.4 %collective-permute-start.14 = (bf16[2,192,128]{2,1,0:T(8,128)(2,1)S(1)}, bf16[2,192,128]{2,1,0:T(8,128)(2,1)S(1)}, u32[]{:S(2)}, u32[]{:S(2)}) collective-permute-start(bf16[2,192,128]{2,1,0:T(8,128)(2,1)S(1)} %bitcast.25), channel_id=1, source_target_pairs={{0,48},{16,0},{32,16},{48,32},{1,49},{17,1},{33,17},{49,33},{2,50}... | collective-permute-start | bytes 294920 | tf_op jit(solution)/shard_map/ppermute | solution.py:23
  49.5 4.5 %collective-permute-done.12.refs_6_ = bf16[2,192,128]{2,1,0:T(8,128)(2,1)S(1)} collective-permute-done((bf16[2,192,128]{2,1,0:T(8,128)(2,1)S(1)}, bf16[2,192,128]{2,1,0:T(8,128)(2,1)S(1)}, u32[]{:S(2)}, u32[]{:S(2)}) %collective-permute-start.12) | collective-permute-done | bytes 98336 | tf_op jit(solution)/shard_map/ppermute | solution.py:23
  54.5 1.5 %add_over_y.1.refs_7_ = bf16[4,2,48,512]{3,2,1,0:T(8,128)(2,1)} custom-call(s32[4]{0:T(128)S(1)} %pad_add_fusion.refs_0_.place, bf16[2,192,384]{2,1,0:T(8,128)(2,1)S(1)} %bitcast.21, bf16[2,192,384]{2,1,0:T(8,128)(2,1)S(1)} %collective-permute-done.7.refs_2_, bf16[2,192,384]{2,1,0:T(8,128)(2,1)S(1)} %collective-permute-done.10.refs_3_, ...), custom_call_target="tpu_custom_call" | custom-call | flops 786432 | bytes 1966080 | tf_op jit(solution)/shard_map/add_over_y/pallas_call | solution.py:101
  56.0 7.5 %all-to-all-start = ((bf16[8,48,512]{2,1,0:T(8,128)(2,1)}), bf16[8,48,512]{2,1,0:T(8,128)(2,1)S(1)}, u32[]{:S(2)}, u32[]{:S(2)}) async-start(bf16[8,48,512]{2,1,0:T(8,128)(2,1)} %bitcast.12), calls=%async_computation | async-start | bytes 786432 | tf_op jit(solution)/shard_map/all_to_all | solution.py:541
  67.0 4.1 %values_near.1 = (bf16[2,3,128,1024]{3,2,1,0:T(8,128)(2,1)}, bf16[3,128,1024]{2,1,0:T(8,128)(2,1)S(1)}) custom-call(s32[4]{0:T(128)S(1)} %pad_add_fusion.refs_0_.place, bf16[4,128,768]{2,1,0:T(8,128)(2,1)S(1)} %tie.5.refs_1_, bf16[4,128,768]{2,1,0:T(8,128)(2,1)S(1)} %copy-done.4, bf16[4,128,768]{2,1,0:T(8,128)(2,1)S(1)} %tie.6.refs_2_.refs_3_, ...), custom_call_target="tpu_custom_call" | custom-call | flops 1207959552 | bytes 7471104 | tf_op jit(solution)/shard_map/values_near/pallas_call | solution.py:101
  72.0 3.3 %all-to-all-done = bf16[8,48,512]{2,1,0:T(8,128)(2,1)S(1)} async-done(((bf16[8,48,512]{2,1,0:T(8,128)(2,1)}), bf16[8,48,512]{2,1,0:T(8,128)(2,1)S(1)}, u32[]{:S(2)}, u32[]{:S(2)}) %all-to-all-start) | async-done | bytes 393248 | tf_op jit(solution)/shard_map/all_to_all | solution.py:541
  76.1 2.5 %collective-permute-start.23 = (bf16[2,3,128,1024]{3,2,1,0:T(8,128)(2,1)}, bf16[2,3,128,1024]{3,2,1,0:T(8,128)(2,1)S(1)}, u32[]{:S(2)}, u32[]{:S(2)}) collective-permute-start(bf16[2,3,128,1024]{3,2,1,0:T(8,128)(2,1)} %get-tuple-element.52.refs_2_), channel_id=1, source_target_pairs={{0,2},{2,4},{4,6},{6,0},{8,14},{10,8},{12,10},{14,12},{1,3},{3,5},... | collective-permute-start | bytes 4718600 | tf_op jit(solution)/shard_map/ppermute | solution.py:417
  79.1 2.9 %collective-permute-start.18 = (bf16[48,1024]{1,0:T(8,128)(2,1)S(1)}, bf16[48,1024]{1,0:T(8,128)(2,1)S(1)}, u32[]{:S(2)}, u32[]{:S(2)}) collective-permute-start(bf16[48,1024]{1,0:T(8,128)(2,1)S(1)} %get-tuple-element.50.refs_1_), channel_id=1, source_target_pairs={{0,128},{64,192},{128,0},{192,64},{1,129},{65,193},{129,1},{193,65... | collective-permute-start | bytes 294920 | tf_op jit(solution)/shard_map/ppermute | solution.py:23
  82.0 1.9 %collective-permute-start.19 = (bf16[48,1024]{1,0:T(8,128)(2,1)S(1)}, bf16[48,1024]{1,0:T(8,128)(2,1)S(1)}, u32[]{:S(2)}, u32[]{:S(2)}) collective-permute-start(bf16[48,1024]{1,0:T(8,128)(2,1)S(1)} %get-tuple-element.50.refs_1_), channel_id=1, source_target_pairs={{0,192},{64,0},{128,64},{192,128},{1,193},{65,1},{129,65},{193,129... | collective-permute-start | bytes 294920 | tf_op jit(solution)/shard_map/ppermute | solution.py:23
  84.0 1.4 %collective-permute-done.17.refs_2_ = bf16[48,1024]{1,0:T(8,128)(2,1)S(1)} collective-permute-done((bf16[48,1024]{1,0:T(8,128)(2,1)S(1)}, bf16[48,1024]{1,0:T(8,128)(2,1)S(1)}, u32[]{:S(2)}, u32[]{:S(2)}) %collective-permute-start.17) | collective-permute-done | bytes 98336 | tf_op jit(solution)/shard_map/ppermute | solution.py:23
  85.3 3.4 %collective-permute-done.18.refs_3_ = bf16[48,1024]{1,0:T(8,128)(2,1)S(1)} collective-permute-done((bf16[48,1024]{1,0:T(8,128)(2,1)S(1)}, bf16[48,1024]{1,0:T(8,128)(2,1)S(1)}, u32[]{:S(2)}, u32[]{:S(2)}) %collective-permute-start.18) | collective-permute-done | bytes 98336 | tf_op jit(solution)/shard_map/ppermute | solution.py:23
  88.7 4.3 %collective-permute-done.19.refs_4_ = bf16[48,1024]{1,0:T(8,128)(2,1)S(1)} collective-permute-done((bf16[48,1024]{1,0:T(8,128)(2,1)S(1)}, bf16[48,1024]{1,0:T(8,128)(2,1)S(1)}, u32[]{:S(2)}, u32[]{:S(2)}) %collective-permute-start.19) | collective-permute-done | bytes 98336 | tf_op jit(solution)/shard_map/ppermute | solution.py:23
  93.7 2.2 %collective-permute-start.20 = (bf16[3,64,1024]{2,1,0:T(8,128)(2,1)S(1)}, bf16[3,64,1024]{2,1,0:T(8,128)(2,1)S(1)}, u32[]{:S(2)}, u32[]{:S(2)}) collective-permute-start(bf16[3,64,1024]{2,1,0:T(8,128)(2,1)S(1)} %bitcast.15), channel_id=1, source_target_pairs={{0,16},{16,32},{32,48},{48,0},{1,17},{17,33},{33,49},{49,1},{2,18}... | collective-permute-start | bytes 1179656 | tf_op jit(solution)/shard_map/ppermute | solution.py:23
  95.8 2.5 %collective-permute-start.22 = (bf16[3,64,1024]{2,1,0:T(8,128)(2,1)S(1)}, bf16[3,64,1024]{2,1,0:T(8,128)(2,1)S(1)}, u32[]{:S(2)}, u32[]{:S(2)}) collective-permute-start(bf16[3,64,1024]{2,1,0:T(8,128)(2,1)S(1)} %bitcast.17), channel_id=1, source_target_pairs={{0,48},{16,0},{32,16},{48,32},{1,49},{17,1},{33,17},{49,33},{2,50}... | collective-permute-start | bytes 1179656 | tf_op jit(solution)/shard_map/ppermute | solution.py:23
  98.3 1.8 %gather_values.1.refs_5_ = bf16[3,1024,1024]{2,1,0:T(8,128)(2,1)S(1)} custom-call(s32[4]{0:T(128)S(1)} %pad_add_fusion.refs_0_.place, bf16[3,128,1024]{2,1,0:T(8,128)(2,1)S(1)} %copy-done.8, bf16[2,3,128,1024]{3,2,1,0:T(8,128)(2,1)} %get-tuple-element.52.refs_2_, bf16[3,128,1024]{2,1,0:T(8,128)(2,1)S(1)} %copy-done.10, ...), custom_call_target="tpu_custom_call" | custom-call | bytes 12582912 | tf_op jit(solution)/shard_map/gather_values/pallas_call | solution.py:101
  100.2 13.4 %collective-permute-done.20.refs_2_ = bf16[3,64,1024]{2,1,0:T(8,128)(2,1)S(1)} collective-permute-done((bf16[3,64,1024]{2,1,0:T(8,128)(2,1)S(1)}, bf16[3,64,1024]{2,1,0:T(8,128)(2,1)S(1)}, u32[]{:S(2)}, u32[]{:S(2)}) %collective-permute-start.20) | collective-permute-done | bytes 393248 | tf_op jit(solution)/shard_map/ppermute | solution.py:23
  114.0 2.4 %mix.1 = (bf16[4,128,384]{2,1,0:T(8,128)(2,1)S(1)}, bf16[4,128,384]{2,1,0:T(8,128)(2,1)S(1)}) custom-call(s32[4]{0:T(128)S(1)} %pad_add_fusion.refs_0_.place, bf16[3,64,1024]{2,1,0:T(8,128)(2,1)S(1)} %bitcast.18, bf16[3,64,1024]{2,1,0:T(8,128)(2,1)S(1)} %collective-permute-done.20.refs_2_, bf16[3,64,1024]{2,1,0:T(8,128)(2,1)S(1)} %collective-permute-done.21.refs_3_, ...), custom_call_target="tpu_custom_call" | custom-call | flops 1610612736 | bytes 8650752 | tf_op jit(solution)/shard_map/mix/pallas_call | solution.py:101
  116.3 1.6 %collective-permute-start.24 = (bf16[4,128,384]{2,1,0:T(8,128)(2,1)S(1)}, bf16[4,128,384]{2,1,0:T(8,128)(2,1)S(1)}, u32[]{:S(2)}, u32[]{:S(2)}) collective-permute-start(bf16[4,128,384]{2,1,0:T(8,128)(2,1)S(1)} %get-tuple-element.56), channel_id=1, source_target_pairs={{0,8},{8,0},{1,9},{9,1},{2,10},{10,2},{3,11},{11,3},{4,12},{12,4},... | collective-permute-start | bytes 1179656 | tf_op jit(solution)/shard_map/ppermute | solution.py:23
  119.3 1.9 %finish.1 = bf16[4,128,768]{2,1,0:T(8,128)(2,1)} custom-call(bf16[4,128,384]{2,1,0:T(8,128)(2,1)S(1)} %get-tuple-element.55.mine, bf16[4,128,384]{2,1,0:T(8,128)(2,1)S(1)} %collective-permute-done.24.theirs, bf16[384,768]{1,0:T(8,128)(2,1)S(1)} %get-tuple-element.58.weight_mine, bf16[384,768]{1,0:T(8,128)(2,1)S(1)} %get-tuple-element.57.weight_theirs), custom_call_target="tpu_custom_call" | custom-call | flops 603979776 | bytes 2752512 | tf_op jit(solution)/shard_map/finish/pallas_call | solution.py:391
  (70 shorter events, 20.0 us)
Async XLA Ops:
  0.0 6.0 %collective-permute-start = (bf16[4,128,768]{2,1,0:T(8,128)(2,1)}, bf16[4,128,768]{2,1,0:T(8,128)(2,1)S(1)}, u32[]{:S(2)}, u32[]{:S(2)}) collective-permute-start(bf16[4,128,768]{2,1,0:T(8,128)(2,1)} %refs_1_.1), channel_id=1, source_target_pairs={{0,8},{8,0},{1,9},{9,1},{2,10},{10,2},{3,11},{11,3},{4,12},{12,4},... | collective-permute-start | bytes 2359304 | tf_op jit(solution)/shard_map/ppermute | solution.py:23
  3.2 19.4 %collective-permute-start.2 = (bf16[4,128,768]{2,1,0:T(8,128)(2,1)}, bf16[4,128,768]{2,1,0:T(8,128)(2,1)S(1)}, u32[]{:S(2)}, u32[]{:S(2)}) collective-permute-start(bf16[4,128,768]{2,1,0:T(8,128)(2,1)} %refs_1_.1), channel_id=1, source_target_pairs={{0,6},{2,0},{4,2},{6,4},{8,10},{10,12},{12,14},{14,8},{1,7},{3,1},... | collective-permute-start | bytes 2359304 | tf_op jit(solution)/shard_map/ppermute | solution.py:417
  3.2 20.2 %collective-permute-start.1 = (bf16[4,128,768]{2,1,0:T(8,128)(2,1)}, bf16[4,128,768]{2,1,0:T(8,128)(2,1)S(1)}, u32[]{:S(2)}, u32[]{:S(2)}) collective-permute-start(bf16[4,128,768]{2,1,0:T(8,128)(2,1)} %refs_1_.1), channel_id=1, source_target_pairs={{0,2},{2,4},{4,6},{6,0},{8,14},{10,8},{12,10},{14,12},{1,3},{3,5},... | collective-permute-start | bytes 2359304 | tf_op jit(solution)/shard_map/ppermute | solution.py:417
  5.9 19.4 %collective-permute-start.3 = (bf16[4,128,768]{2,1,0:T(8,128)(2,1)}, bf16[4,128,768]{2,1,0:T(8,128)(2,1)S(1)}, u32[]{:S(2)}, u32[]{:S(2)}) collective-permute-start(bf16[4,128,768]{2,1,0:T(8,128)(2,1)} %refs_1_.1), channel_id=1, source_target_pairs={{0,1},{1,0},{2,3},{3,2},{4,5},{5,4},{6,7},{7,6},{8,9},{9,8},{10,11... | collective-permute-start | bytes 2359304 | tf_op jit(solution)/shard_map/ppermute | solution.py:23
  16.1 6.6 %copy-start.7 = (bf16[3,128,1024]{2,1,0:T(8,128)(2,1)}, bf16[3,128,1024]{2,1,0:T(8,128)(2,1)S(1)}, u32[]{:S(2)}) copy-start(bf16[3,128,1024]{2,1,0:T(8,128)(2,1)S(1)} %get-tuple-element.51.refs_1_) | copy-start | bytes 2359300
  22.7 5.0 %collective-permute-start.4 = (bf16[4,128,768]{2,1,0:T(8,128)(2,1)S(1)}, bf16[4,128,768]{2,1,0:T(8,128)(2,1)S(1)}, u32[]{:S(2)}, u32[]{:S(2)}) collective-permute-start(bf16[4,128,768]{2,1,0:T(8,128)(2,1)S(1)} %tie.6.refs_2_.refs_3_), channel_id=1, source_target_pairs={{0,8},{8,0},{1,9},{9,1},{2,10},{10,2},{3,11},{11,3},{4,12},{12,4},... | collective-permute-start | bytes 2359304 | tf_op jit(solution)/shard_map/ppermute | solution.py:23
  23.4 4.3 %collective-permute-start.5 = (bf16[4,128,768]{2,1,0:T(8,128)(2,1)S(1)}, bf16[4,128,768]{2,1,0:T(8,128)(2,1)S(1)}, u32[]{:S(2)}, u32[]{:S(2)}) collective-permute-start(bf16[4,128,768]{2,1,0:T(8,128)(2,1)S(1)} %tie.5.refs_1_), channel_id=1, source_target_pairs={{0,8},{8,0},{1,9},{9,1},{2,10},{10,2},{3,11},{11,3},{4,12},{12,4},... | collective-permute-start | bytes 2359304 | tf_op jit(solution)/shard_map/ppermute | solution.py:23
  25.3 4.6 %collective-permute-start.6 = (bf16[4,128,768]{2,1,0:T(8,128)(2,1)S(1)}, bf16[4,128,768]{2,1,0:T(8,128)(2,1)S(1)}, u32[]{:S(2)}, u32[]{:S(2)}) collective-permute-start(bf16[4,128,768]{2,1,0:T(8,128)(2,1)S(1)} %tie.7.refs_3_.refs_1_), channel_id=1, source_target_pairs={{0,8},{8,0},{1,9},{9,1},{2,10},{10,2},{3,11},{11,3},{4,12},{12,4},... | collective-permute-start | bytes 2359304 | tf_op jit(solution)/shard_map/ppermute | solution.py:23
  27.7 1.6 %copy-start.3 = (bf16[4,128,768]{2,1,0:T(8,128)(2,1)}, bf16[4,128,768]{2,1,0:T(8,128)(2,1)S(1)}, u32[]{:S(2)}) copy-start(bf16[4,128,768]{2,1,0:T(8,128)(2,1)S(1)} %collective-permute-done.4.refs_3_.refs_2_) | copy-start | bytes 2359300
  29.3 11.4 %collective-permute-start.9 = (bf16[6,128,512]{2,1,0:T(8,128)(2,1)S(1)}, bf16[6,128,512]{2,1,0:T(8,128)(2,1)S(1)}, u32[]{:S(2)}, u32[]{:S(2)}) collective-permute-start(bf16[6,128,512]{2,1,0:T(8,128)(2,1)S(1)} %get-tuple-element.38.refs_4_), channel_id=1, source_target_pairs={{0,2},{2,4},{4,6},{6,0},{8,14},{10,8},{12,10},{14,12},{1,3},{3,5},... | collective-permute-start | bytes 2359304 | tf_op jit(solution)/shard_map/ppermute | solution.py:417
  29.9 6.8 %copy-start.1 = (bf16[768,768]{1,0:T(8,128)(2,1)S(1)}, bf16[768,768]{1,0:T(8,128)(2,1)}, u32[]{:S(2)}) copy-start(bf16[768,768]{1,0:T(8,128)(2,1)} %refs_6_.1) | copy-start | bytes 3538948
  31.9 10.1 %collective-permute-start.8 = (bf16[2,192,384]{2,1,0:T(8,128)(2,1)S(1)}, bf16[2,192,384]{2,1,0:T(8,128)(2,1)S(1)}, u32[]{:S(2)}, u32[]{:S(2)}) collective-permute-start(bf16[2,192,384]{2,1,0:T(8,128)(2,1)S(1)} %bitcast.24), channel_id=1, source_target_pairs={{0,16},{8,56},{16,32},{24,8},{32,48},{40,24},{48,0},{56,40},{1,17}... | collective-permute-start | bytes 884744 | tf_op jit(solution)/shard_map/ppermute | solution.py:424
  35.2 11.5 %collective-permute-start.11 = (bf16[2,192,384]{2,1,0:T(8,128)(2,1)S(1)}, bf16[2,192,384]{2,1,0:T(8,128)(2,1)S(1)}, u32[]{:S(2)}, u32[]{:S(2)}) collective-permute-start(bf16[2,192,384]{2,1,0:T(8,128)(2,1)S(1)} %bitcast.23), channel_id=1, source_target_pairs={{0,48},{16,0},{32,16},{48,32},{1,49},{17,1},{33,17},{49,33},{2,50}... | collective-permute-start | bytes 884744 | tf_op jit(solution)/shard_map/ppermute | solution.py:23
  35.7 12.4 %collective-permute-start.7 = (bf16[2,192,384]{2,1,0:T(8,128)(2,1)S(1)}, bf16[2,192,384]{2,1,0:T(8,128)(2,1)S(1)}, u32[]{:S(2)}, u32[]{:S(2)}) collective-permute-start(bf16[2,192,384]{2,1,0:T(8,128)(2,1)S(1)} %bitcast.22), channel_id=1, source_target_pairs={{0,16},{16,32},{32,48},{48,0},{1,17},{17,33},{33,49},{49,1},{2,18}... | collective-permute-start | bytes 884744 | tf_op jit(solution)/shard_map/ppermute | solution.py:23
  42.1 12.5 %collective-permute-start.10 = (bf16[2,192,384]{2,1,0:T(8,128)(2,1)S(1)}, bf16[2,192,384]{2,1,0:T(8,128)(2,1)S(1)}, u32[]{:S(2)}, u32[]{:S(2)}) collective-permute-start(bf16[2,192,384]{2,1,0:T(8,128)(2,1)S(1)} %tie.9), channel_id=1, source_target_pairs={{0,16},{8,56},{16,32},{24,8},{32,48},{40,24},{48,0},{56,40},{1,17}... | collective-permute-start | bytes 884744 | tf_op jit(solution)/shard_map/ppermute | solution.py:424
  45.4 18.1 %collective-permute-start.16 = (bf16[3,128,1024]{2,1,0:T(8,128)(2,1)S(1)}, bf16[3,128,1024]{2,1,0:T(8,128)(2,1)}, u32[]{:S(2)}, u32[]{:S(2)}) collective-permute-start(bf16[3,128,1024]{2,1,0:T(8,128)(2,1)S(1)} %tie.8.refs_1_.refs_5_), channel_id=1, source_target_pairs={{0,2},{2,4},{4,6},{6,0},{8,14},{10,8},{12,10},{14,12},{1,3},{3,5},... | collective-permute-start | bytes 2359304 | tf_op jit(solution)/shard_map/ppermute | solution.py:417
  46.7 7.2 %collective-permute-start.12 = (bf16[2,192,128]{2,1,0:T(8,128)(2,1)S(1)}, bf16[2,192,128]{2,1,0:T(8,128)(2,1)S(1)}, u32[]{:S(2)}, u32[]{:S(2)}) collective-permute-start(bf16[2,192,128]{2,1,0:T(8,128)(2,1)S(1)} %bitcast.27), channel_id=1, source_target_pairs={{0,16},{16,32},{32,48},{48,0},{1,17},{17,33},{33,49},{49,1},{2,18}... | collective-permute-start | bytes 294920 | tf_op jit(solution)/shard_map/ppermute | solution.py:23
  46.8 7.2 %collective-permute-start.13 = (bf16[2,192,128]{2,1,0:T(8,128)(2,1)S(1)}, bf16[2,192,128]{2,1,0:T(8,128)(2,1)S(1)}, u32[]{:S(2)}, u32[]{:S(2)}) collective-permute-start(bf16[2,192,128]{2,1,0:T(8,128)(2,1)S(1)} %bitcast.26), channel_id=1, source_target_pairs={{0,32},{16,48},{32,0},{48,16},{1,33},{17,49},{33,1},{49,17},{2,34}... | collective-permute-start | bytes 294920 | tf_op jit(solution)/shard_map/ppermute | solution.py:23
  48.1 6.4 %collective-permute-start.14 = (bf16[2,192,128]{2,1,0:T(8,128)(2,1)S(1)}, bf16[2,192,128]{2,1,0:T(8,128)(2,1)S(1)}, u32[]{:S(2)}, u32[]{:S(2)}) collective-permute-start(bf16[2,192,128]{2,1,0:T(8,128)(2,1)S(1)} %bitcast.25), channel_id=1, source_target_pairs={{0,48},{16,0},{32,16},{48,32},{1,49},{17,1},{33,17},{49,33},{2,50}... | collective-permute-start | bytes 294920 | tf_op jit(solution)/shard_map/ppermute | solution.py:23
  54.0 18.0 %collective-permute-start.15 = (bf16[3,128,1024]{2,1,0:T(8,128)(2,1)S(1)}, bf16[3,128,1024]{2,1,0:T(8,128)(2,1)S(1)}, u32[]{:S(2)}, u32[]{:S(2)}) collective-permute-start(bf16[3,128,1024]{2,1,0:T(8,128)(2,1)S(1)} %tie.8.refs_1_.refs_5_), channel_id=1, source_target_pairs={{0,6},{2,0},{4,2},{6,4},{8,10},{10,12},{12,14},{14,8},{1,7},{3,1},... | collective-permute-start | bytes 2359304 | tf_op jit(solution)/shard_map/ppermute | solution.py:417
  56.0 19.3 %all-to-all-start = ((bf16[8,48,512]{2,1,0:T(8,128)(2,1)}), bf16[8,48,512]{2,1,0:T(8,128)(2,1)S(1)}, u32[]{:S(2)}, u32[]{:S(2)}) async-start(bf16[8,48,512]{2,1,0:T(8,128)(2,1)} %bitcast.12), calls=%async_computation | async-start | bytes 786432 | tf_op jit(solution)/shard_map/all_to_all | solution.py:541
  75.3 23.0 %copy-start.8 = (bf16[3,128,1024]{2,1,0:T(8,128)(2,1)S(1)}, bf16[3,128,1024]{2,1,0:T(8,128)(2,1)}, u32[]{:S(2)}) copy-start(bf16[3,128,1024]{2,1,0:T(8,128)(2,1)} %copy-done.7) | copy-start | bytes 2359300
  75.3 23.0 %copy-start.10 = (bf16[3,128,1024]{2,1,0:T(8,128)(2,1)S(1)}, bf16[3,128,1024]{2,1,0:T(8,128)(2,1)}, u32[]{:S(2)}) copy-start(bf16[3,128,1024]{2,1,0:T(8,128)(2,1)} %copy-done.9) | copy-start | bytes 2359300
  76.1 22.2 %collective-permute-start.23 = (bf16[2,3,128,1024]{3,2,1,0:T(8,128)(2,1)}, bf16[2,3,128,1024]{3,2,1,0:T(8,128)(2,1)S(1)}, u32[]{:S(2)}, u32[]{:S(2)}) collective-permute-start(bf16[2,3,128,1024]{3,2,1,0:T(8,128)(2,1)} %get-tuple-element.52.refs_2_), channel_id=1, source_target_pairs={{0,2},{2,4},{4,6},{6,0},{8,14},{10,8},{12,10},{14,12},{1,3},{3,5},... | collective-permute-start | bytes 4718600 | tf_op jit(solution)/shard_map/ppermute | solution.py:417
  78.6 6.7 %collective-permute-start.17 = (bf16[48,1024]{1,0:T(8,128)(2,1)S(1)}, bf16[48,1024]{1,0:T(8,128)(2,1)S(1)}, u32[]{:S(2)}, u32[]{:S(2)}) collective-permute-start(bf16[48,1024]{1,0:T(8,128)(2,1)S(1)} %get-tuple-element.50.refs_1_), channel_id=1, source_target_pairs={{0,64},{64,128},{128,192},{192,0},{1,65},{65,129},{129,193},{193,1... | collective-permute-start | bytes 294920 | tf_op jit(solution)/shard_map/ppermute | solution.py:23
  79.1 9.7 %collective-permute-start.18 = (bf16[48,1024]{1,0:T(8,128)(2,1)S(1)}, bf16[48,1024]{1,0:T(8,128)(2,1)S(1)}, u32[]{:S(2)}, u32[]{:S(2)}) collective-permute-start(bf16[48,1024]{1,0:T(8,128)(2,1)S(1)} %get-tuple-element.50.refs_1_), channel_id=1, source_target_pairs={{0,128},{64,192},{128,0},{192,64},{1,129},{65,193},{129,1},{193,65... | collective-permute-start | bytes 294920 | tf_op jit(solution)/shard_map/ppermute | solution.py:23
  82.0 11.1 %collective-permute-start.19 = (bf16[48,1024]{1,0:T(8,128)(2,1)S(1)}, bf16[48,1024]{1,0:T(8,128)(2,1)S(1)}, u32[]{:S(2)}, u32[]{:S(2)}) collective-permute-start(bf16[48,1024]{1,0:T(8,128)(2,1)S(1)} %get-tuple-element.50.refs_1_), channel_id=1, source_target_pairs={{0,192},{64,0},{128,64},{192,128},{1,193},{65,1},{129,65},{193,129... | collective-permute-start | bytes 294920 | tf_op jit(solution)/shard_map/ppermute | solution.py:23
  93.7 19.9 %collective-permute-start.20 = (bf16[3,64,1024]{2,1,0:T(8,128)(2,1)S(1)}, bf16[3,64,1024]{2,1,0:T(8,128)(2,1)S(1)}, u32[]{:S(2)}, u32[]{:S(2)}) collective-permute-start(bf16[3,64,1024]{2,1,0:T(8,128)(2,1)S(1)} %bitcast.15), channel_id=1, source_target_pairs={{0,16},{16,32},{32,48},{48,0},{1,17},{17,33},{33,49},{49,1},{2,18}... | collective-permute-start | bytes 1179656 | tf_op jit(solution)/shard_map/ppermute | solution.py:23
  95.8 17.7 %collective-permute-start.21 = (bf16[3,64,1024]{2,1,0:T(8,128)(2,1)S(1)}, bf16[3,64,1024]{2,1,0:T(8,128)(2,1)S(1)}, u32[]{:S(2)}, u32[]{:S(2)}) collective-permute-start(bf16[3,64,1024]{2,1,0:T(8,128)(2,1)S(1)} %bitcast.16), channel_id=1, source_target_pairs={{0,32},{16,48},{32,0},{48,16},{1,33},{17,49},{33,1},{49,17},{2,34}... | collective-permute-start | bytes 1179656 | tf_op jit(solution)/shard_map/ppermute | solution.py:23
  95.8 18.1 %collective-permute-start.22 = (bf16[3,64,1024]{2,1,0:T(8,128)(2,1)S(1)}, bf16[3,64,1024]{2,1,0:T(8,128)(2,1)S(1)}, u32[]{:S(2)}, u32[]{:S(2)}) collective-permute-start(bf16[3,64,1024]{2,1,0:T(8,128)(2,1)S(1)} %bitcast.17), channel_id=1, source_target_pairs={{0,48},{16,0},{32,16},{48,32},{1,49},{17,1},{33,17},{49,33},{2,50}... | collective-permute-start | bytes 1179656 | tf_op jit(solution)/shard_map/ppermute | solution.py:23
  100.2 17.8 %copy-start.14 = (bf16[768,768]{1,0:T(8,128)(2,1)S(1)}, bf16[768,768]{1,0:T(8,128)(2,1)}, u32[]{:S(2)}) copy-start(bf16[768,768]{1,0:T(8,128)(2,1)} %param.9) | copy-start | bytes 3538948
  116.3 3.0 %collective-permute-start.24 = (bf16[4,128,384]{2,1,0:T(8,128)(2,1)S(1)}, bf16[4,128,384]{2,1,0:T(8,128)(2,1)S(1)}, u32[]{:S(2)}, u32[]{:S(2)}) collective-permute-start(bf16[4,128,384]{2,1,0:T(8,128)(2,1)S(1)} %get-tuple-element.56), channel_id=1, source_target_pairs={{0,8},{8,0},{1,9},{9,1},{2,10},{10,2},{3,11},{11,3},{4,12},{12,4},... | collective-permute-start | bytes 1179656 | tf_op jit(solution)/shard_map/ppermute | solution.py:23
  (9 other events, 11.0 us)

commit v6 on v4

--- a/solution.py
+++ b/solution.py
@@ -350,8 +350,8 @@
     for pair in range(pairs):
         p = jnp.concatenate([ref[pair] for ref in probs], axis=0)
         got = jnp.dot(p, values[pair], preferred_element_type=F32)
-        for d in range(PARTS):
-            at = pl.multiple_of(rel(y - d) * group, group)
+        for d, step in enumerate((0, 1 - 2 * place[0], 2 * place[0] - 1, 2)):
+            at = pl.multiple_of(rel(y - step) * group, group)
             for s in range(2 * seqs):
                 one, two = (
                     got[(2 * d + h) * group : (2 * d + h + 1) * group, s * lanes : (s + 1) * lanes]
@@ -417,6 +417,13 @@
     return lax.ppermute(arr, ("core", "x"), ring_table(way))
 
 
+def send_y(arr, way):
+    table = [
+        (i * 2 + c, (i + (1 if c == way else -1)) % PARTS * 2 + c) for i in range(PARTS) for c in range(2)
+    ]
+    return lax.ppermute(arr, ("y", "core"), table)
+
+
 def per_device(data, query_matrix, key_matrix, value_matrix, output_matrix):
     seqs, rows, width = data.shape
     place = jnp.stack([lax.axis_index(a) for a in ("core", "y", "z_hi", "z_lo")])
@@ -534,7 +541,8 @@
     probs = probs.reshape(pairs, 2 * group, probs.shape[-1])
     parts = [values, both_values, second_values, far_values, z_own, z_second]
     (values,) = local(gather_body, place, parts, of((pairs, 8 * rows, span)), 0, "gather_values")
-    probs = [probs] + [shift(probs, "y", d) for d in range(1, PARTS)]
+    probs = [probs, send_y(probs, 0), send_y(probs, 1)]
+    probs.append(send_y(probs[1], 0))
     mine, theirs = mix(place, probs, values, seqs)
     return finish(mine, swap(theirs), output_mine, output_theirs)
 

time: 122 us -> 122 us (level)
  starting transfers between devices: 38 us -> 42.2 us
  waiting for transfers between devices: 45.1 us -> 41.3 us
    ppermute x18 -> x15, waiting for transfers between devices: 32.3 us -> 18.7 us  [shift(): return lax.ppermute(arr, axis, [(i, (i + step) % n) for i in range(n)])]
    ppermute x0 -> x3, waiting for transfers between devices: none -> 9.84 us  [send_y(): return lax.ppermute(arr, ('y', 'core'), table)]
    ppermute x0 -> x3, starting transfers between devices: none -> 3.92 us  [send_y(): return lax.ppermute(arr, ('y', 'core'), table)]
    ppermute x18 -> x15, starting transfers between devices: 26.9 us -> 27.1 us  [shift(): return lax.ppermute(arr, axis, [(i, (i + step) % n) for i in range(n)])]
  transfers between devices with their start and end apart: 25 -> 25, of which waited for: 18 -> 16; matrix products, arithmetic and copies ran while one was open for 0% -> 0% of each run, Pallas kernels for 18% -> 18%
where the time goes in v6:
time: 122 us
  starting transfers between devices  42.2 us (35%)
  waiting for transfers between devices  41.3 us (34%)
  Pallas kernels  26.3 us (22%)
  local copies, waits for them, and re-layouts  11.5 us (9%)
    ppermute x15, starting transfers between devices, shift(): return lax.ppermute(arr, axis, [(i, (i + step) % n) for i in range(n)])  27.1 us
    ppermute x15, waiting for transfers between devices, shift(): return lax.ppermute(arr, axis, [(i, (i + step) % n) for i in range(n)])  18.7 us
    pallas_call x9, Pallas kernels, local(): pl.pallas_call(run, out_shape=outs, in_specs=[pl.BlockSpec(memory_space=p...  17.9 us
    unnamed x34, local copies, waits for them, and re-layouts  11.4 us
    ppermute x3, waiting for transfers between devices, send_y(): return lax.ppermute(arr, ('y', 'core'), table)  9.84 us
    all_to_all x1, starting transfers between devices, per_device(): got = lax.all_to_all(sent, ('z_hi', 'z_lo'), 0, 0, tiled=True)  7.3 us
    all_to_all x1, waiting for transfers between devices, per_device(): got = lax.all_to_all(sent, ('z_hi', 'z_lo'), 0, 0, tiled=True)  6.62 us
    ppermute x6, waiting for transfers between devices, send_x(): return lax.ppermute(arr, ('core', 'x'), ring_table(way))  6.12 us
  transfers between devices with their start and end apart: 25, of which 16 were waited for; matrix products, arithmetic and copies ran while one was open for 0% of the time, Pallas kernels for 18%

profile of v6, /device:TPU:1, one launch (start us, length us, event | category | flops | bytes accessed | tf_op | source)
XLA Modules:
  0.0 121.6 jit_solution(3299793273831365682)
XLA Ops:
  0.0 3.2 %collective-permute-start = (bf16[4,128,768]{2,1,0:T(8,128)(2,1)}, bf16[4,128,768]{2,1,0:T(8,128)(2,1)S(1)}, u32[]{:S(2)}, u32[]{:S(2)}) collective-permute-start(bf16[4,128,768]{2,1,0:T(8,128)(2,1)} %refs_1_.1), channel_id=1, source_target_pairs={{0,8},{8,0},{1,9},{9,1},{2,10},{10,2},{3,11},{11,3},{4,12},{12,4},... | collective-permute-start | bytes 2359304 | tf_op jit(solution)/shard_map/ppermute | solution.py:23
  3.2 2.7 %collective-permute-start.1 = (bf16[4,128,768]{2,1,0:T(8,128)(2,1)}, bf16[4,128,768]{2,1,0:T(8,128)(2,1)S(1)}, u32[]{:S(2)}, u32[]{:S(2)}) collective-permute-start(bf16[4,128,768]{2,1,0:T(8,128)(2,1)} %refs_1_.1), channel_id=1, source_target_pairs={{0,2},{2,4},{4,6},{6,0},{8,14},{10,8},{12,10},{14,12},{1,3},{3,5},... | collective-permute-start | bytes 2359304 | tf_op jit(solution)/shard_map/ppermute | solution.py:417
  6.9 1.3 %copy-done = bf16[768,768]{1,0:T(8,128)(2,1)S(1)} copy-done((bf16[768,768]{1,0:T(8,128)(2,1)S(1)}, bf16[768,768]{1,0:T(8,128)(2,1)}, u32[]{:S(2)}) %copy-start) | copy-done | bytes 1179672
  8.2 1.3 %copy-done.11 = bf16[768,768]{1,0:T(8,128)(2,1)S(1)} copy-done((bf16[768,768]{1,0:T(8,128)(2,1)S(1)}, bf16[768,768]{1,0:T(8,128)(2,1)}, u32[]{:S(2)}) %copy-start.11) | copy-done | bytes 1179672
  13.0 5.1 %own.1 = (bf16[6,4,32,512]{3,2,1,0:T(8,128)(2,1)S(1)}, bf16[6,128,512]{2,1,0:T(8,128)(2,1)S(1)}, bf16[3,128,1024]{2,1,0:T(8,128)(2,1)S(1)}, bf16[2,768,384]{2,1,0:T(8,128)(2,1)S(1)}, bf16[2,768,384]{2,1,0:T(8,128)(2,1)S(1)}) custom-call(s32[4]{0:T(128)S(1)} %pad_add_fusion.refs_0_.place, bf16[4,128,768]{2,1,0:T(8,128)(2,1)S(1)} %copy-done.13, ...), custom_call_target="tpu_custom_call" | custom-call | flops 1811939328 | bytes 9830400 | tf_op jit(solution)/shard_map/own/pallas_call | solution.py:78
  18.1 4.6 %collective-permute-done.2.refs_0_ = bf16[4,128,768]{2,1,0:T(8,128)(2,1)S(1)} collective-permute-done((bf16[4,128,768]{2,1,0:T(8,128)(2,1)}, bf16[4,128,768]{2,1,0:T(8,128)(2,1)S(1)}, u32[]{:S(2)}, u32[]{:S(2)}) %collective-permute-start.2) | collective-permute-done | bytes 786464 | tf_op jit(solution)/shard_map/ppermute | solution.py:417
  25.7 2.0 %near.1 = (bf16[6,4,32,256]{3,2,1,0:T(8,128)(2,1)S(1)}, bf16[6,128,256]{2,1,0:T(8,128)(2,1)S(1)}, bf16[6,128,256]{2,1,0:T(8,128)(2,1)S(1)}) custom-call(s32[4]{0:T(128)S(1)} %pad_add_fusion.refs_0_.place, bf16[4,128,768]{2,1,0:T(8,128)(2,1)S(1)} %tie.3.refs_1_, bf16[4,128,768]{2,1,0:T(8,128)(2,1)S(1)} %tie.4.refs_2_.refs_3_, ...), custom_call_target="tpu_custom_call" | custom-call | flops 905969664 | bytes 5898240 | tf_op jit(solution)/shard_map/near/pallas_call | solution.py:101
  27.7 1.6 %near_keys.1 = (bf16[6,128,512]{2,1,0:T(8,128)(2,1)S(1)}, bf16[6,128,512]{2,1,0:T(8,128)(2,1)S(1)}) custom-call(s32[4]{0:T(128)S(1)} %pad_add_fusion.refs_0_.place, bf16[6,128,256]{2,1,0:T(8,128)(2,1)S(1)} %get-tuple-element.36.refs_1_, bf16[6,128,256]{2,1,0:T(8,128)(2,1)S(1)} %get-tuple-element.37.refs_2_, ...), custom_call_target="tpu_custom_call" | custom-call | flops 603979776 | bytes 5111808 | tf_op jit(solution)/shard_map/near_keys/pallas_call | solution.py:101
  30.0 2.0 %near_logits.1 = (bf16[6,4,32,256]{3,2,1,0:T(8,128)(2,1)S(1)}, bf16[2,3,64,384]{3,2,1,0:T(8,128)(2,1)S(1)}, bf16[2,3,64,384]{3,2,1,0:T(8,128)(2,1)S(1)}, bf16[2,...) custom-call(s32[4]{0:T(128)S(1)} %pad_add_fusion.refs_0_.place, ...), custom_call_target="tpu_custom_call" | custom-call | flops 1207959552 | bytes 7077888 | tf_op jit(solution)/shard_map/near_logits/pallas_call | solution.py:101
  31.9 1.9 %collective-permute-start.7 = (bf16[2,192,384]{2,1,0:T(8,128)(2,1)S(1)}, bf16[2,192,384]{2,1,0:T(8,128)(2,1)S(1)}, u32[]{:S(2)}, u32[]{:S(2)}) collective-permute-start(bf16[2,192,384]{2,1,0:T(8,128)(2,1)S(1)} %bitcast.23), channel_id=1, source_target_pairs={{0,16},{16,32},{32,48},{48,0},{1,17},{17,33},{33,49},{49,1},{2,18}... | collective-permute-start | bytes 884744 | tf_op jit(solution)/shard_map/ppermute | solution.py:23
  33.8 2.6 %collective-permute-start.8 = (bf16[2,192,384]{2,1,0:T(8,128)(2,1)S(1)}, bf16[2,192,384]{2,1,0:T(8,128)(2,1)S(1)}, u32[]{:S(2)}, u32[]{:S(2)}) collective-permute-start(bf16[2,192,384]{2,1,0:T(8,128)(2,1)S(1)} %bitcast.22), channel_id=1, source_target_pairs={{0,32},{16,48},{32,0},{48,16},{1,33},{17,49},{33,1},{49,17},{2,34}... | collective-permute-start | bytes 884744 | tf_op jit(solution)/shard_map/ppermute | solution.py:23
  37.5 1.5 %values_partner.1.refs_5_ = bf16[3,128,1024]{2,1,0:T(8,128)(2,1)S(1)} custom-call(s32[4]{0:T(128)S(1)} %pad_add_fusion.refs_0_.place, bf16[4,128,768]{2,1,0:T(8,128)(2,1)S(1)} %tie.5.refs_3_.refs_1_, bf16[4,128,768]{2,1,0:T(8,128)(2,1)S(1)} %collective-permute-done.6.refs_6_.refs_2_, bf16[768,768]{1,0:T(8,128)(2,1)S(1)} %copy-done.1, ...), custom_call_target="tpu_custom_call" | custom-call | flops 603979776 | bytes 3538944 | tf_op jit(solution)/shard_map/values_partner/pallas_call | solution.py:101
  39.1 1.6 %collective-permute-done.10.refs_4_ = bf16[6,128,512]{2,1,0:T(8,128)(2,1)S(1)} collective-permute-done((bf16[6,128,512]{2,1,0:T(8,128)(2,1)S(1)}, bf16[6,128,512]{2,1,0:T(8,128)(2,1)S(1)}, u32[]{:S(2)}, u32[]{:S(2)}) %collective-permute-start.10) | collective-permute-done | bytes 786464 | tf_op jit(solution)/shard_map/ppermute | solution.py:417
  42.0 1.6 %collective-permute-done.7.refs_2_ = bf16[2,192,384]{2,1,0:T(8,128)(2,1)S(1)} collective-permute-done((bf16[2,192,384]{2,1,0:T(8,128)(2,1)S(1)}, bf16[2,192,384]{2,1,0:T(8,128)(2,1)S(1)}, u32[]{:S(2)}, u32[]{:S(2)}) %collective-permute-start.7) | collective-permute-done | bytes 294944 | tf_op jit(solution)/shard_map/ppermute | solution.py:23
  43.7 5.4 %collective-permute-start.12 = (bf16[2,192,128]{2,1,0:T(8,128)(2,1)S(1)}, bf16[2,192,128]{2,1,0:T(8,128)(2,1)S(1)}, u32[]{:S(2)}, u32[]{:S(2)}) collective-permute-start(bf16[2,192,128]{2,1,0:T(8,128)(2,1)S(1)} %bitcast.25), channel_id=1, source_target_pairs={{0,32},{16,48},{32,0},{48,16},{1,33},{17,49},{33,1},{49,17},{2,34}... | collective-permute-start | bytes 294920 | tf_op jit(solution)/shard_map/ppermute | solution.py:23
  51.4 1.5 %collective-permute-done.12.refs_7_ = bf16[2,192,128]{2,1,0:T(8,128)(2,1)S(1)} collective-permute-done((bf16[2,192,128]{2,1,0:T(8,128)(2,1)S(1)}, bf16[2,192,128]{2,1,0:T(8,128)(2,1)S(1)}, u32[]{:S(2)}, u32[]{:S(2)}) %collective-permute-start.12) | collective-permute-done | bytes 98336 | tf_op jit(solution)/shard_map/ppermute | solution.py:23
  53.9 1.5 %add_over_y.1.refs_7_ = bf16[4,2,48,512]{3,2,1,0:T(8,128)(2,1)} custom-call(s32[4]{0:T(128)S(1)} %pad_add_fusion.refs_0_.place, bf16[2,192,384]{2,1,0:T(8,128)(2,1)S(1)} %bitcast.19, bf16[2,192,384]{2,1,0:T(8,128)(2,1)S(1)} %collective-permute-done.7.refs_2_, bf16[2,192,384]{2,1,0:T(8,128)(2,1)S(1)} %collective-permute-done.8.refs_3_, ...), custom_call_target="tpu_custom_call" | custom-call | flops 786432 | bytes 1966080 | tf_op jit(solution)/shard_map/add_over_y/pallas_call | solution.py:101
  55.4 7.3 %all-to-all-start = ((bf16[8,48,512]{2,1,0:T(8,128)(2,1)}), bf16[8,48,512]{2,1,0:T(8,128)(2,1)S(1)}, u32[]{:S(2)}, u32[]{:S(2)}) async-start(bf16[8,48,512]{2,1,0:T(8,128)(2,1)} %bitcast.12), calls=%async_computation | async-start | bytes 786432 | tf_op jit(solution)/shard_map/all_to_all | solution.py:534
  66.2 4.1 %values_near.1 = (bf16[2,3,128,1024]{3,2,1,0:T(8,128)(2,1)}, bf16[3,128,1024]{2,1,0:T(8,128)(2,1)S(1)}) custom-call(s32[4]{0:T(128)S(1)} %pad_add_fusion.refs_0_.place, bf16[4,128,768]{2,1,0:T(8,128)(2,1)S(1)} %tie.3.refs_1_, bf16[4,128,768]{2,1,0:T(8,128)(2,1)S(1)} %copy-done.4, bf16[4,128,768]{2,1,0:T(8,128)(2,1)S(1)} %tie.4.refs_2_.refs_3_, ...), custom_call_target="tpu_custom_call" | custom-call | flops 1207959552 | bytes 7471104 | tf_op jit(solution)/shard_map/values_near/pallas_call | solution.py:101
  71.3 6.6 %all-to-all-done = bf16[8,48,512]{2,1,0:T(8,128)(2,1)S(1)} async-done(((bf16[8,48,512]{2,1,0:T(8,128)(2,1)}), bf16[8,48,512]{2,1,0:T(8,128)(2,1)S(1)}, u32[]{:S(2)}, u32[]{:S(2)}) %all-to-all-start) | async-done | bytes 393248 | tf_op jit(solution)/shard_map/all_to_all | solution.py:534
  78.8 2.1 %collective-permute-start.17 = (bf16[48,1024]{1,0:T(8,128)(2,1)S(1)}, bf16[48,1024]{1,0:T(8,128)(2,1)S(1)}, u32[]{:S(2)}, u32[]{:S(2)}) collective-permute-start(bf16[48,1024]{1,0:T(8,128)(2,1)S(1)} %get-tuple-element.50.refs_1_), channel_id=1, source_target_pairs={{0,128},{64,192},{128,0},{192,64},{1,129},{65,193},{129,1},{193,65... | collective-permute-start | bytes 294920 | tf_op jit(solution)/shard_map/ppermute | solution.py:23
  80.9 1.5 %collective-permute-start.18 = (bf16[48,1024]{1,0:T(8,128)(2,1)S(1)}, bf16[48,1024]{1,0:T(8,128)(2,1)S(1)}, u32[]{:S(2)}, u32[]{:S(2)}) collective-permute-start(bf16[48,1024]{1,0:T(8,128)(2,1)S(1)} %get-tuple-element.50.refs_1_), channel_id=1, source_target_pairs={{0,192},{64,0},{128,64},{192,128},{1,193},{65,1},{129,65},{193,129... | collective-permute-start | bytes 294920 | tf_op jit(solution)/shard_map/ppermute | solution.py:23
  82.4 3.1 %collective-permute-done.16.refs_2_ = bf16[48,1024]{1,0:T(8,128)(2,1)S(1)} collective-permute-done((bf16[48,1024]{1,0:T(8,128)(2,1)S(1)}, bf16[48,1024]{1,0:T(8,128)(2,1)S(1)}, u32[]{:S(2)}, u32[]{:S(2)}) %collective-permute-start.16) | collective-permute-done | bytes 98336 | tf_op jit(solution)/shard_map/ppermute | solution.py:23
  85.5 2.7 %collective-permute-done.17.refs_3_ = bf16[48,1024]{1,0:T(8,128)(2,1)S(1)} collective-permute-done((bf16[48,1024]{1,0:T(8,128)(2,1)S(1)}, bf16[48,1024]{1,0:T(8,128)(2,1)S(1)}, u32[]{:S(2)}, u32[]{:S(2)}) %collective-permute-start.17) | collective-permute-done | bytes 98336 | tf_op jit(solution)/shard_map/ppermute | solution.py:23
  88.2 4.9 %collective-permute-done.18.refs_4_ = bf16[48,1024]{1,0:T(8,128)(2,1)S(1)} collective-permute-done((bf16[48,1024]{1,0:T(8,128)(2,1)S(1)}, bf16[48,1024]{1,0:T(8,128)(2,1)S(1)}, u32[]{:S(2)}, u32[]{:S(2)}) %collective-permute-start.18) | collective-permute-done | bytes 98336 | tf_op jit(solution)/shard_map/ppermute | solution.py:23
  95.2 7.0 %collective-permute-done.19.refs_2_ = bf16[3,64,1024]{2,1,0:T(8,128)(2,1)S(1)} collective-permute-done((bf16[3,64,1024]{2,1,0:T(8,128)(2,1)S(1)}, bf16[3,64,1024]{2,1,0:T(8,128)(2,1)S(1)}, u32[]{:S(2)}, u32[]{:S(2)}) %collective-permute-start.19) | collective-permute-done | bytes 393248 | tf_op jit(solution)/shard_map/ppermute | solution.py:424
  102.2 2.4 %collective-permute-start.21 = (bf16[3,64,1024]{2,1,0:T(8,128)(2,1)S(1)}, bf16[3,64,1024]{2,1,0:T(8,128)(2,1)S(1)}, u32[]{:S(2)}, u32[]{:S(2)}) collective-permute-start(bf16[3,64,1024]{2,1,0:T(8,128)(2,1)S(1)} %collective-permute-done.19.refs_2_), channel_id=1, source_target_pairs={{0,16},{8,56},{16,32},{24,8},{32,48},{40,24},{48,0},{56,40},{1,17}... | collective-permute-start | bytes 1179656 | tf_op jit(solution)/shard_map/ppermute | solution.py:424
  104.6 1.8 %gather_values.1.refs_5_ = bf16[3,1024,1024]{2,1,0:T(8,128)(2,1)S(1)} custom-call(s32[4]{0:T(128)S(1)} %pad_add_fusion.refs_0_.place, bf16[3,128,1024]{2,1,0:T(8,128)(2,1)S(1)} %copy-done.8, bf16[2,3,128,1024]{3,2,1,0:T(8,128)(2,1)} %get-tuple-element.52.refs_2_, bf16[3,128,1024]{2,1,0:T(8,128)(2,1)S(1)} %copy-done.10, ...), custom_call_target="tpu_custom_call" | custom-call | bytes 12582912 | tf_op jit(solution)/shard_map/gather_values/pallas_call | solution.py:101
  106.4 2.9 %collective-permute-done.21.refs_4_ = bf16[3,64,1024]{2,1,0:T(8,128)(2,1)S(1)} collective-permute-done((bf16[3,64,1024]{2,1,0:T(8,128)(2,1)S(1)}, bf16[3,64,1024]{2,1,0:T(8,128)(2,1)S(1)}, u32[]{:S(2)}, u32[]{:S(2)}) %collective-permute-start.21) | collective-permute-done | bytes 393248 | tf_op jit(solution)/shard_map/ppermute | solution.py:424
  109.3 2.3 %mix.1 = (bf16[4,128,384]{2,1,0:T(8,128)(2,1)S(1)}, bf16[4,128,384]{2,1,0:T(8,128)(2,1)S(1)}) custom-call(s32[4]{0:T(128)S(1)} %pad_add_fusion.refs_0_.place, bf16[3,64,1024]{2,1,0:T(8,128)(2,1)S(1)} %bitcast.17, bf16[3,64,1024]{2,1,0:T(8,128)(2,1)S(1)} %collective-permute-done.19.refs_2_, bf16[3,64,1024]{2,1,0:T(8,128)(2,1)S(1)} %collective-permute-done.20.refs_3_, ...), custom_call_target="tpu_custom_call" | custom-call | flops 1610612736 | bytes 8650752 | tf_op jit(solution)/shard_map/mix/pallas_call | solution.py:101
  111.6 6.7 %collective-permute-start.23 = (bf16[4,128,384]{2,1,0:T(8,128)(2,1)S(1)}, bf16[4,128,384]{2,1,0:T(8,128)(2,1)S(1)}, u32[]{:S(2)}, u32[]{:S(2)}) collective-permute-start(bf16[4,128,384]{2,1,0:T(8,128)(2,1)S(1)} %get-tuple-element.56), channel_id=1, source_target_pairs={{0,8},{8,0},{1,9},{9,1},{2,10},{10,2},{3,11},{11,3},{4,12},{12,4},... | collective-permute-start | bytes 1179656 | tf_op jit(solution)/shard_map/ppermute | solution.py:23
  119.7 1.9 %finish.1 = bf16[4,128,768]{2,1,0:T(8,128)(2,1)} custom-call(bf16[4,128,384]{2,1,0:T(8,128)(2,1)S(1)} %get-tuple-element.55.mine, bf16[4,128,384]{2,1,0:T(8,128)(2,1)S(1)} %collective-permute-done.23.theirs, bf16[384,768]{1,0:T(8,128)(2,1)S(1)} %get-tuple-element.58.weight_mine, bf16[384,768]{1,0:T(8,128)(2,1)S(1)} %get-tuple-element.57.weight_theirs), custom_call_target="tpu_custom_call" | custom-call | flops 603979776 | bytes 2752512 | tf_op jit(solution)/shard_map/finish/pallas_call | solution.py:391
  (70 shorter events, 22.8 us)
Async XLA Ops:
  0.0 6.0 %collective-permute-start = (bf16[4,128,768]{2,1,0:T(8,128)(2,1)}, bf16[4,128,768]{2,1,0:T(8,128)(2,1)S(1)}, u32[]{:S(2)}, u32[]{:S(2)}) collective-permute-start(bf16[4,128,768]{2,1,0:T(8,128)(2,1)} %refs_1_.1), channel_id=1, source_target_pairs={{0,8},{8,0},{1,9},{9,1},{2,10},{10,2},{3,11},{11,3},{4,12},{12,4},... | collective-permute-start | bytes 2359304 | tf_op jit(solution)/shard_map/ppermute | solution.py:23
  3.2 19.4 %collective-permute-start.2 = (bf16[4,128,768]{2,1,0:T(8,128)(2,1)}, bf16[4,128,768]{2,1,0:T(8,128)(2,1)S(1)}, u32[]{:S(2)}, u32[]{:S(2)}) collective-permute-start(bf16[4,128,768]{2,1,0:T(8,128)(2,1)} %refs_1_.1), channel_id=1, source_target_pairs={{0,6},{2,0},{4,2},{6,4},{8,10},{10,12},{12,14},{14,8},{1,7},{3,1},... | collective-permute-start | bytes 2359304 | tf_op jit(solution)/shard_map/ppermute | solution.py:417
  3.2 20.2 %collective-permute-start.1 = (bf16[4,128,768]{2,1,0:T(8,128)(2,1)}, bf16[4,128,768]{2,1,0:T(8,128)(2,1)S(1)}, u32[]{:S(2)}, u32[]{:S(2)}) collective-permute-start(bf16[4,128,768]{2,1,0:T(8,128)(2,1)} %refs_1_.1), channel_id=1, source_target_pairs={{0,2},{2,4},{4,6},{6,0},{8,14},{10,8},{12,10},{14,12},{1,3},{3,5},... | collective-permute-start | bytes 2359304 | tf_op jit(solution)/shard_map/ppermute | solution.py:417
  5.9 19.4 %collective-permute-start.3 = (bf16[4,128,768]{2,1,0:T(8,128)(2,1)}, bf16[4,128,768]{2,1,0:T(8,128)(2,1)S(1)}, u32[]{:S(2)}, u32[]{:S(2)}) collective-permute-start(bf16[4,128,768]{2,1,0:T(8,128)(2,1)} %refs_1_.1), channel_id=1, source_target_pairs={{0,1},{1,0},{2,3},{3,2},{4,5},{5,4},{6,7},{7,6},{8,9},{9,8},{10,11... | collective-permute-start | bytes 2359304 | tf_op jit(solution)/shard_map/ppermute | solution.py:23
  18.1 4.6 %copy-start.7 = (bf16[3,128,1024]{2,1,0:T(8,128)(2,1)}, bf16[3,128,1024]{2,1,0:T(8,128)(2,1)S(1)}, u32[]{:S(2)}) copy-start(bf16[3,128,1024]{2,1,0:T(8,128)(2,1)S(1)} %get-tuple-element.51.refs_1_) | copy-start | bytes 2359300
  22.7 5.0 %collective-permute-start.4 = (bf16[4,128,768]{2,1,0:T(8,128)(2,1)S(1)}, bf16[4,128,768]{2,1,0:T(8,128)(2,1)S(1)}, u32[]{:S(2)}, u32[]{:S(2)}) collective-permute-start(bf16[4,128,768]{2,1,0:T(8,128)(2,1)S(1)} %tie.4.refs_2_.refs_3_), channel_id=1, source_target_pairs={{0,8},{8,0},{1,9},{9,1},{2,10},{10,2},{3,11},{11,3},{4,12},{12,4},... | collective-permute-start | bytes 2359304 | tf_op jit(solution)/shard_map/ppermute | solution.py:23
  23.4 4.3 %collective-permute-start.5 = (bf16[4,128,768]{2,1,0:T(8,128)(2,1)S(1)}, bf16[4,128,768]{2,1,0:T(8,128)(2,1)S(1)}, u32[]{:S(2)}, u32[]{:S(2)}) collective-permute-start(bf16[4,128,768]{2,1,0:T(8,128)(2,1)S(1)} %tie.3.refs_1_), channel_id=1, source_target_pairs={{0,8},{8,0},{1,9},{9,1},{2,10},{10,2},{3,11},{11,3},{4,12},{12,4},... | collective-permute-start | bytes 2359304 | tf_op jit(solution)/shard_map/ppermute | solution.py:23
  25.3 4.6 %collective-permute-start.6 = (bf16[4,128,768]{2,1,0:T(8,128)(2,1)S(1)}, bf16[4,128,768]{2,1,0:T(8,128)(2,1)S(1)}, u32[]{:S(2)}, u32[]{:S(2)}) collective-permute-start(bf16[4,128,768]{2,1,0:T(8,128)(2,1)S(1)} %tie.5.refs_3_.refs_1_), channel_id=1, source_target_pairs={{0,8},{8,0},{1,9},{9,1},{2,10},{10,2},{3,11},{11,3},{4,12},{12,4},... | collective-permute-start | bytes 2359304 | tf_op jit(solution)/shard_map/ppermute | solution.py:23
  27.7 1.6 %copy-start.3 = (bf16[4,128,768]{2,1,0:T(8,128)(2,1)}, bf16[4,128,768]{2,1,0:T(8,128)(2,1)S(1)}, u32[]{:S(2)}) copy-start(bf16[4,128,768]{2,1,0:T(8,128)(2,1)S(1)} %collective-permute-done.4.refs_3_.refs_2_) | copy-start | bytes 2359300
  27.7 1.6 %copy-start.5 = (bf16[4,128,768]{2,1,0:T(8,128)(2,1)}, bf16[4,128,768]{2,1,0:T(8,128)(2,1)S(1)}, u32[]{:S(2)}) copy-start(bf16[4,128,768]{2,1,0:T(8,128)(2,1)S(1)} %collective-permute-done.5.refs_4_) | copy-start | bytes 2359300
  29.3 11.4 %collective-permute-start.10 = (bf16[6,128,512]{2,1,0:T(8,128)(2,1)S(1)}, bf16[6,128,512]{2,1,0:T(8,128)(2,1)S(1)}, u32[]{:S(2)}, u32[]{:S(2)}) collective-permute-start(bf16[6,128,512]{2,1,0:T(8,128)(2,1)S(1)} %get-tuple-element.38.refs_4_), channel_id=1, source_target_pairs={{0,2},{2,4},{4,6},{6,0},{8,14},{10,8},{12,10},{14,12},{1,3},{3,5},... | collective-permute-start | bytes 2359304 | tf_op jit(solution)/shard_map/ppermute | solution.py:417
  30.0 7.5 %copy-start.1 = (bf16[768,768]{1,0:T(8,128)(2,1)S(1)}, bf16[768,768]{1,0:T(8,128)(2,1)}, u32[]{:S(2)}) copy-start(bf16[768,768]{1,0:T(8,128)(2,1)} %refs_6_.1) | copy-start | bytes 3538948
  31.9 11.7 %collective-permute-start.7 = (bf16[2,192,384]{2,1,0:T(8,128)(2,1)S(1)}, bf16[2,192,384]{2,1,0:T(8,128)(2,1)S(1)}, u32[]{:S(2)}, u32[]{:S(2)}) collective-permute-start(bf16[2,192,384]{2,1,0:T(8,128)(2,1)S(1)} %bitcast.23), channel_id=1, source_target_pairs={{0,16},{16,32},{32,48},{48,0},{1,17},{17,33},{33,49},{49,1},{2,18}... | collective-permute-start | bytes 884744 | tf_op jit(solution)/shard_map/ppermute | solution.py:23
  33.8 15.5 %collective-permute-start.8 = (bf16[2,192,384]{2,1,0:T(8,128)(2,1)S(1)}, bf16[2,192,384]{2,1,0:T(8,128)(2,1)S(1)}, u32[]{:S(2)}, u32[]{:S(2)}) collective-permute-start(bf16[2,192,384]{2,1,0:T(8,128)(2,1)S(1)} %bitcast.22), channel_id=1, source_target_pairs={{0,32},{16,48},{32,0},{48,16},{1,33},{17,49},{33,1},{49,17},{2,34}... | collective-permute-start | bytes 884744 | tf_op jit(solution)/shard_map/ppermute | solution.py:23
  36.4 13.5 %collective-permute-start.9 = (bf16[2,192,384]{2,1,0:T(8,128)(2,1)S(1)}, bf16[2,192,384]{2,1,0:T(8,128)(2,1)S(1)}, u32[]{:S(2)}, u32[]{:S(2)}) collective-permute-start(bf16[2,192,384]{2,1,0:T(8,128)(2,1)S(1)} %bitcast.21), channel_id=1, source_target_pairs={{0,48},{16,0},{32,16},{48,32},{1,49},{17,1},{33,17},{49,33},{2,50}... | collective-permute-start | bytes 884744 | tf_op jit(solution)/shard_map/ppermute | solution.py:23
  39.0 23.7 %collective-permute-start.15 = (bf16[3,128,1024]{2,1,0:T(8,128)(2,1)S(1)}, bf16[3,128,1024]{2,1,0:T(8,128)(2,1)}, u32[]{:S(2)}, u32[]{:S(2)}) collective-permute-start(bf16[3,128,1024]{2,1,0:T(8,128)(2,1)S(1)} %values_partner.1.refs_5_), channel_id=1, source_target_pairs={{0,2},{2,4},{4,6},{6,0},{8,14},{10,8},{12,10},{14,12},{1,3},{3,5},... | collective-permute-start | bytes 2359304 | tf_op jit(solution)/shard_map/ppermute | solution.py:417
  41.8 9.6 %collective-permute-start.11 = (bf16[2,192,128]{2,1,0:T(8,128)(2,1)S(1)}, bf16[2,192,128]{2,1,0:T(8,128)(2,1)S(1)}, u32[]{:S(2)}, u32[]{:S(2)}) collective-permute-start(bf16[2,192,128]{2,1,0:T(8,128)(2,1)S(1)} %bitcast.26), channel_id=1, source_target_pairs={{0,16},{16,32},{32,48},{48,0},{1,17},{17,33},{33,49},{49,1},{2,18}... | collective-permute-start | bytes 294920 | tf_op jit(solution)/shard_map/ppermute | solution.py:23
  43.7 9.3 %collective-permute-start.12 = (bf16[2,192,128]{2,1,0:T(8,128)(2,1)S(1)}, bf16[2,192,128]{2,1,0:T(8,128)(2,1)S(1)}, u32[]{:S(2)}, u32[]{:S(2)}) collective-permute-start(bf16[2,192,128]{2,1,0:T(8,128)(2,1)S(1)} %bitcast.25), channel_id=1, source_target_pairs={{0,32},{16,48},{32,0},{48,16},{1,33},{17,49},{33,1},{49,17},{2,34}... | collective-permute-start | bytes 294920 | tf_op jit(solution)/shard_map/ppermute | solution.py:23
  49.3 4.6 %collective-permute-start.13 = (bf16[2,192,128]{2,1,0:T(8,128)(2,1)S(1)}, bf16[2,192,128]{2,1,0:T(8,128)(2,1)S(1)}, u32[]{:S(2)}, u32[]{:S(2)}) collective-permute-start(bf16[2,192,128]{2,1,0:T(8,128)(2,1)S(1)} %bitcast.24), channel_id=1, source_target_pairs={{0,48},{16,0},{32,16},{48,32},{1,49},{17,1},{33,17},{49,33},{2,50}... | collective-permute-start | bytes 294920 | tf_op jit(solution)/shard_map/ppermute | solution.py:23
  49.9 21.3 %collective-permute-start.14 = (bf16[3,128,1024]{2,1,0:T(8,128)(2,1)S(1)}, bf16[3,128,1024]{2,1,0:T(8,128)(2,1)S(1)}, u32[]{:S(2)}, u32[]{:S(2)}) collective-permute-start(bf16[3,128,1024]{2,1,0:T(8,128)(2,1)S(1)} %values_partner.1.refs_5_), channel_id=1, source_target_pairs={{0,6},{2,0},{4,2},{6,4},{8,10},{10,12},{12,14},{14,8},{1,7},{3,1},... | collective-permute-start | bytes 2359304 | tf_op jit(solution)/shard_map/ppermute | solution.py:417
  55.4 22.5 %all-to-all-start = ((bf16[8,48,512]{2,1,0:T(8,128)(2,1)}), bf16[8,48,512]{2,1,0:T(8,128)(2,1)S(1)}, u32[]{:S(2)}, u32[]{:S(2)}) async-start(bf16[8,48,512]{2,1,0:T(8,128)(2,1)} %bitcast.12), calls=%async_computation | async-start | bytes 786432 | tf_op jit(solution)/shard_map/all_to_all | solution.py:534
  77.9 26.7 %copy-start.8 = (bf16[3,128,1024]{2,1,0:T(8,128)(2,1)S(1)}, bf16[3,128,1024]{2,1,0:T(8,128)(2,1)}, u32[]{:S(2)}) copy-start(bf16[3,128,1024]{2,1,0:T(8,128)(2,1)} %copy-done.7) | copy-start | bytes 2359300
  77.9 26.7 %copy-start.10 = (bf16[3,128,1024]{2,1,0:T(8,128)(2,1)S(1)}, bf16[3,128,1024]{2,1,0:T(8,128)(2,1)}, u32[]{:S(2)}) copy-start(bf16[3,128,1024]{2,1,0:T(8,128)(2,1)} %copy-done.9) | copy-start | bytes 2359300
  78.7 25.9 %collective-permute-start.22 = (bf16[2,3,128,1024]{3,2,1,0:T(8,128)(2,1)}, bf16[2,3,128,1024]{3,2,1,0:T(8,128)(2,1)S(1)}, u32[]{:S(2)}, u32[]{:S(2)}) collective-permute-start(bf16[2,3,128,1024]{3,2,1,0:T(8,128)(2,1)} %get-tuple-element.52.refs_2_), channel_id=1, source_target_pairs={{0,2},{2,4},{4,6},{6,0},{8,14},{10,8},{12,10},{14,12},{1,3},{3,5},... | collective-permute-start | bytes 4718600 | tf_op jit(solution)/shard_map/ppermute | solution.py:417
  78.8 6.7 %collective-permute-start.16 = (bf16[48,1024]{1,0:T(8,128)(2,1)S(1)}, bf16[48,1024]{1,0:T(8,128)(2,1)S(1)}, u32[]{:S(2)}, u32[]{:S(2)}) collective-permute-start(bf16[48,1024]{1,0:T(8,128)(2,1)S(1)} %get-tuple-element.50.refs_1_), channel_id=1, source_target_pairs={{0,64},{64,128},{128,192},{192,0},{1,65},{65,129},{129,193},{193,1... | collective-permute-start | bytes 294920 | tf_op jit(solution)/shard_map/ppermute | solution.py:23
  78.8 9.4 %collective-permute-start.17 = (bf16[48,1024]{1,0:T(8,128)(2,1)S(1)}, bf16[48,1024]{1,0:T(8,128)(2,1)S(1)}, u32[]{:S(2)}, u32[]{:S(2)}) collective-permute-start(bf16[48,1024]{1,0:T(8,128)(2,1)S(1)} %get-tuple-element.50.refs_1_), channel_id=1, source_target_pairs={{0,128},{64,192},{128,0},{192,64},{1,129},{65,193},{129,1},{193,65... | collective-permute-start | bytes 294920 | tf_op jit(solution)/shard_map/ppermute | solution.py:23
  80.9 12.1 %collective-permute-start.18 = (bf16[48,1024]{1,0:T(8,128)(2,1)S(1)}, bf16[48,1024]{1,0:T(8,128)(2,1)S(1)}, u32[]{:S(2)}, u32[]{:S(2)}) collective-permute-start(bf16[48,1024]{1,0:T(8,128)(2,1)S(1)} %get-tuple-element.50.refs_1_), channel_id=1, source_target_pairs={{0,192},{64,0},{128,64},{192,128},{1,193},{65,1},{129,65},{193,129... | collective-permute-start | bytes 294920 | tf_op jit(solution)/shard_map/ppermute | solution.py:23
  93.6 8.5 %collective-permute-start.19 = (bf16[3,64,1024]{2,1,0:T(8,128)(2,1)S(1)}, bf16[3,64,1024]{2,1,0:T(8,128)(2,1)S(1)}, u32[]{:S(2)}, u32[]{:S(2)}) collective-permute-start(bf16[3,64,1024]{2,1,0:T(8,128)(2,1)S(1)} %bitcast.15), channel_id=1, source_target_pairs={{0,16},{8,56},{16,32},{24,8},{32,48},{40,24},{48,0},{56,40},{1,17}... | collective-permute-start | bytes 1179656 | tf_op jit(solution)/shard_map/ppermute | solution.py:424
  94.1 12.3 %collective-permute-start.20 = (bf16[3,64,1024]{2,1,0:T(8,128)(2,1)S(1)}, bf16[3,64,1024]{2,1,0:T(8,128)(2,1)S(1)}, u32[]{:S(2)}, u32[]{:S(2)}) collective-permute-start(bf16[3,64,1024]{2,1,0:T(8,128)(2,1)S(1)} %bitcast.16), channel_id=1, source_target_pairs={{0,48},{8,24},{16,0},{24,40},{32,16},{40,56},{48,32},{56,8},{1,49}... | collective-permute-start | bytes 1179656 | tf_op jit(solution)/shard_map/ppermute | solution.py:424
  102.2 7.1 %collective-permute-start.21 = (bf16[3,64,1024]{2,1,0:T(8,128)(2,1)S(1)}, bf16[3,64,1024]{2,1,0:T(8,128)(2,1)S(1)}, u32[]{:S(2)}, u32[]{:S(2)}) collective-permute-start(bf16[3,64,1024]{2,1,0:T(8,128)(2,1)S(1)} %collective-permute-done.19.refs_2_), channel_id=1, source_target_pairs={{0,16},{8,56},{16,32},{24,8},{32,48},{40,24},{48,0},{56,40},{1,17}... | collective-permute-start | bytes 1179656 | tf_op jit(solution)/shard_map/ppermute | solution.py:424
  106.4 11.9 %copy-start.16 = (bf16[768,768]{1,0:T(8,128)(2,1)S(1)}, bf16[768,768]{1,0:T(8,128)(2,1)}, u32[]{:S(2)}) copy-start(bf16[768,768]{1,0:T(8,128)(2,1)} %param.9) | copy-start | bytes 3538948
  111.6 8.0 %collective-permute-start.23 = (bf16[4,128,384]{2,1,0:T(8,128)(2,1)S(1)}, bf16[4,128,384]{2,1,0:T(8,128)(2,1)S(1)}, u32[]{:S(2)}, u32[]{:S(2)}) collective-permute-start(bf16[4,128,384]{2,1,0:T(8,128)(2,1)S(1)} %get-tuple-element.56), channel_id=1, source_target_pairs={{0,8},{8,0},{1,9},{9,1},{2,10},{10,2},{3,11},{11,3},{4,12},{12,4},... | collective-permute-start | bytes 1179656 | tf_op jit(solution)/shard_map/ppermute | solution.py:23
  (10 other events, 11.4 us)

commit v7 on v5

--- a/solution.py
+++ b/solution.py
@@ -505,6 +505,7 @@
         "values_partner",
         [qb],
     )
+    z_first, z_second = send_x(z_own, 0), send_x(z_own, 1)
     far_logits = local(
         far_logits_body,
         place,
@@ -514,16 +515,9 @@
         "far_logits",
         [z_own],
     )
-    (z_own,) = tie([z_own], far_logits[0])
-    z_first, z_second = send_x(z_own, 0), send_x(z_own, 1)
-
     def over_y(parts, split):
         parts = [a.reshape(2, -1, a.shape[-1]) for a in parts]
-        if split:
-            (opposite,) = tie([send_y(parts[2], 0)], z_own)
-            opposite = send_y(opposite, 0)
-        else:
-            opposite = shift(parts[2], "y", 2)
+        opposite = send_y(send_y(parts[2], 0), 0) if split else shift(parts[2], "y", 2)
         return [parts[0], shift(parts[1], "y", 1), opposite, shift(parts[3], "y", 3)]
 
     groups = [over_y(near_logits, True), over_y(far_logits, False)]

time: 122 us -> 122 us (level)
  starting transfers between devices: 42.7 us -> 39.8 us
  local copies, waits for them, and re-layouts: 9.46 us -> 11.5 us
  waiting for transfers between devices: 42.5 us -> 43.8 us
    ppermute x2, waiting for transfers between devices: 0.24 us -> 5.36 us  [send_y(): return lax.ppermute(arr, ('y', 'core'), table)]
    ppermute x17, waiting for transfers between devices: 29.9 us -> 26.3 us  [shift(): return lax.ppermute(arr, axis, [(i, (i + step) % n) for i in range(n)])]
    ppermute x6, waiting for transfers between devices: 9.03 us -> 5.55 us  [send_x(): return lax.ppermute(arr, ('core', 'x'), ring_table(way))]
    all_to_all x1, waiting for transfers between devices: 3.3 us -> 6.6 us  [per_device(): got = lax.all_to_all(sent, ('z_hi', 'z_lo'), 0, 0, tiled=True)]
    unnamed x30 -> x34, local copies, waits for them, and re-layouts: 9.39 us -> 11.4 us
    ppermute x17, starting transfers between devices: 21.4 us -> 20.1 us  [shift(): return lax.ppermute(arr, axis, [(i, (i + step) % n) for i in range(n)])]
    ppermute x6, starting transfers between devices: 7.21 us -> 5.96 us  [send_x(): return lax.ppermute(arr, ('core', 'x'), ring_table(way))]
  transfers between devices with their start and end apart: 26 -> 26, of which waited for: 13 -> 13; matrix products, arithmetic and copies ran while one was open for 0% -> 0% of each run, Pallas kernels for 18% -> 17%
where the time goes in v7:
time: 122 us
  waiting for transfers between devices  43.8 us (36%)
  starting transfers between devices  39.8 us (33%)
  Pallas kernels  26.3 us (22%)
  local copies, waits for them, and re-layouts  11.5 us (9%)
    ppermute x17, waiting for transfers between devices, shift(): return lax.ppermute(arr, axis, [(i, (i + step) % n) for i in range(n)])  26.3 us
    ppermute x17, starting transfers between devices, shift(): return lax.ppermute(arr, axis, [(i, (i + step) % n) for i in range(n)])  20.1 us
    pallas_call x9, Pallas kernels, local(): pl.pallas_call(run, out_shape=outs, in_specs=[pl.BlockSpec(memory_space=p...  17.9 us
    unnamed x34, local copies, waits for them, and re-layouts  11.4 us
    all_to_all x1, starting transfers between devices, per_device(): got = lax.all_to_all(sent, ('z_hi', 'z_lo'), 0, 0, tiled=True)  7.04 us
    ppermute x2, starting transfers between devices, send_y(): return lax.ppermute(arr, ('y', 'core'), table)  6.62 us
    all_to_all x1, waiting for transfers between devices, per_device(): got = lax.all_to_all(sent, ('z_hi', 'z_lo'), 0, 0, tiled=True)  6.6 us
    ppermute x6, starting transfers between devices, send_x(): return lax.ppermute(arr, ('core', 'x'), ring_table(way))  5.96 us
  transfers between devices with their start and end apart: 26, of which 13 were waited for; matrix products, arithmetic and copies ran while one was open for 0% of the time, Pallas kernels for 17%

profile of v7, /device:TPU:1, one launch (start us, length us, event | category | flops | bytes accessed | tf_op | source)
XLA Modules:
  0.0 121.6 jit_solution(16533408906859268625)
XLA Ops:
  0.0 3.2 %collective-permute-start = (bf16[4,128,768]{2,1,0:T(8,128)(2,1)}, bf16[4,128,768]{2,1,0:T(8,128)(2,1)S(1)}, u32[]{:S(2)}, u32[]{:S(2)}) collective-permute-start(bf16[4,128,768]{2,1,0:T(8,128)(2,1)} %refs_1_.1), channel_id=1, source_target_pairs={{0,8},{8,0},{1,9},{9,1},{2,10},{10,2},{3,11},{11,3},{4,12},{12,4},... | collective-permute-start | bytes 2359304 | tf_op jit(solution)/shard_map/ppermute | solution.py:23
  3.2 2.7 %collective-permute-start.1 = (bf16[4,128,768]{2,1,0:T(8,128)(2,1)}, bf16[4,128,768]{2,1,0:T(8,128)(2,1)S(1)}, u32[]{:S(2)}, u32[]{:S(2)}) collective-permute-start(bf16[4,128,768]{2,1,0:T(8,128)(2,1)} %refs_1_.1), channel_id=1, source_target_pairs={{0,2},{2,4},{4,6},{6,0},{8,14},{10,8},{12,10},{14,12},{1,3},{3,5},... | collective-permute-start | bytes 2359304 | tf_op jit(solution)/shard_map/ppermute | solution.py:417
  6.9 1.3 %copy-done = bf16[768,768]{1,0:T(8,128)(2,1)S(1)} copy-done((bf16[768,768]{1,0:T(8,128)(2,1)S(1)}, bf16[768,768]{1,0:T(8,128)(2,1)}, u32[]{:S(2)}) %copy-start) | copy-done | bytes 1179672
  8.2 1.3 %copy-done.11 = bf16[768,768]{1,0:T(8,128)(2,1)S(1)} copy-done((bf16[768,768]{1,0:T(8,128)(2,1)S(1)}, bf16[768,768]{1,0:T(8,128)(2,1)}, u32[]{:S(2)}) %copy-start.11) | copy-done | bytes 1179672
  13.0 5.1 %own.1 = (bf16[6,4,32,512]{3,2,1,0:T(8,128)(2,1)S(1)}, bf16[6,128,512]{2,1,0:T(8,128)(2,1)S(1)}, bf16[3,128,1024]{2,1,0:T(8,128)(2,1)S(1)}, bf16[2,768,384]{2,1,0:T(8,128)(2,1)S(1)}, bf16[2,768,384]{2,1,0:T(8,128)(2,1)S(1)}) custom-call(s32[4]{0:T(128)S(1)} %pad_add_fusion.refs_0_.place, bf16[4,128,768]{2,1,0:T(8,128)(2,1)S(1)} %copy-done.13, ...), custom_call_target="tpu_custom_call" | custom-call | flops 1811939328 | bytes 9830400 | tf_op jit(solution)/shard_map/own/pallas_call | solution.py:78
  18.1 4.6 %collective-permute-done.2.refs_0_ = bf16[4,128,768]{2,1,0:T(8,128)(2,1)S(1)} collective-permute-done((bf16[4,128,768]{2,1,0:T(8,128)(2,1)}, bf16[4,128,768]{2,1,0:T(8,128)(2,1)S(1)}, u32[]{:S(2)}, u32[]{:S(2)}) %collective-permute-start.2) | collective-permute-done | bytes 786464 | tf_op jit(solution)/shard_map/ppermute | solution.py:417
  25.7 2.0 %near.1 = (bf16[6,4,32,256]{3,2,1,0:T(8,128)(2,1)S(1)}, bf16[6,128,256]{2,1,0:T(8,128)(2,1)S(1)}, bf16[6,128,256]{2,1,0:T(8,128)(2,1)S(1)}) custom-call(s32[4]{0:T(128)S(1)} %pad_add_fusion.refs_0_.place, bf16[4,128,768]{2,1,0:T(8,128)(2,1)S(1)} %tie.3.refs_1_, bf16[4,128,768]{2,1,0:T(8,128)(2,1)S(1)} %tie.4.refs_2_.refs_3_, ...), custom_call_target="tpu_custom_call" | custom-call | flops 905969664 | bytes 5898240 | tf_op jit(solution)/shard_map/near/pallas_call | solution.py:101
  27.7 1.6 %near_keys.1 = (bf16[6,128,512]{2,1,0:T(8,128)(2,1)S(1)}, bf16[6,128,512]{2,1,0:T(8,128)(2,1)S(1)}) custom-call(s32[4]{0:T(128)S(1)} %pad_add_fusion.refs_0_.place, bf16[6,128,256]{2,1,0:T(8,128)(2,1)S(1)} %get-tuple-element.36.refs_1_, bf16[6,128,256]{2,1,0:T(8,128)(2,1)S(1)} %get-tuple-element.37.refs_2_, ...), custom_call_target="tpu_custom_call" | custom-call | flops 603979776 | bytes 5111808 | tf_op jit(solution)/shard_map/near_keys/pallas_call | solution.py:101
  30.0 2.0 %near_logits.1 = (bf16[6,4,32,256]{3,2,1,0:T(8,128)(2,1)S(1)}, bf16[2,3,64,384]{3,2,1,0:T(8,128)(2,1)S(1)}, bf16[2,3,64,384]{3,2,1,0:T(8,128)(2,1)S(1)}, bf16[2,...) custom-call(s32[4]{0:T(128)S(1)} %pad_add_fusion.refs_0_.place, ...), custom_call_target="tpu_custom_call" | custom-call | flops 1207959552 | bytes 7077888 | tf_op jit(solution)/shard_map/near_logits/pallas_call | solution.py:101
  31.9 3.3 %collective-permute-start.8 = (bf16[2,192,384]{2,1,0:T(8,128)(2,1)S(1)}, bf16[2,192,384]{2,1,0:T(8,128)(2,1)S(1)}, u32[]{:S(2)}, u32[]{:S(2)}) collective-permute-start(bf16[2,192,384]{2,1,0:T(8,128)(2,1)S(1)} %bitcast.24), channel_id=1, source_target_pairs={{0,16},{8,56},{16,32},{24,8},{32,48},{40,24},{48,0},{56,40},{1,17}... | collective-permute-start | bytes 884744 | tf_op jit(solution)/shard_map/ppermute | solution.py:424
  36.7 5.4 %collective-permute-done.8 = bf16[2,192,384]{2,1,0:T(8,128)(2,1)S(1)} collective-permute-done((bf16[2,192,384]{2,1,0:T(8,128)(2,1)S(1)}, bf16[2,192,384]{2,1,0:T(8,128)(2,1)S(1)}, u32[]{:S(2)}, u32[]{:S(2)}) %collective-permute-start.8) | collective-permute-done | bytes 294944 | tf_op jit(solution)/shard_map/ppermute | solution.py:424
  42.1 3.3 %collective-permute-start.9 = (bf16[2,192,384]{2,1,0:T(8,128)(2,1)S(1)}, bf16[2,192,384]{2,1,0:T(8,128)(2,1)S(1)}, u32[]{:S(2)}, u32[]{:S(2)}) collective-permute-start(bf16[2,192,384]{2,1,0:T(8,128)(2,1)S(1)} %collective-permute-done.8), channel_id=1, source_target_pairs={{0,16},{8,56},{16,32},{24,8},{32,48},{40,24},{48,0},{56,40},{1,17}... | collective-permute-start | bytes 884744 | tf_op jit(solution)/shard_map/ppermute | solution.py:424
  45.4 1.5 %values_partner.1.refs_5_ = bf16[3,128,1024]{2,1,0:T(8,128)(2,1)S(1)} custom-call(s32[4]{0:T(128)S(1)} %pad_add_fusion.refs_0_.place, bf16[4,128,768]{2,1,0:T(8,128)(2,1)S(1)} %tie.5.refs_3_.refs_1_, bf16[4,128,768]{2,1,0:T(8,128)(2,1)S(1)} %collective-permute-done.6.refs_6_.refs_2_, bf16[768,768]{1,0:T(8,128)(2,1)S(1)} %copy-done.1, ...), custom_call_target="tpu_custom_call" | custom-call | flops 603979776 | bytes 3538944 | tf_op jit(solution)/shard_map/values_partner/pallas_call | solution.py:101
  49.4 1.6 %collective-permute-start.14 = (bf16[2,192,128]{2,1,0:T(8,128)(2,1)S(1)}, bf16[2,192,128]{2,1,0:T(8,128)(2,1)S(1)}, u32[]{:S(2)}, u32[]{:S(2)}) collective-permute-start(bf16[2,192,128]{2,1,0:T(8,128)(2,1)S(1)} %bitcast.25), channel_id=1, source_target_pairs={{0,48},{16,0},{32,16},{48,32},{1,49},{17,1},{33,17},{49,33},{2,50}... | collective-permute-start | bytes 294920 | tf_op jit(solution)/shard_map/ppermute | solution.py:23
  51.0 1.4 %collective-permute-start.15 = (bf16[3,128,1024]{2,1,0:T(8,128)(2,1)S(1)}, bf16[3,128,1024]{2,1,0:T(8,128)(2,1)S(1)}, u32[]{:S(2)}, u32[]{:S(2)}) collective-permute-start(bf16[3,128,1024]{2,1,0:T(8,128)(2,1)S(1)} %values_partner.1.refs_5_), channel_id=1, source_target_pairs={{0,6},{2,0},{4,2},{6,4},{8,10},{10,12},{12,14},{14,8},{1,7},{3,1},... | collective-permute-start | bytes 2359304 | tf_op jit(solution)/shard_map/ppermute | solution.py:417
  52.4 3.0 %collective-permute-done.12.refs_6_ = bf16[2,192,128]{2,1,0:T(8,128)(2,1)S(1)} collective-permute-done((bf16[2,192,128]{2,1,0:T(8,128)(2,1)S(1)}, bf16[2,192,128]{2,1,0:T(8,128)(2,1)S(1)}, u32[]{:S(2)}, u32[]{:S(2)}) %collective-permute-start.12) | collective-permute-done | bytes 98336 | tf_op jit(solution)/shard_map/ppermute | solution.py:23
  55.8 1.5 %add_over_y.1.refs_7_ = bf16[4,2,48,512]{3,2,1,0:T(8,128)(2,1)} custom-call(s32[4]{0:T(128)S(1)} %pad_add_fusion.refs_0_.place, bf16[2,192,384]{2,1,0:T(8,128)(2,1)S(1)} %bitcast.20, bf16[2,192,384]{2,1,0:T(8,128)(2,1)S(1)} %collective-permute-done.7.refs_2_, bf16[2,192,384]{2,1,0:T(8,128)(2,1)S(1)} %collective-permute-done.9.refs_3_, ...), custom_call_target="tpu_custom_call" | custom-call | flops 786432 | bytes 1966080 | tf_op jit(solution)/shard_map/add_over_y/pallas_call | solution.py:101
  57.3 7.0 %all-to-all-start = ((bf16[8,48,512]{2,1,0:T(8,128)(2,1)}), bf16[8,48,512]{2,1,0:T(8,128)(2,1)S(1)}, u32[]{:S(2)}, u32[]{:S(2)}) async-start(bf16[8,48,512]{2,1,0:T(8,128)(2,1)} %bitcast.12), calls=%async_computation | async-start | bytes 786432 | tf_op jit(solution)/shard_map/all_to_all | solution.py:535
  67.9 4.1 %values_near.1 = (bf16[2,3,128,1024]{3,2,1,0:T(8,128)(2,1)}, bf16[3,128,1024]{2,1,0:T(8,128)(2,1)S(1)}) custom-call(s32[4]{0:T(128)S(1)} %pad_add_fusion.refs_0_.place, bf16[4,128,768]{2,1,0:T(8,128)(2,1)S(1)} %tie.3.refs_1_, bf16[4,128,768]{2,1,0:T(8,128)(2,1)S(1)} %copy-done.4, bf16[4,128,768]{2,1,0:T(8,128)(2,1)S(1)} %tie.4.refs_2_.refs_3_, ...), custom_call_target="tpu_custom_call" | custom-call | flops 1207959552 | bytes 7471104 | tf_op jit(solution)/shard_map/values_near/pallas_call | solution.py:101
  72.9 6.6 %all-to-all-done = bf16[8,48,512]{2,1,0:T(8,128)(2,1)S(1)} async-done(((bf16[8,48,512]{2,1,0:T(8,128)(2,1)}), bf16[8,48,512]{2,1,0:T(8,128)(2,1)S(1)}, u32[]{:S(2)}, u32[]{:S(2)}) %all-to-all-start) | async-done | bytes 393248 | tf_op jit(solution)/shard_map/all_to_all | solution.py:535
  81.4 1.7 %collective-permute-start.18 = (bf16[48,1024]{1,0:T(8,128)(2,1)S(1)}, bf16[48,1024]{1,0:T(8,128)(2,1)S(1)}, u32[]{:S(2)}, u32[]{:S(2)}) collective-permute-start(bf16[48,1024]{1,0:T(8,128)(2,1)S(1)} %get-tuple-element.50.refs_1_), channel_id=1, source_target_pairs={{0,128},{64,192},{128,0},{192,64},{1,129},{65,193},{129,1},{193,65... | collective-permute-start | bytes 294920 | tf_op jit(solution)/shard_map/ppermute | solution.py:23
  83.0 1.9 %collective-permute-start.19 = (bf16[48,1024]{1,0:T(8,128)(2,1)S(1)}, bf16[48,1024]{1,0:T(8,128)(2,1)S(1)}, u32[]{:S(2)}, u32[]{:S(2)}) collective-permute-start(bf16[48,1024]{1,0:T(8,128)(2,1)S(1)} %get-tuple-element.50.refs_1_), channel_id=1, source_target_pairs={{0,192},{64,0},{128,64},{192,128},{1,193},{65,1},{129,65},{193,129... | collective-permute-start | bytes 294920 | tf_op jit(solution)/shard_map/ppermute | solution.py:23
  85.0 2.0 %collective-permute-done.17.refs_2_ = bf16[48,1024]{1,0:T(8,128)(2,1)S(1)} collective-permute-done((bf16[48,1024]{1,0:T(8,128)(2,1)S(1)}, bf16[48,1024]{1,0:T(8,128)(2,1)S(1)}, u32[]{:S(2)}, u32[]{:S(2)}) %collective-permute-start.17) | collective-permute-done | bytes 98336 | tf_op jit(solution)/shard_map/ppermute | solution.py:23
  87.0 3.3 %collective-permute-done.18.refs_3_ = bf16[48,1024]{1,0:T(8,128)(2,1)S(1)} collective-permute-done((bf16[48,1024]{1,0:T(8,128)(2,1)S(1)}, bf16[48,1024]{1,0:T(8,128)(2,1)S(1)}, u32[]{:S(2)}, u32[]{:S(2)}) %collective-permute-start.18) | collective-permute-done | bytes 98336 | tf_op jit(solution)/shard_map/ppermute | solution.py:23
  90.3 3.2 %collective-permute-done.19.refs_4_ = bf16[48,1024]{1,0:T(8,128)(2,1)S(1)} collective-permute-done((bf16[48,1024]{1,0:T(8,128)(2,1)S(1)}, bf16[48,1024]{1,0:T(8,128)(2,1)S(1)}, u32[]{:S(2)}, u32[]{:S(2)}) %collective-permute-start.19) | collective-permute-done | bytes 98336 | tf_op jit(solution)/shard_map/ppermute | solution.py:23
  94.1 2.6 %collective-permute-start.20 = (bf16[3,64,1024]{2,1,0:T(8,128)(2,1)S(1)}, bf16[3,64,1024]{2,1,0:T(8,128)(2,1)S(1)}, u32[]{:S(2)}, u32[]{:S(2)}) collective-permute-start(bf16[3,64,1024]{2,1,0:T(8,128)(2,1)S(1)} %bitcast.15), channel_id=1, source_target_pairs={{0,16},{16,32},{32,48},{48,0},{1,17},{17,33},{33,49},{49,1},{2,18}... | collective-permute-start | bytes 1179656 | tf_op jit(solution)/shard_map/ppermute | solution.py:23
  96.6 2.5 %collective-permute-start.22 = (bf16[3,64,1024]{2,1,0:T(8,128)(2,1)S(1)}, bf16[3,64,1024]{2,1,0:T(8,128)(2,1)S(1)}, u32[]{:S(2)}, u32[]{:S(2)}) collective-permute-start(bf16[3,64,1024]{2,1,0:T(8,128)(2,1)S(1)} %bitcast.17), channel_id=1, source_target_pairs={{0,48},{16,0},{32,16},{48,32},{1,49},{17,1},{33,17},{49,33},{2,50}... | collective-permute-start | bytes 1179656 | tf_op jit(solution)/shard_map/ppermute | solution.py:23
  100.1 1.8 %gather_values.1.refs_5_ = bf16[3,1024,1024]{2,1,0:T(8,128)(2,1)S(1)} custom-call(s32[4]{0:T(128)S(1)} %pad_add_fusion.refs_0_.place, bf16[3,128,1024]{2,1,0:T(8,128)(2,1)S(1)} %copy-done.8, bf16[2,3,128,1024]{3,2,1,0:T(8,128)(2,1)} %get-tuple-element.52.refs_2_, bf16[3,128,1024]{2,1,0:T(8,128)(2,1)S(1)} %copy-done.10, ...), custom_call_target="tpu_custom_call" | custom-call | bytes 12582912 | tf_op jit(solution)/shard_map/gather_values/pallas_call | solution.py:101
  102.0 11.2 %collective-permute-done.20.refs_2_ = bf16[3,64,1024]{2,1,0:T(8,128)(2,1)S(1)} collective-permute-done((bf16[3,64,1024]{2,1,0:T(8,128)(2,1)S(1)}, bf16[3,64,1024]{2,1,0:T(8,128)(2,1)S(1)}, u32[]{:S(2)}, u32[]{:S(2)}) %collective-permute-start.20) | collective-permute-done | bytes 393248 | tf_op jit(solution)/shard_map/ppermute | solution.py:23
  114.4 2.4 %mix.1 = (bf16[4,128,384]{2,1,0:T(8,128)(2,1)S(1)}, bf16[4,128,384]{2,1,0:T(8,128)(2,1)S(1)}) custom-call(s32[4]{0:T(128)S(1)} %pad_add_fusion.refs_0_.place, bf16[3,64,1024]{2,1,0:T(8,128)(2,1)S(1)} %bitcast.18, bf16[3,64,1024]{2,1,0:T(8,128)(2,1)S(1)} %collective-permute-done.20.refs_2_, bf16[3,64,1024]{2,1,0:T(8,128)(2,1)S(1)} %collective-permute-done.21.refs_3_, ...), custom_call_target="tpu_custom_call" | custom-call | flops 1610612736 | bytes 8650752 | tf_op jit(solution)/shard_map/mix/pallas_call | solution.py:101
  116.7 1.6 %collective-permute-start.24 = (bf16[4,128,384]{2,1,0:T(8,128)(2,1)S(1)}, bf16[4,128,384]{2,1,0:T(8,128)(2,1)S(1)}, u32[]{:S(2)}, u32[]{:S(2)}) collective-permute-start(bf16[4,128,384]{2,1,0:T(8,128)(2,1)S(1)} %get-tuple-element.56), channel_id=1, source_target_pairs={{0,8},{8,0},{1,9},{9,1},{2,10},{10,2},{3,11},{11,3},{4,12},{12,4},... | collective-permute-start | bytes 1179656 | tf_op jit(solution)/shard_map/ppermute | solution.py:23
  119.7 1.9 %finish.1 = bf16[4,128,768]{2,1,0:T(8,128)(2,1)} custom-call(bf16[4,128,384]{2,1,0:T(8,128)(2,1)S(1)} %get-tuple-element.55.mine, bf16[4,128,384]{2,1,0:T(8,128)(2,1)S(1)} %collective-permute-done.24.theirs, bf16[384,768]{1,0:T(8,128)(2,1)S(1)} %get-tuple-element.58.weight_mine, bf16[384,768]{1,0:T(8,128)(2,1)S(1)} %get-tuple-element.57.weight_theirs), custom_call_target="tpu_custom_call" | custom-call | flops 603979776 | bytes 2752512 | tf_op jit(solution)/shard_map/finish/pallas_call | solution.py:391
  (72 shorter events, 23.0 us)
Async XLA Ops:
  0.0 6.0 %collective-permute-start = (bf16[4,128,768]{2,1,0:T(8,128)(2,1)}, bf16[4,128,768]{2,1,0:T(8,128)(2,1)S(1)}, u32[]{:S(2)}, u32[]{:S(2)}) collective-permute-start(bf16[4,128,768]{2,1,0:T(8,128)(2,1)} %refs_1_.1), channel_id=1, source_target_pairs={{0,8},{8,0},{1,9},{9,1},{2,10},{10,2},{3,11},{11,3},{4,12},{12,4},... | collective-permute-start | bytes 2359304 | tf_op jit(solution)/shard_map/ppermute | solution.py:23
  3.2 19.4 %collective-permute-start.2 = (bf16[4,128,768]{2,1,0:T(8,128)(2,1)}, bf16[4,128,768]{2,1,0:T(8,128)(2,1)S(1)}, u32[]{:S(2)}, u32[]{:S(2)}) collective-permute-start(bf16[4,128,768]{2,1,0:T(8,128)(2,1)} %refs_1_.1), channel_id=1, source_target_pairs={{0,6},{2,0},{4,2},{6,4},{8,10},{10,12},{12,14},{14,8},{1,7},{3,1},... | collective-permute-start | bytes 2359304 | tf_op jit(solution)/shard_map/ppermute | solution.py:417
  3.2 20.2 %collective-permute-start.1 = (bf16[4,128,768]{2,1,0:T(8,128)(2,1)}, bf16[4,128,768]{2,1,0:T(8,128)(2,1)S(1)}, u32[]{:S(2)}, u32[]{:S(2)}) collective-permute-start(bf16[4,128,768]{2,1,0:T(8,128)(2,1)} %refs_1_.1), channel_id=1, source_target_pairs={{0,2},{2,4},{4,6},{6,0},{8,14},{10,8},{12,10},{14,12},{1,3},{3,5},... | collective-permute-start | bytes 2359304 | tf_op jit(solution)/shard_map/ppermute | solution.py:417
  5.9 19.4 %collective-permute-start.3 = (bf16[4,128,768]{2,1,0:T(8,128)(2,1)}, bf16[4,128,768]{2,1,0:T(8,128)(2,1)S(1)}, u32[]{:S(2)}, u32[]{:S(2)}) collective-permute-start(bf16[4,128,768]{2,1,0:T(8,128)(2,1)} %refs_1_.1), channel_id=1, source_target_pairs={{0,1},{1,0},{2,3},{3,2},{4,5},{5,4},{6,7},{7,6},{8,9},{9,8},{10,11... | collective-permute-start | bytes 2359304 | tf_op jit(solution)/shard_map/ppermute | solution.py:23
  18.1 4.6 %copy-start.7 = (bf16[3,128,1024]{2,1,0:T(8,128)(2,1)}, bf16[3,128,1024]{2,1,0:T(8,128)(2,1)S(1)}, u32[]{:S(2)}) copy-start(bf16[3,128,1024]{2,1,0:T(8,128)(2,1)S(1)} %get-tuple-element.51.refs_1_) | copy-start | bytes 2359300
  22.7 5.0 %collective-permute-start.4 = (bf16[4,128,768]{2,1,0:T(8,128)(2,1)S(1)}, bf16[4,128,768]{2,1,0:T(8,128)(2,1)S(1)}, u32[]{:S(2)}, u32[]{:S(2)}) collective-permute-start(bf16[4,128,768]{2,1,0:T(8,128)(2,1)S(1)} %tie.4.refs_2_.refs_3_), channel_id=1, source_target_pairs={{0,8},{8,0},{1,9},{9,1},{2,10},{10,2},{3,11},{11,3},{4,12},{12,4},... | collective-permute-start | bytes 2359304 | tf_op jit(solution)/shard_map/ppermute | solution.py:23
  23.4 4.3 %collective-permute-start.5 = (bf16[4,128,768]{2,1,0:T(8,128)(2,1)S(1)}, bf16[4,128,768]{2,1,0:T(8,128)(2,1)S(1)}, u32[]{:S(2)}, u32[]{:S(2)}) collective-permute-start(bf16[4,128,768]{2,1,0:T(8,128)(2,1)S(1)} %tie.3.refs_1_), channel_id=1, source_target_pairs={{0,8},{8,0},{1,9},{9,1},{2,10},{10,2},{3,11},{11,3},{4,12},{12,4},... | collective-permute-start | bytes 2359304 | tf_op jit(solution)/shard_map/ppermute | solution.py:23
  25.3 4.6 %collective-permute-start.6 = (bf16[4,128,768]{2,1,0:T(8,128)(2,1)S(1)}, bf16[4,128,768]{2,1,0:T(8,128)(2,1)S(1)}, u32[]{:S(2)}, u32[]{:S(2)}) collective-permute-start(bf16[4,128,768]{2,1,0:T(8,128)(2,1)S(1)} %tie.5.refs_3_.refs_1_), channel_id=1, source_target_pairs={{0,8},{8,0},{1,9},{9,1},{2,10},{10,2},{3,11},{11,3},{4,12},{12,4},... | collective-permute-start | bytes 2359304 | tf_op jit(solution)/shard_map/ppermute | solution.py:23
  27.7 1.6 %copy-start.3 = (bf16[4,128,768]{2,1,0:T(8,128)(2,1)}, bf16[4,128,768]{2,1,0:T(8,128)(2,1)S(1)}, u32[]{:S(2)}) copy-start(bf16[4,128,768]{2,1,0:T(8,128)(2,1)S(1)} %collective-permute-done.4.refs_3_.refs_2_) | copy-start | bytes 2359300
  29.3 17.7 %collective-permute-start.11 = (bf16[6,128,512]{2,1,0:T(8,128)(2,1)S(1)}, bf16[6,128,512]{2,1,0:T(8,128)(2,1)S(1)}, u32[]{:S(2)}, u32[]{:S(2)}) collective-permute-start(bf16[6,128,512]{2,1,0:T(8,128)(2,1)S(1)} %get-tuple-element.38.refs_4_), channel_id=1, source_target_pairs={{0,2},{2,4},{4,6},{6,0},{8,14},{10,8},{12,10},{14,12},{1,3},{3,5},... | collective-permute-start | bytes 2359304 | tf_op jit(solution)/shard_map/ppermute | solution.py:417
  30.0 15.4 %copy-start.1 = (bf16[768,768]{1,0:T(8,128)(2,1)S(1)}, bf16[768,768]{1,0:T(8,128)(2,1)}, u32[]{:S(2)}) copy-start(bf16[768,768]{1,0:T(8,128)(2,1)} %refs_6_.1) | copy-start | bytes 3538948
  31.9 10.1 %collective-permute-start.8 = (bf16[2,192,384]{2,1,0:T(8,128)(2,1)S(1)}, bf16[2,192,384]{2,1,0:T(8,128)(2,1)S(1)}, u32[]{:S(2)}, u32[]{:S(2)}) collective-permute-start(bf16[2,192,384]{2,1,0:T(8,128)(2,1)S(1)} %bitcast.24), channel_id=1, source_target_pairs={{0,16},{8,56},{16,32},{24,8},{32,48},{40,24},{48,0},{56,40},{1,17}... | collective-permute-start | bytes 884744 | tf_op jit(solution)/shard_map/ppermute | solution.py:424
  35.2 13.0 %collective-permute-start.10 = (bf16[2,192,384]{2,1,0:T(8,128)(2,1)S(1)}, bf16[2,192,384]{2,1,0:T(8,128)(2,1)S(1)}, u32[]{:S(2)}, u32[]{:S(2)}) collective-permute-start(bf16[2,192,384]{2,1,0:T(8,128)(2,1)S(1)} %bitcast.23), channel_id=1, source_target_pairs={{0,48},{16,0},{32,16},{48,32},{1,49},{17,1},{33,17},{49,33},{2,50}... | collective-permute-start | bytes 884744 | tf_op jit(solution)/shard_map/ppermute | solution.py:23
  35.7 13.7 %collective-permute-start.7 = (bf16[2,192,384]{2,1,0:T(8,128)(2,1)S(1)}, bf16[2,192,384]{2,1,0:T(8,128)(2,1)S(1)}, u32[]{:S(2)}, u32[]{:S(2)}) collective-permute-start(bf16[2,192,384]{2,1,0:T(8,128)(2,1)S(1)} %bitcast.22), channel_id=1, source_target_pairs={{0,16},{16,32},{32,48},{48,0},{1,17},{17,33},{33,49},{49,1},{2,18}... | collective-permute-start | bytes 884744 | tf_op jit(solution)/shard_map/ppermute | solution.py:23
  42.1 8.9 %collective-permute-start.9 = (bf16[2,192,384]{2,1,0:T(8,128)(2,1)S(1)}, bf16[2,192,384]{2,1,0:T(8,128)(2,1)S(1)}, u32[]{:S(2)}, u32[]{:S(2)}) collective-permute-start(bf16[2,192,384]{2,1,0:T(8,128)(2,1)S(1)} %collective-permute-done.8), channel_id=1, source_target_pairs={{0,16},{8,56},{16,32},{24,8},{32,48},{40,24},{48,0},{56,40},{1,17}... | collective-permute-start | bytes 884744 | tf_op jit(solution)/shard_map/ppermute | solution.py:424
  46.9 17.4 %collective-permute-start.16 = (bf16[3,128,1024]{2,1,0:T(8,128)(2,1)S(1)}, bf16[3,128,1024]{2,1,0:T(8,128)(2,1)}, u32[]{:S(2)}, u32[]{:S(2)}) collective-permute-start(bf16[3,128,1024]{2,1,0:T(8,128)(2,1)S(1)} %values_partner.1.refs_5_), channel_id=1, source_target_pairs={{0,2},{2,4},{4,6},{6,0},{8,14},{10,8},{12,10},{14,12},{1,3},{3,5},... | collective-permute-start | bytes 2359304 | tf_op jit(solution)/shard_map/ppermute | solution.py:417
  48.1 7.3 %collective-permute-start.12 = (bf16[2,192,128]{2,1,0:T(8,128)(2,1)S(1)}, bf16[2,192,128]{2,1,0:T(8,128)(2,1)S(1)}, u32[]{:S(2)}, u32[]{:S(2)}) collective-permute-start(bf16[2,192,128]{2,1,0:T(8,128)(2,1)S(1)} %bitcast.27), channel_id=1, source_target_pairs={{0,16},{16,32},{32,48},{48,0},{1,17},{17,33},{33,49},{49,1},{2,18}... | collective-permute-start | bytes 294920 | tf_op jit(solution)/shard_map/ppermute | solution.py:23
  48.2 7.2 %collective-permute-start.13 = (bf16[2,192,128]{2,1,0:T(8,128)(2,1)S(1)}, bf16[2,192,128]{2,1,0:T(8,128)(2,1)S(1)}, u32[]{:S(2)}, u32[]{:S(2)}) collective-permute-start(bf16[2,192,128]{2,1,0:T(8,128)(2,1)S(1)} %bitcast.26), channel_id=1, source_target_pairs={{0,32},{16,48},{32,0},{48,16},{1,33},{17,49},{33,1},{49,17},{2,34}... | collective-permute-start | bytes 294920 | tf_op jit(solution)/shard_map/ppermute | solution.py:23
  49.4 6.4 %collective-permute-start.14 = (bf16[2,192,128]{2,1,0:T(8,128)(2,1)S(1)}, bf16[2,192,128]{2,1,0:T(8,128)(2,1)S(1)}, u32[]{:S(2)}, u32[]{:S(2)}) collective-permute-start(bf16[2,192,128]{2,1,0:T(8,128)(2,1)S(1)} %bitcast.25), channel_id=1, source_target_pairs={{0,48},{16,0},{32,16},{48,32},{1,49},{17,1},{33,17},{49,33},{2,50}... | collective-permute-start | bytes 294920 | tf_op jit(solution)/shard_map/ppermute | solution.py:23
  51.0 21.9 %collective-permute-start.15 = (bf16[3,128,1024]{2,1,0:T(8,128)(2,1)S(1)}, bf16[3,128,1024]{2,1,0:T(8,128)(2,1)S(1)}, u32[]{:S(2)}, u32[]{:S(2)}) collective-permute-start(bf16[3,128,1024]{2,1,0:T(8,128)(2,1)S(1)} %values_partner.1.refs_5_), channel_id=1, source_target_pairs={{0,6},{2,0},{4,2},{6,4},{8,10},{10,12},{12,14},{14,8},{1,7},{3,1},... | collective-permute-start | bytes 2359304 | tf_op jit(solution)/shard_map/ppermute | solution.py:417
  57.3 22.2 %all-to-all-start = ((bf16[8,48,512]{2,1,0:T(8,128)(2,1)}), bf16[8,48,512]{2,1,0:T(8,128)(2,1)S(1)}, u32[]{:S(2)}, u32[]{:S(2)}) async-start(bf16[8,48,512]{2,1,0:T(8,128)(2,1)} %bitcast.12), calls=%async_computation | async-start | bytes 786432 | tf_op jit(solution)/shard_map/all_to_all | solution.py:535
  79.5 20.6 %copy-start.8 = (bf16[3,128,1024]{2,1,0:T(8,128)(2,1)S(1)}, bf16[3,128,1024]{2,1,0:T(8,128)(2,1)}, u32[]{:S(2)}) copy-start(bf16[3,128,1024]{2,1,0:T(8,128)(2,1)} %copy-done.7) | copy-start | bytes 2359300
  79.5 20.6 %copy-start.10 = (bf16[3,128,1024]{2,1,0:T(8,128)(2,1)S(1)}, bf16[3,128,1024]{2,1,0:T(8,128)(2,1)}, u32[]{:S(2)}) copy-start(bf16[3,128,1024]{2,1,0:T(8,128)(2,1)} %copy-done.9) | copy-start | bytes 2359300
  80.3 19.8 %collective-permute-start.23 = (bf16[2,3,128,1024]{3,2,1,0:T(8,128)(2,1)}, bf16[2,3,128,1024]{3,2,1,0:T(8,128)(2,1)S(1)}, u32[]{:S(2)}, u32[]{:S(2)}) collective-permute-start(bf16[2,3,128,1024]{3,2,1,0:T(8,128)(2,1)} %get-tuple-element.52.refs_2_), channel_id=1, source_target_pairs={{0,2},{2,4},{4,6},{6,0},{8,14},{10,8},{12,10},{14,12},{1,3},{3,5},... | collective-permute-start | bytes 4718600 | tf_op jit(solution)/shard_map/ppermute | solution.py:417
  81.4 5.6 %collective-permute-start.17 = (bf16[48,1024]{1,0:T(8,128)(2,1)S(1)}, bf16[48,1024]{1,0:T(8,128)(2,1)S(1)}, u32[]{:S(2)}, u32[]{:S(2)}) collective-permute-start(bf16[48,1024]{1,0:T(8,128)(2,1)S(1)} %get-tuple-element.50.refs_1_), channel_id=1, source_target_pairs={{0,64},{64,128},{128,192},{192,0},{1,65},{65,129},{129,193},{193,1... | collective-permute-start | bytes 294920 | tf_op jit(solution)/shard_map/ppermute | solution.py:23
  81.4 8.9 %collective-permute-start.18 = (bf16[48,1024]{1,0:T(8,128)(2,1)S(1)}, bf16[48,1024]{1,0:T(8,128)(2,1)S(1)}, u32[]{:S(2)}, u32[]{:S(2)}) collective-permute-start(bf16[48,1024]{1,0:T(8,128)(2,1)S(1)} %get-tuple-element.50.refs_1_), channel_id=1, source_target_pairs={{0,128},{64,192},{128,0},{192,64},{1,129},{65,193},{129,1},{193,65... | collective-permute-start | bytes 294920 | tf_op jit(solution)/shard_map/ppermute | solution.py:23
  83.0 10.4 %collective-permute-start.19 = (bf16[48,1024]{1,0:T(8,128)(2,1)S(1)}, bf16[48,1024]{1,0:T(8,128)(2,1)S(1)}, u32[]{:S(2)}, u32[]{:S(2)}) collective-permute-start(bf16[48,1024]{1,0:T(8,128)(2,1)S(1)} %get-tuple-element.50.refs_1_), channel_id=1, source_target_pairs={{0,192},{64,0},{128,64},{192,128},{1,193},{65,1},{129,65},{193,129... | collective-permute-start | bytes 294920 | tf_op jit(solution)/shard_map/ppermute | solution.py:23
  94.1 19.1 %collective-permute-start.20 = (bf16[3,64,1024]{2,1,0:T(8,128)(2,1)S(1)}, bf16[3,64,1024]{2,1,0:T(8,128)(2,1)S(1)}, u32[]{:S(2)}, u32[]{:S(2)}) collective-permute-start(bf16[3,64,1024]{2,1,0:T(8,128)(2,1)S(1)} %bitcast.15), channel_id=1, source_target_pairs={{0,16},{16,32},{32,48},{48,0},{1,17},{17,33},{33,49},{49,1},{2,18}... | collective-permute-start | bytes 1179656 | tf_op jit(solution)/shard_map/ppermute | solution.py:23
  96.6 16.5 %collective-permute-start.21 = (bf16[3,64,1024]{2,1,0:T(8,128)(2,1)S(1)}, bf16[3,64,1024]{2,1,0:T(8,128)(2,1)S(1)}, u32[]{:S(2)}, u32[]{:S(2)}) collective-permute-start(bf16[3,64,1024]{2,1,0:T(8,128)(2,1)S(1)} %bitcast.16), channel_id=1, source_target_pairs={{0,32},{16,48},{32,0},{48,16},{1,33},{17,49},{33,1},{49,17},{2,34}... | collective-permute-start | bytes 1179656 | tf_op jit(solution)/shard_map/ppermute | solution.py:23
  96.6 17.7 %collective-permute-start.22 = (bf16[3,64,1024]{2,1,0:T(8,128)(2,1)S(1)}, bf16[3,64,1024]{2,1,0:T(8,128)(2,1)S(1)}, u32[]{:S(2)}, u32[]{:S(2)}) collective-permute-start(bf16[3,64,1024]{2,1,0:T(8,128)(2,1)S(1)} %bitcast.17), channel_id=1, source_target_pairs={{0,48},{16,0},{32,16},{48,32},{1,49},{17,1},{33,17},{49,33},{2,50}... | collective-permute-start | bytes 1179656 | tf_op jit(solution)/shard_map/ppermute | solution.py:23
  102.0 16.4 %copy-start.16 = (bf16[768,768]{1,0:T(8,128)(2,1)S(1)}, bf16[768,768]{1,0:T(8,128)(2,1)}, u32[]{:S(2)}) copy-start(bf16[768,768]{1,0:T(8,128)(2,1)} %param.9) | copy-start | bytes 3538948
  116.7 3.0 %collective-permute-start.24 = (bf16[4,128,384]{2,1,0:T(8,128)(2,1)S(1)}, bf16[4,128,384]{2,1,0:T(8,128)(2,1)S(1)}, u32[]{:S(2)}, u32[]{:S(2)}) collective-permute-start(bf16[4,128,384]{2,1,0:T(8,128)(2,1)S(1)} %get-tuple-element.56), channel_id=1, source_target_pairs={{0,8},{8,0},{1,9},{9,1},{2,10},{10,2},{3,11},{11,3},{4,12},{12,4},... | collective-permute-start | bytes 1179656 | tf_op jit(solution)/shard_map/ppermute | solution.py:23
  (11 other events, 13.0 us)
